TPU v7x, 32 devices: a whole 2x2x4 slice. The times are simulated.
32 devices in a mesh: gx: 8 (over z, x), gy: 4 (over y, core).
Axes of the slice: x: 2, y: 2, z: 4, core: 2. Of those that a mesh axis runs over, the one named last changes fastest.
Arguments:
- flow_state: float32 [4, 128, 128, 128], P(None, 'gx', 'gy'), may hold values from -10 to 10
- viscosity: float32 [128, 128, 128], P('gx', 'gy'), may hold values from 300 to 1200
Outputs:
- flow_next: float32 [4, 128, 128, 128], P(None, 'gx', 'gy')
All inputs are finite; a program needn't handle non-finite values.
Results may differ from a plain program's by a relative error of at most 0.0003.
Values sent between devices are 32-bit elements; how exact they have to be, the bound alone decides.
No kernel may reach another device: no remote copies, remote signals or barrier semaphores. Data moves between devices by JAX's collectives and lax.ppermute only.
A program may use at most 64 MiB of HBM per device.

v0:
```python
import jax
import jax.numpy as jnp
from jax import lax
from jax.sharding import PartitionSpec as P

ADVECT = 0.2
BUOYANT = 0.5
CONDUCT = 0.6


def extended_2(cells, sides, width):
    for axis, dim in sides:
        count = lax.axis_size(axis)
        ends = count - 1
        head = lax.slice_in_dim(cells, 0, width, axis=dim)
        tail = lax.slice_in_dim(cells, cells.shape[dim] - width, cells.shape[dim], axis=dim)
        cells = jnp.concatenate(
            [
                lax.ppermute(tail, axis, [(i, (i + 1) % count) for i in range(ends)]),
                cells,
                lax.ppermute(head, axis, [((i + 1) % count, i) for i in range(ends)]),
            ],
            axis=dim,
        )
    return cells


def slice_at(array, position, along):
    return lax.index_in_dim(array, position, along, keepdims=False)


def advect(flow_state, padded):
    along_x = 0.5 * (padded[:, 2:, 1:-1] - padded[:, :-2, 1:-1])
    along_y = 0.5 * (padded[:, 1:-1, 2:] - padded[:, 1:-1, :-2])
    along_z = 0.5 * (jnp.roll(flow_state, -1, 3) - jnp.roll(flow_state, 1, 3))
    carried = flow_state[0:1] * along_x + flow_state[1:2] * along_y + flow_state[2:3] * along_z
    source = flow_state - ADVECT * carried
    return jnp.concatenate([source[:2], source[2:3] + BUOYANT * flow_state[3:4], source[3:]], 0)


def edge_faces(viscosity, neighbours, along, at_start, at_end):
    length = viscosity.shape[along]
    before = jnp.where(
        at_start,
        lax.slice_in_dim(viscosity, 0, 1, axis=along),
        lax.slice_in_dim(neighbours, 0, 1, axis=along),
    )
    beyond = jnp.where(
        at_end,
        lax.slice_in_dim(viscosity, length - 1, length, axis=along),
        lax.slice_in_dim(neighbours, length + 1, length + 2, axis=along),
    )
    extended = jnp.concatenate([before, viscosity, beyond], along)
    face_values = 0.5 * (
        lax.slice_in_dim(extended, 0, length + 1, axis=along)
        + lax.slice_in_dim(extended, 1, length + 2, axis=along)
    )
    scales = jnp.array([1.0, 1.0, 1.0, CONDUCT], jnp.float32).reshape(4, 1, 1, 1)
    return scales * face_values[None]


def factor(lowers, middle, uppers):
    inverse, ratios = ([], [])
    for k in range(len(middle)):
        divisor = middle[k] if k == 0 else middle[k] - lowers[k] * ratios[k - 1]
        inverse.append(1.0 / divisor)
        ratios.append(uppers[k] * inverse[k])
    return (inverse, ratios)


def sweep_down(values, lowers, inverse, ratios):
    forward = []
    for k in range(len(values)):
        running = values[k] if k == 0 else values[k] - lowers[k] * forward[k - 1]
        forward.append(running * inverse[k])
    result = [forward[-1]]
    for k in range(len(values) - 2, -1, -1):
        result.append(forward[k] - ratios[k] * result[-1])
    return result[::-1]


def pack_rows(row_pair):
    stacked = jnp.stack(row_pair, 0)
    return jnp.transpose(stacked, (0, 2, 1, 3)).reshape(2, -1, stacked.shape[-1])


def prepare(faces, along):
    length = faces.shape[along] - 1
    face_list = [slice_at(faces, i, along) for i in range(length + 1)]
    lowers = [-face_list[i] for i in range(length)]
    uppers = [-face_list[i + 1] for i in range(length)]
    middle = [1.0 + face_list[i] + face_list[i + 1] for i in range(length)]
    inverse, ratios = factor(lowers[1:-1], middle[1:-1], uppers[1:-1])
    empty_row = jnp.zeros_like(middle[0])
    interior_rows = length - 2
    first_column = sweep_down(
        [-lowers[1]] + [empty_row] * (interior_rows - 1), lowers[1:-1], inverse, ratios
    )
    last_column = sweep_down(
        [empty_row] * (interior_rows - 1) + [-uppers[length - 2]], lowers[1:-1], inverse, ratios
    )
    below = (lowers[0], lowers[-1] * first_column[-1])
    centre = (middle[0] + uppers[0] * first_column[0], middle[-1] + lowers[-1] * last_column[-1])
    above = (uppers[0] * last_column[0], uppers[-1])
    return {
        "lowers": lowers,
        "uppers": uppers,
        "inverse": inverse,
        "ratios": ratios,
        "first_column": first_column,
        "last_column": last_column,
        "field_rows": (pack_rows(below), pack_rows(centre), pack_rows(above)),
        "group_rows": (
            pack_rows((below[0][0::3], below[1][0::3])),
            pack_rows((centre[0][0::3], centre[1][0::3])),
            pack_rows((above[0][0::3], above[1][0::3])),
        ),
    }


def reduced_solve(below, centre, above, source):
    length = centre.shape[0]
    position = lax.broadcasted_iota(jnp.int32, centre.shape, 0)
    below = jnp.where(position == 0, 0.0, below)
    above = jnp.where(position == length - 1, 0.0, above)
    solution = lax.linalg.tridiagonal_solve(
        jnp.moveaxis(below, 0, -1),
        jnp.moveaxis(centre, 0, -1),
        jnp.moveaxis(above, 0, -1),
        jnp.moveaxis(source, 0, -1)[..., None],
    )[..., 0]
    return jnp.moveaxis(solution, -1, 0)


def solve_items(pieces):
    return reduced_solve(pieces[0], pieces[1], pieces[2], pieces[3])


def right_sides(field, factors, along):
    length = field.shape[along]
    values = [slice_at(field, i, along) for i in range(length)]
    interior = sweep_down(
        values[1:-1], factors["lowers"][1:-1], factors["inverse"], factors["ratios"]
    )
    first = values[0] - factors["uppers"][0] * interior[0]
    last = values[-1] - factors["lowers"][-1] * interior[-1]
    return (pack_rows((first, last)), interior)


def assemble(returned, interior, factors, along):
    unpacked = returned.reshape(2, returned.shape[1] // 4, 4, returned.shape[2])
    unpacked = jnp.transpose(unpacked, (0, 2, 1, 3))
    start, finish = (unpacked[0], unpacked[1])
    middle_rows = [
        interior[k] + factors["first_column"][k] * start + factors["last_column"][k] * finish
        for k in range(len(interior))
    ]
    return jnp.stack([start] + middle_rows + [finish], along)


def solve_along_x(field, factors):
    packed, interior = right_sides(field, factors, 1)
    rows = factors["field_rows"]
    solution = solve_items(
        (
            lax.all_to_all(rows[0], "gx", split_axis=1, concat_axis=0, tiled=True),
            lax.all_to_all(rows[1], "gx", split_axis=1, concat_axis=0, tiled=True),
            lax.all_to_all(rows[2], "gx", split_axis=1, concat_axis=0, tiled=True),
            lax.all_to_all(packed, "gx", split_axis=1, concat_axis=0, tiled=True),
        )
    )
    returned = lax.all_to_all(solution, "gx", split_axis=0, concat_axis=1, tiled=True)
    return assemble(returned, interior, factors, 1)


def solve_along_y(field, factors):
    packed, interior = right_sides(field, factors, 2)
    rows = factors["field_rows"]
    solution = solve_items(
        (
            lax.all_to_all(rows[0], "gy", split_axis=1, concat_axis=0, tiled=True),
            lax.all_to_all(rows[1], "gy", split_axis=1, concat_axis=0, tiled=True),
            lax.all_to_all(rows[2], "gy", split_axis=1, concat_axis=0, tiled=True),
            lax.all_to_all(packed, "gy", split_axis=1, concat_axis=0, tiled=True),
        )
    )
    returned = lax.all_to_all(solution, "gy", split_axis=0, concat_axis=1, tiled=True)
    return assemble(returned, interior, factors, 2)


def per_device(flow_state, viscosity):
    neighbours = extended_2(viscosity, (("gx", 0), ("gy", 1)), 1)
    x_index = lax.axis_index("gx")
    y_index = lax.axis_index("gy")
    faces_x = edge_faces(
        viscosity, neighbours[:, 1:-1], 0, x_index == 0, x_index == lax.axis_size("gx") - 1
    )
    faces_y = edge_faces(
        viscosity, neighbours[1:-1], 1, y_index == 0, y_index == lax.axis_size("gy") - 1
    )
    factors_x = prepare(faces_x, 1)
    factors_y = prepare(faces_y, 2)
    current = flow_state
    padded = extended_2(current, (("gx", 1), ("gy", 2)), 1)
    source = advect(current, padded)
    current = solve_along_y(solve_along_x(source, factors_x), factors_y)
    return current


def solution(mesh):
    placed = (P(None, "gx", "gy", None), P("gx", "gy", None))
    return jax.shard_map(
        per_device, mesh=mesh, in_specs=placed, out_specs=P(None, "gx", "gy", None), check_vma=False
    )
```

profile of v0, /device:TPU:0, one launch (start us, length us, event | category | flops | bytes accessed | tf_op | source)
XLA Modules:
  0.0 160.5 jit_solution(4520253129296581705)
XLA Ops:
  1.6 5.4 %collective-permute-start.1 = (f32[4,1,32,128]{3,2,1,0:T(8,128)}, f32[4,1,32,128]{3,2,1,0:T(8,128)}, u32[]{:S(2)}, u32[]{:S(2)}) collective-permute-start(f32[4,1,32,128]{3,2,1,0:T(8,128)} %get-tuple-element.419), channel_id=1, source_target_pairs={{0,4},{4,8},{8,12},{12,16},{16,20},{20,24},{24,28},{1,5},{5,9},{9,... | collective-permute-start | bytes 196616 | tf_op jit(solution)/shard_map/ppermute | solution.py:19
  10.4 5.2 %collective-permute-start.4 = (f32[1,32,128]{2,1,0:T(8,128)S(1)}, f32[1,32,128]{2,1,0:T(8,128)S(1)}, u32[]{:S(2)}, u32[]{:S(2)}) collective-permute-start(f32[1,32,128]{2,1,0:T(8,128)S(1)} %get-tuple-element.427), channel_id=1, source_target_pairs={{0,4},{4,8},{8,12},{12,16},{16,20},{20,24},{24,28},{1,5},{5,9},{9,... | collective-permute-start | bytes 49160 | tf_op jit(solution)/shard_map/ppermute | solution.py:19
  23.6 3.2 %collective-permute-done.7 = f32[18,1,128]{2,1,0:T(1,128)S(1)} collective-permute-done((f32[18,1,128]{2,1,0:T(1,128)S(1)}, f32[18,1,128]{2,1,0:T(1,128)S(1)}, u32[]{:S(2)}, u32[]{:S(2)}) %collective-permute-start.7) | collective-permute-done | bytes 9248 | tf_op jit(solution)/shard_map/ppermute | solution.py:21
  30.3 4.9 %collective-permute-start.3 = (f32[4,18,1,128]{3,2,1,0:T(1,128)S(1)}, f32[4,18,1,128]{3,2,1,0:T(1,128)S(1)}, u32[]{:S(2)}, u32[]{:S(2)}) collective-permute-start(f32[4,18,1,128]{3,2,1,0:T(1,128)S(1)} %get-tuple-element.370), channel_id=1, source_target_pairs={{0,1},{1,2},{2,3},{4,5},{5,6},{6,7},{8,9},{9,10},{10,11},{12,13},{... | collective-permute-start | bytes 110600 | tf_op jit(solution)/shard_map/ppermute | solution.py:19
  42.0 5.7 %all-to-all-start.3 = ((f32[2,128,128]{2,0,1:T(2,128)}), f32[2,128,128]{2,0,1:T(2,128)}, u32[]{:S(2)}, u32[]{:S(2)}) async-start(f32[2,128,128]{2,0,1:T(2,128)} %copy.1072), calls=%async_computation.3 | async-start | bytes 262144 | tf_op jit(solution)/shard_map/all_to_all | solution.py:166
  50.7 4.7 %all-to-all-done.3 = f32[2,128,128]{2,0,1:T(2,128)} async-done(((f32[2,128,128]{2,0,1:T(2,128)}), f32[2,128,128]{2,0,1:T(2,128)}, u32[]{:S(2)}, u32[]{:S(2)}) %all-to-all-start.3) | async-done | bytes 131104 | tf_op jit(solution)/shard_map/all_to_all | solution.py:166
  55.4 4.0 %all-to-all-start.2 = ((f32[2,128,128]{2,0,1:T(2,128)}), f32[2,128,128]{2,0,1:T(2,128)}, u32[]{:S(2)}, u32[]{:S(2)}) async-start(f32[2,128,128]{2,0,1:T(2,128)} %copy.1067), calls=%async_computation.2 | async-start | bytes 262144 | tf_op jit(solution)/shard_map/all_to_all | solution.py:168
  62.4 5.0 %all-to-all-done.2 = f32[2,128,128]{2,0,1:T(2,128)} async-done(((f32[2,128,128]{2,0,1:T(2,128)}), f32[2,128,128]{2,0,1:T(2,128)}, u32[]{:S(2)}, u32[]{:S(2)}) %all-to-all-start.2) | async-done | bytes 131104 | tf_op jit(solution)/shard_map/all_to_all | solution.py:168
  67.5 4.0 %all-to-all-start = ((f32[2,128,128]{2,0,1:T(2,128)}), f32[2,128,128]{2,0,1:T(2,128)}, u32[]{:S(2)}, u32[]{:S(2)}) async-start(f32[2,128,128]{2,0,1:T(2,128)} %copy.1057), calls=%async_computation | async-start | bytes 262144 | tf_op jit(solution)/shard_map/all_to_all | solution.py:169
  75.7 3.1 %all-to-all-done = f32[2,128,128]{2,0,1:T(2,128)} async-done(((f32[2,128,128]{2,0,1:T(2,128)}), f32[2,128,128]{2,0,1:T(2,128)}, u32[]{:S(2)}, u32[]{:S(2)}) %all-to-all-start) | async-done | bytes 131104 | tf_op jit(solution)/shard_map/all_to_all | solution.py:169
  78.8 4.0 %all-to-all-start.1 = ((f32[2,128,128]{2,0,1:T(2,128)}), f32[2,128,128]{2,0,1:T(2,128)}, u32[]{:S(2)}, u32[]{:S(2)}) async-start(f32[2,128,128]{2,0,1:T(2,128)} %copy.1063), calls=%async_computation.1 | async-start | bytes 262144 | tf_op jit(solution)/shard_map/all_to_all | solution.py:167
  84.5 5.7 %all-to-all-done.1 = f32[2,128,128]{2,0,1:T(2,128)} async-done(((f32[2,128,128]{2,0,1:T(2,128)}), f32[2,128,128]{2,0,1:T(2,128)}, u32[]{:S(2)}, u32[]{:S(2)}) %all-to-all-start.1) | async-done | bytes 131104 | tf_op jit(solution)/shard_map/all_to_all | solution.py:167
  93.3 4.2 %all-to-all-start.4 = ((f32[16,16,128]{2,1,0:T(8,128)}), f32[16,16,128]{2,1,0:T(8,128)}, u32[]{:S(2)}, u32[]{:S(2)}) async-start(f32[16,16,128]{2,1,0:T(8,128)} %maximum_bitcast_fusion.4), calls=%async_computation.4 | async-start | bytes 262144 | tf_op jit(solution)/shard_map/all_to_all | solution.py:172
  98.8 5.8 %all-to-all-done.4 = f32[16,16,128]{2,1,0:T(8,128)} async-done(((f32[16,16,128]{2,1,0:T(8,128)}), f32[16,16,128]{2,1,0:T(8,128)}, u32[]{:S(2)}, u32[]{:S(2)}) %all-to-all-start.4) | async-done | bytes 131104 | tf_op jit(solution)/shard_map/all_to_all | solution.py:172
  105.6 2.3 %constant_dynamic-update-slice_fusion.32 = (f32[4,16,32,128]{3,2,0,1:T(8,128)S(1)}, f32[4,1,32,128]{3,2,0,1:T(8,128)S(1)}, f32[4,1,32,128]{3,2,0,1:T(8,128)S(1)}...) fusion(f32[4,16,32,128]{3,2,0,1:T(8,128)S(1)} %constant_dynamic, ...), kind=kLoop, calls=%fused_computation.86 | loop fusion | flops 3194880 | bytes 5963776
  113.8 4.5 %all-to-all-start.8 = ((f32[2,64,128]{2,0,1:T(2,128)}), f32[2,64,128]{2,0,1:T(2,128)S(1)}, u32[]{:S(2)}, u32[]{:S(2)}) async-start(f32[2,64,128]{2,0,1:T(2,128)} %copy.1162), calls=%async_computation.8 | async-start | bytes 131072 | tf_op jit(solution)/shard_map/all_to_all | solution.py:181
  122.3 3.3 %all-to-all-start.7 = ((f32[2,64,128]{2,0,1:T(2,128)}), f32[2,64,128]{2,0,1:T(2,128)S(1)}, u32[]{:S(2)}, u32[]{:S(2)}) async-start(f32[2,64,128]{2,0,1:T(2,128)} %copy.1158), calls=%async_computation.7 | async-start | bytes 131072 | tf_op jit(solution)/shard_map/all_to_all | solution.py:183
  125.7 4.0 %all-to-all-done.7 = f32[2,64,128]{2,0,1:T(2,128)S(1)} async-done(((f32[2,64,128]{2,0,1:T(2,128)}), f32[2,64,128]{2,0,1:T(2,128)S(1)}, u32[]{:S(2)}, u32[]{:S(2)}) %all-to-all-start.7) | async-done | bytes 65568 | tf_op jit(solution)/shard_map/all_to_all | solution.py:183
  129.7 3.3 %all-to-all-start.5 = ((f32[2,64,128]{2,0,1:T(2,128)}), f32[2,64,128]{2,0,1:T(2,128)S(1)}, u32[]{:S(2)}, u32[]{:S(2)}) async-start(f32[2,64,128]{2,0,1:T(2,128)} %copy.1150), calls=%async_computation.5 | async-start | bytes 131072 | tf_op jit(solution)/shard_map/all_to_all | solution.py:184
  133.1 4.0 %all-to-all-done.5 = f32[2,64,128]{2,0,1:T(2,128)S(1)} async-done(((f32[2,64,128]{2,0,1:T(2,128)}), f32[2,64,128]{2,0,1:T(2,128)S(1)}, u32[]{:S(2)}, u32[]{:S(2)}) %all-to-all-start.5) | async-done | bytes 65568 | tf_op jit(solution)/shard_map/all_to_all | solution.py:184
  137.1 3.3 %all-to-all-start.6 = ((f32[2,64,128]{2,0,1:T(2,128)}), f32[2,64,128]{2,0,1:T(2,128)S(1)}, u32[]{:S(2)}, u32[]{:S(2)}) async-start(f32[2,64,128]{2,0,1:T(2,128)} %copy.1155), calls=%async_computation.6 | async-start | bytes 131072 | tf_op jit(solution)/shard_map/all_to_all | solution.py:182
  140.5 4.0 %all-to-all-done.6 = f32[2,64,128]{2,0,1:T(2,128)S(1)} async-done(((f32[2,64,128]{2,0,1:T(2,128)}), f32[2,64,128]{2,0,1:T(2,128)S(1)}, u32[]{:S(2)}, u32[]{:S(2)}) %all-to-all-start.6) | async-done | bytes 65568 | tf_op jit(solution)/shard_map/all_to_all | solution.py:182
  145.3 3.3 %all-to-all-start.9 = ((f32[8,16,128]{2,1,0:T(8,128)}), f32[8,16,128]{2,1,0:T(8,128)S(1)}, u32[]{:S(2)}, u32[]{:S(2)}) async-start(f32[8,16,128]{2,1,0:T(8,128)} %maximum_bitcast_fusion.5), calls=%async_computation.9 | async-start | bytes 131072 | tf_op jit(solution)/shard_map/all_to_all | solution.py:187
  152.7 3.4 %constant_dynamic-update-slice_fusion.74 = (f32[4,16,32,128]{3,0,1,2:T(4,128)S(1)}, f32[4,16,1,128]{3,0,1,2:T(4,128)S(1)}, f32[4,16,1,128]{3,0,1,2:T(4,128)S(1)}...) fusion(f32[4,16,32,128]{3,0,1,2:T(4,128)S(1)} %constant_dynamic, ...), kind=kLoop, calls=%fused_computation.128 | loop fusion | flops 3309568 | bytes 6324224
  (302 shorter events, 58.7 us)
Async XLA Ops:
  0.0 17.6 %copy-start = (f32[4,16,32,128]{3,2,1,0:T(8,128)S(1)}, f32[4,16,32,128]{3,2,1,0:T(8,128)}, u32[]{:S(2)}) copy-start(f32[4,16,32,128]{3,2,1,0:T(8,128)} %param.4) | copy-start | bytes 3145732
  1.6 25.3 %collective-permute-start.1 = (f32[4,1,32,128]{3,2,1,0:T(8,128)}, f32[4,1,32,128]{3,2,1,0:T(8,128)}, u32[]{:S(2)}, u32[]{:S(2)}) collective-permute-start(f32[4,1,32,128]{3,2,1,0:T(8,128)} %get-tuple-element.419), channel_id=1, source_target_pairs={{0,4},{4,8},{8,12},{12,16},{16,20},{20,24},{24,28},{1,5},{5,9},{9,... | collective-permute-start | bytes 196616 | tf_op jit(solution)/shard_map/ppermute | solution.py:19
  7.1 20.9 %collective-permute-start = (f32[4,1,32,128]{3,2,1,0:T(8,128)}, f32[4,1,32,128]{3,2,1,0:T(8,128)}, u32[]{:S(2)}, u32[]{:S(2)}) collective-permute-start(f32[4,1,32,128]{3,2,1,0:T(8,128)} %get-tuple-element.418), channel_id=1, source_target_pairs={{4,0},{8,4},{12,8},{16,12},{20,16},{24,20},{28,24},{5,1},{9,5},{13... | collective-permute-start | bytes 196616 | tf_op jit(solution)/shard_map/ppermute | solution.py:21
  9.1 11.6 %collective-permute-start.5 = (f32[1,32,128]{2,1,0:T(8,128)S(1)}, f32[1,32,128]{2,1,0:T(8,128)S(1)}, u32[]{:S(2)}, u32[]{:S(2)}) collective-permute-start(f32[1,32,128]{2,1,0:T(8,128)S(1)} %get-tuple-element.426), channel_id=1, source_target_pairs={{4,0},{8,4},{12,8},{16,12},{20,16},{24,20},{28,24},{5,1},{9,5},{13... | collective-permute-start | bytes 49160 | tf_op jit(solution)/shard_map/ppermute | solution.py:21
  10.4 10.3 %collective-permute-start.4 = (f32[1,32,128]{2,1,0:T(8,128)S(1)}, f32[1,32,128]{2,1,0:T(8,128)S(1)}, u32[]{:S(2)}, u32[]{:S(2)}) collective-permute-start(f32[1,32,128]{2,1,0:T(8,128)S(1)} %get-tuple-element.427), channel_id=1, source_target_pairs={{0,4},{4,8},{8,12},{12,16},{16,20},{20,24},{24,28},{1,5},{5,9},{9,... | collective-permute-start | bytes 49160 | tf_op jit(solution)/shard_map/ppermute | solution.py:19
  20.8 2.9 %collective-permute-start.6 = (f32[18,1,128]{2,1,0:T(1,128)S(1)}, f32[18,1,128]{2,1,0:T(1,128)S(1)}, u32[]{:S(2)}, u32[]{:S(2)}) collective-permute-start(f32[18,1,128]{2,1,0:T(1,128)S(1)} %get-tuple-element.421), channel_id=1, source_target_pairs={{0,1},{1,2},{2,3},{4,5},{5,6},{6,7},{8,9},{9,10},{10,11},{12,13},{... | collective-permute-start | bytes 27656 | tf_op jit(solution)/shard_map/ppermute | solution.py:19
  22.1 4.8 %collective-permute-start.7 = (f32[18,1,128]{2,1,0:T(1,128)S(1)}, f32[18,1,128]{2,1,0:T(1,128)S(1)}, u32[]{:S(2)}, u32[]{:S(2)}) collective-permute-start(f32[18,1,128]{2,1,0:T(1,128)S(1)} %get-tuple-element.420), channel_id=1, source_target_pairs={{1,0},{2,1},{3,2},{5,4},{6,5},{7,6},{9,8},{10,9},{11,10},{13,12},{... | collective-permute-start | bytes 27656 | tf_op jit(solution)/shard_map/ppermute | solution.py:21
  23.4 12.7 %copy-start.11 = (f32[16,32,128]{2,1,0:T(8,128)S(1)}, f32[16,32,128]{2,1,0:T(8,128)}, u32[]{:S(2)}) copy-start(f32[16,32,128]{2,1,0:T(8,128)} %get-tuple-element.413) | copy-start | bytes 786436
  26.9 9.2 %copy-start.10 = (f32[16,32,128]{2,1,0:T(8,128)S(1)}, f32[16,32,128]{2,1,0:T(8,128)}, u32[]{:S(2)}) copy-start(f32[16,32,128]{2,1,0:T(8,128)} %get-tuple-element.412) | copy-start | bytes 786436
  29.0 6.4 %collective-permute-start.2 = (f32[4,18,1,128]{3,2,1,0:T(1,128)S(1)}, f32[4,18,1,128]{3,2,1,0:T(1,128)S(1)}, u32[]{:S(2)}, u32[]{:S(2)}) collective-permute-start(f32[4,18,1,128]{3,2,1,0:T(1,128)S(1)} %get-tuple-element.369), channel_id=1, source_target_pairs={{1,0},{2,1},{3,2},{5,4},{6,5},{7,6},{9,8},{10,9},{11,10},{13,12},{... | collective-permute-start | bytes 110600 | tf_op jit(solution)/shard_map/ppermute | solution.py:21
  30.3 5.8 %collective-permute-start.3 = (f32[4,18,1,128]{3,2,1,0:T(1,128)S(1)}, f32[4,18,1,128]{3,2,1,0:T(1,128)S(1)}, u32[]{:S(2)}, u32[]{:S(2)}) collective-permute-start(f32[4,18,1,128]{3,2,1,0:T(1,128)S(1)} %get-tuple-element.370), channel_id=1, source_target_pairs={{0,1},{1,2},{2,3},{4,5},{5,6},{6,7},{8,9},{9,10},{10,11},{12,13},{... | collective-permute-start | bytes 110600 | tf_op jit(solution)/shard_map/ppermute | solution.py:19
  42.0 13.4 %all-to-all-start.3 = ((f32[2,128,128]{2,0,1:T(2,128)}), f32[2,128,128]{2,0,1:T(2,128)}, u32[]{:S(2)}, u32[]{:S(2)}) async-start(f32[2,128,128]{2,0,1:T(2,128)} %copy.1072), calls=%async_computation.3 | async-start | bytes 262144 | tf_op jit(solution)/shard_map/all_to_all | solution.py:166
  55.4 12.1 %all-to-all-start.2 = ((f32[2,128,128]{2,0,1:T(2,128)}), f32[2,128,128]{2,0,1:T(2,128)}, u32[]{:S(2)}, u32[]{:S(2)}) async-start(f32[2,128,128]{2,0,1:T(2,128)} %copy.1067), calls=%async_computation.2 | async-start | bytes 262144 | tf_op jit(solution)/shard_map/all_to_all | solution.py:168
  67.5 11.4 %all-to-all-start = ((f32[2,128,128]{2,0,1:T(2,128)}), f32[2,128,128]{2,0,1:T(2,128)}, u32[]{:S(2)}, u32[]{:S(2)}) async-start(f32[2,128,128]{2,0,1:T(2,128)} %copy.1057), calls=%async_computation | async-start | bytes 262144 | tf_op jit(solution)/shard_map/all_to_all | solution.py:169
  78.8 11.4 %all-to-all-start.1 = ((f32[2,128,128]{2,0,1:T(2,128)}), f32[2,128,128]{2,0,1:T(2,128)}, u32[]{:S(2)}, u32[]{:S(2)}) async-start(f32[2,128,128]{2,0,1:T(2,128)} %copy.1063), calls=%async_computation.1 | async-start | bytes 262144 | tf_op jit(solution)/shard_map/all_to_all | solution.py:167
  93.3 11.4 %all-to-all-start.4 = ((f32[16,16,128]{2,1,0:T(8,128)}), f32[16,16,128]{2,1,0:T(8,128)}, u32[]{:S(2)}, u32[]{:S(2)}) async-start(f32[16,16,128]{2,1,0:T(8,128)} %maximum_bitcast_fusion.4), calls=%async_computation.4 | async-start | bytes 262144 | tf_op jit(solution)/shard_map/all_to_all | solution.py:172
  113.8 8.6 %all-to-all-start.8 = ((f32[2,64,128]{2,0,1:T(2,128)}), f32[2,64,128]{2,0,1:T(2,128)S(1)}, u32[]{:S(2)}, u32[]{:S(2)}) async-start(f32[2,64,128]{2,0,1:T(2,128)} %copy.1162), calls=%async_computation.8 | async-start | bytes 131072 | tf_op jit(solution)/shard_map/all_to_all | solution.py:181
  122.3 7.4 %all-to-all-start.7 = ((f32[2,64,128]{2,0,1:T(2,128)}), f32[2,64,128]{2,0,1:T(2,128)S(1)}, u32[]{:S(2)}, u32[]{:S(2)}) async-start(f32[2,64,128]{2,0,1:T(2,128)} %copy.1158), calls=%async_computation.7 | async-start | bytes 131072 | tf_op jit(solution)/shard_map/all_to_all | solution.py:183
  129.7 7.4 %all-to-all-start.5 = ((f32[2,64,128]{2,0,1:T(2,128)}), f32[2,64,128]{2,0,1:T(2,128)S(1)}, u32[]{:S(2)}, u32[]{:S(2)}) async-start(f32[2,64,128]{2,0,1:T(2,128)} %copy.1150), calls=%async_computation.5 | async-start | bytes 131072 | tf_op jit(solution)/shard_map/all_to_all | solution.py:184
  133.0 15.6 %copy-start.49 = (f32[4,16,1,128]{3,2,0,1:T(1,128)S(1)}, f32[4,16,1,128]{3,2,0,1:T(1,128)}, u32[]{:S(2)}) copy-start(f32[4,16,1,128]{3,2,0,1:T(1,128)} %copy-done.48) | copy-start | bytes 98308
  133.0 15.6 %copy-start.51 = (f32[4,16,1,128]{3,2,0,1:T(1,128)S(1)}, f32[4,16,1,128]{3,2,0,1:T(1,128)}, u32[]{:S(2)}) copy-start(f32[4,16,1,128]{3,2,0,1:T(1,128)} %copy-done.50) | copy-start | bytes 98308
  133.1 15.6 %copy-start.53 = (f32[4,16,1,128]{3,2,0,1:T(1,128)S(1)}, f32[4,16,1,128]{3,2,0,1:T(1,128)}, u32[]{:S(2)}) copy-start(f32[4,16,1,128]{3,2,0,1:T(1,128)} %copy-done.52) | copy-start | bytes 98308
  137.1 7.4 %all-to-all-start.6 = ((f32[2,64,128]{2,0,1:T(2,128)}), f32[2,64,128]{2,0,1:T(2,128)S(1)}, u32[]{:S(2)}, u32[]{:S(2)}) async-start(f32[2,64,128]{2,0,1:T(2,128)} %copy.1155), calls=%async_computation.6 | async-start | bytes 131072 | tf_op jit(solution)/shard_map/all_to_all | solution.py:182
  145.3 7.4 %all-to-all-start.9 = ((f32[8,16,128]{2,1,0:T(8,128)}), f32[8,16,128]{2,1,0:T(8,128)S(1)}, u32[]{:S(2)}, u32[]{:S(2)}) async-start(f32[8,16,128]{2,1,0:T(8,128)} %maximum_bitcast_fusion.5), calls=%async_computation.9 | async-start | bytes 131072 | tf_op jit(solution)/shard_map/all_to_all | solution.py:187
  (53 other events, 93.7 us)
where the time goes:
time: 163 us; the launch traced here: 161 us
  starting transfers between devices  61.5 us (38%)
  waiting for transfers between devices  43.9 us (27%)
  other arithmetic  28.2 us (17%)
  local copies, waits for them, and re-layouts  25.5 us (16%)
    ppermute x4, starting transfers between devices, extended_2(): lax.ppermute(tail, axis, [(i, (i + 1) % count) for i in range(ends)])  16.9 us
    unnamed x54, other arithmetic  7.57 us
    all_to_all x1, waiting for transfers between devices, solve_along_x(): lax.all_to_all(solution, 'gx', split_axis=0, concat_axis=1, tiled=True)  5.82 us
    reshape x8, local copies, waits for them, and re-layouts, pack_rows(): jnp.transpose(stacked, (0, 2, 1, 3)).reshape(2, -1, stacked.shape[-1])  5.72 us
    all_to_all x1, waiting for transfers between devices, solve_along_x(): lax.all_to_all(rows[1], 'gx', split_axis=1, concat_axis=0, tiled=True)  5.71 us
    all_to_all x1, starting transfers between devices, solve_along_x(): lax.all_to_all(rows[0], 'gx', split_axis=1, concat_axis=0, tiled=True)  5.71 us
    ppermute x4, starting transfers between devices, extended_2(): lax.ppermute(head, axis, [((i + 1) % count, i) for i in range(ends)])  5.14 us
    all_to_all x1, waiting for transfers between devices, solve_along_x(): lax.all_to_all(rows[2], 'gx', split_axis=1, concat_axis=0, tiled=True)  5.04 us
  transfers between devices with their start and end apart: 18, of which 12 were waited for; matrix products, arithmetic and copies ran while one was open for 15% of the time, Pallas kernels for 0%

commit v1 on v0

v1 whole, which is shorter than its diff:
```python
import functools

import jax
import jax.numpy as jnp
from jax import lax
from jax.experimental import pallas as pl
from jax.experimental.pallas import tpu as pltpu
from jax.sharding import PartitionSpec as P

ADVECT = 0.2
BUOYANT = 0.5
CONDUCT = 0.6
GROUPS = (0, 0, 0, 1)
SCALES = (1.0, CONDUCT)
VMEM = pl.BlockSpec(memory_space=pltpu.VMEM)
ANY = pl.BlockSpec(memory_space=pl.ANY)
F32 = jnp.float32


def call(kernel, ins, outs, scratch=(), in_specs=None, cost=1000000):
    return pl.pallas_call(
        kernel,
        out_shape=[jax.ShapeDtypeStruct(shape, F32) for shape in outs],
        in_specs=in_specs or [VMEM] * len(ins),
        out_specs=[VMEM] * len(outs),
        scratch_shapes=list(scratch),
        compiler_params=pltpu.CompilerParams(vmem_limit_bytes=40 * 1024 * 1024),
        cost_estimate=pl.CostEstimate(flops=cost, bytes_accessed=cost, transcendentals=0),
    )(*ins)


def pick(flag, a, b):
    return jnp.where(flag, a, b)


def pack_kernel(flow, visc, x_even, x_odd, y_even, y_odd, sems):
    nx, ny = flow.shape[1], flow.shape[2]
    x_par = lax.rem(lax.axis_index("gx"), 2)
    y_par = lax.rem(lax.axis_index("gy"), 2)
    copies = []
    for out, row in ((x_even, (1 - x_par) * (nx - 1)), (x_odd, x_par * (nx - 1))):
        copies.append((flow.at[:, row], out.at[pl.ds(0, 4)]))
        copies.append((visc.at[row], out.at[4]))
    for out, row in ((y_even, (1 - y_par) * (ny - 1)), (y_odd, y_par * (ny - 1))):
        copies.append((flow.at[:, :, row], out.at[pl.ds(0, 4)]))
        copies.append((visc.at[:, row], out.at[4]))
    started = [pltpu.make_async_copy(a, b, sems.at[i]) for i, (a, b) in enumerate(copies)]
    for copy in started:
        copy.start()
    for copy in started:
        copy.wait()


def factor_line(load, count, first, last, inv, ratio, left, right):
    for group, scale in enumerate(SCALES):
        here = load(0)
        excess = 1.0 + pick(first, scale * here, 0.0)
        column = None
        columns = []
        for i in range(count):
            if i < count - 1:
                beyond = load(i + 1)
                face = (0.5 * scale) * (here + beyond)
                inverse = 1.0 / (excess + face)
                portion = face * inverse
                ratio[group, i] = portion
                inv[group, i] = inverse
                columns.append(column)
                column = portion if column is None else column * portion
                excess = 1.0 + portion * excess
                here = beyond
            else:
                excess = excess + pick(last, scale * here, 0.0)
                inverse = 1.0 / excess
                inv[group, i] = inverse
                ratio[group, i] = inverse
                columns.append(column)
        response = inverse
        onward = column * inverse
        right[group, count - 1] = response
        left[group, count - 1] = onward
        for i in range(count - 2, -1, -1):
            portion = ratio[group, i]
            response = portion * response
            start = inv[group, i] if i == 0 else columns[i] * inv[group, i]
            onward = start + portion * onward
            right[group, i] = response
            left[group, i] = onward


def factor_kernel(visc, ivx, rx, cx, wx, ivy, ry, cy, wy):
    nx, ny, nz = visc.shape
    ix, iy = lax.axis_index("gx"), lax.axis_index("gy")
    mx, my = lax.axis_size("gx"), lax.axis_size("gy")
    factor_line(lambda i: visc[i], nx, ix == 0, ix == mx - 1, ivx, rx, cx, wx)
    rows = visc.reshape(nx * ny, nz)
    factor_line(
        lambda j: rows[pl.ds(j, nx, stride=ny), :], ny, iy == 0, iy == my - 1, ivy, ry, cy, wy
    )


def source_kernel(flow, visc, x_even, x_odd, y_even, y_odd, cx, wx, source, message):
    _, nx, ny, nz = flow.shape
    x_par = lax.rem(lax.axis_index("gx"), 2) == 0
    y_par = lax.rem(lax.axis_index("gy"), 2) == 0
    row = lax.broadcasted_iota(jnp.int32, (ny, nz), 0)
    left = [None] * 4
    right = [None] * 4
    for i in range(nx):
        velocity = [ADVECT * 0.5 * flow[c, i] for c in range(3)]
        temperature = None
        for c in (3, 0, 1, 2):
            f = flow[c, i]
            if i == 0:
                down = pick(x_par, x_odd[c], x_even[c])
            else:
                down = flow[c, i - 1]
            if i == nx - 1:
                up = pick(x_par, x_even[c], x_odd[c])
            else:
                up = flow[c, i + 1]
            y_low = pick(y_par, y_odd[c, pl.ds(i, 1)], y_even[c, pl.ds(i, 1)])
            y_high = pick(y_par, y_even[c, pl.ds(i, 1)], y_odd[c, pl.ds(i, 1)])
            below = pick(row == 0, y_low, pltpu.roll(f, 1, 0))
            above = pick(row == ny - 1, y_high, pltpu.roll(f, ny - 1, 0))
            z_low = pltpu.roll(f, 1, 1)
            z_high = pltpu.roll(f, nz - 1, 1)
            s = f - (
                velocity[0] * (up - down)
                + velocity[1] * (above - below)
                + velocity[2] * (z_high - z_low)
            )
            if c == 3:
                temperature = f
            if c == 2:
                s = s + BUOYANT * temperature
            source[c, i] = s
            group = GROUPS[c]
            a, b = cx[group, i] * s, wx[group, i] * s
            left[c] = a if i == 0 else left[c] + a
            right[c] = b if i == 0 else right[c] + b
    for c in range(4):
        message[c] = left[c]
        message[4 + c] = right[c]
    beyond = pick(x_par, x_even[4], x_odd[4])
    face = 0.5 * (visc[nx - 1] + beyond)
    for group, scale in enumerate(SCALES):
        message[8 + group] = cx[group, 0]
        message[10 + group] = cx[group, nx - 1]
        message[12 + group] = wx[group, nx - 1] + 1.0 / (scale * face)


def merge_kernel(axis, bit, last, mine, theirs, union, saved):
    is_left = (lax.axis_index(axis) & bit) == 0
    next_left = (lax.axis_index(axis) & (2 * bit)) == 0

    def a(k):
        return pick(is_left, mine[k], theirs[k])

    def b(k):
        return pick(is_left, theirs[k], mine[k])

    for group in range(2):
        a_lr, b_lr = a(10 + group), b(10 + group)
        m = 1.0 / (a(12 + group) + b(8 + group))
        pa, pb = m * a_lr, m * b_lr
        saved[4 + group] = pa
        saved[6 + group] = pb
        out_ll = a(8 + group) - a_lr * pa
        out_rr = b(12 + group) - b_lr * pb
        if last:
            union[4 + group] = pick(next_left, out_rr, out_ll)
        else:
            union[8 + group] = out_ll
            union[10 + group] = a_lr * pb
            union[12 + group] = out_rr
        for c in range(4):
            if GROUPS[c] != group:
                continue
            d = b(c) - a(4 + c)
            saved[c] = m * d
            out_l = a(c) + pa * d
            out_r = b(4 + c) - pb * d
            if last:
                union[c] = pick(next_left, out_r, out_l)
            else:
                union[c] = out_l
                union[4 + c] = out_r


def near_of(axis, message):
    is_left = (lax.axis_index(axis) & 1) == 0
    rows = jnp.where(is_left, message[4:8], message[0:4])
    coef = jnp.where(is_left, message[12:14], message[8:10])
    return jnp.concatenate([rows, coef], 0)


def fluxes(axis, mine, theirs, saved):
    index = lax.axis_index(axis)
    bit = lax.axis_size(axis) // 2
    is_left = (index & bit) == 0
    result = []
    for c in range(4):
        group = GROUPS[c]
        m = 1.0 / (mine[4 + group] + theirs[4 + group])
        d = theirs[c] - mine[c]
        flux = m * pick(is_left, d, -d)
        zero = jnp.zeros_like(flux)
        low = pick(is_left, zero, flux)
        high = pick(is_left, flux, zero)
        this = bit
        for part in saved[::-1]:
            this = this // 2
            flux = part[c] + part[6 + group] * high + part[4 + group] * low
            side = (index & this) == 0
            low, high = pick(side, low, flux), pick(side, flux, high)
        result.append((low, high))
    return result


def local_kernel(source, ivx, rx, cx, wx, local_t, cx_t, wx_t, scratch):
    _, nx, ny, nz = source.shape
    for c in range(4):
        group = GROUPS[c]
        running = source[c, 0]
        forward = [running]
        for i in range(1, nx):
            running = source[c, i] + rx[group, i - 1] * running
            forward.append(running)
        value = running * ivx[group, nx - 1]
        scratch[c, pl.ds((nx - 1) * ny, ny)] = value
        for i in range(nx - 2, -1, -1):
            value = forward[i] * ivx[group, i] + rx[group, i] * value
            scratch[c, pl.ds(i * ny, ny)] = value
        for j in range(ny):
            local_t[c, j] = scratch[c, pl.ds(j, nx, stride=ny), :]
    for group in range(2):
        c_rows = cx.at[group].reshape(nx * ny, nz)
        w_rows = wx.at[group].reshape(nx * ny, nz)
        for j in range(ny):
            cx_t[group, j] = c_rows[pl.ds(j, nx, stride=ny), :]
            wx_t[group, j] = w_rows[pl.ds(j, nx, stride=ny), :]


def y_start_kernel(stages, *refs):
    mine, theirs = refs[0], refs[1]
    saved = refs[2 : 2 + stages]
    visc, y_even, y_odd, local_t, cx_t, wx_t, cy, wy, solved, message, flux_low, flux_high = refs[2 + stages :]
    _, ny, nx, nz = local_t.shape
    for c, (low, high) in enumerate(fluxes("gx", mine, theirs, saved)):
        flux_low[c] = low
        flux_high[c] = high
    for c in range(4):
        group = GROUPS[c]
        left = right = None
        for j in range(ny):
            low = flux_low[c, pl.ds(j, 1)]
            high = flux_high[c, pl.ds(j, 1)]
            value = local_t[c, j] + (wx_t[group, j] * high - cx_t[group, j] * low)
            solved[c, j] = value
            a, b = cy[group, j] * value, wy[group, j] * value
            left = a if j == 0 else left + a
            right = b if j == 0 else right + b
        message[c] = left
        message[4 + c] = right
    y_par = lax.rem(lax.axis_index("gy"), 2) == 0
    beyond = pick(y_par, y_even[4], y_odd[4])
    edge = visc.reshape(nx * ny, nz)[pl.ds(ny - 1, nx, stride=ny), :]
    face = 0.5 * (edge + beyond)
    for group, scale in enumerate(SCALES):
        message[8 + group] = cy[group, 0]
        message[10 + group] = cy[group, ny - 1]
        message[12 + group] = wy[group, ny - 1] + 1.0 / (scale * face)


def y_local_kernel(solved, ivy, ry, local):
    _, ny, nx, nz = solved.shape
    for c in range(4):
        group = GROUPS[c]
        running = solved[c, 0]
        forward = [running]
        for j in range(1, ny):
            running = solved[c, j] + ry[group, j - 1] * running
            forward.append(running)
        value = running * ivy[group, ny - 1]
        local[c, ny - 1] = value
        for j in range(ny - 2, -1, -1):
            value = forward[j] * ivy[group, j] + ry[group, j] * value
            local[c, j] = value


def finish_kernel(stages, *refs):
    mine, theirs = refs[0], refs[1]
    saved = refs[2 : 2 + stages]
    local, cy, wy, out = refs[2 + stages :]
    _, ny, nx, nz = local.shape
    ends = fluxes("gy", mine, theirs, saved)
    for c in range(4):
        group = GROUPS[c]
        low, high = ends[c]
        rows = out.at[c].reshape(nx * ny, nz)
        for j in range(ny):
            value = local[c, j] + (wy[group, j] * high - cy[group, j] * low)
            rows[pl.ds(j, nx, stride=ny), :] = value


def reduce_line(axis, message):
    count = lax.axis_size(axis)
    shape = message.shape[1:]
    saved = []
    bit = 1
    if count == 2:
        message = near_of(axis, message)
    while bit * 2 < count:
        theirs = lax.ppermute(message, axis, [(i, i ^ bit) for i in range(count)])
        last = bit * 4 == count
        message, part = call(
            functools.partial(merge_kernel, axis, bit, last),
            (message, theirs),
            [(6 if last else 14,) + shape, (8,) + shape],
        )
        saved.append(part)
        bit *= 2
    theirs = lax.ppermute(message, axis, [(i, i ^ bit) for i in range(count)])
    return message, theirs, saved


def per_device(flow, visc):
    fields, nx, ny, nz = flow.shape
    mx, my = lax.axis_size("gx"), lax.axis_size("gy")
    edges = call(
        pack_kernel,
        (flow, visc),
        [(5, ny, nz), (5, ny, nz), (5, nx, nz), (5, nx, nz)],
        scratch=[pltpu.SemaphoreType.DMA((8,))],
        in_specs=[ANY, ANY],
    )
    x_even = lax.ppermute(edges[0], "gx", [(i, i ^ 1) for i in range(mx)])
    y_even = lax.ppermute(edges[2], "gy", [(i, i ^ 1) for i in range(my)])
    odd = lambda n: [(i, i + 1) for i in range(1, n - 1, 2)] + [(i + 1, i) for i in range(1, n - 1, 2)]
    x_odd = lax.ppermute(edges[1], "gx", odd(mx))
    y_odd = lax.ppermute(edges[3], "gy", odd(my))

    along_x, along_y = (2, nx, ny, nz), (2, ny, nx, nz)
    ivx, rx, cx, wx, ivy, ry, cy, wy = call(
        factor_kernel, (visc,), [along_x] * 4 + [along_y] * 4, cost=8000000
    )
    source, message = call(
        source_kernel,
        (flow, visc, x_even, x_odd, y_even, y_odd, cx, wx),
        [(fields, nx, ny, nz), (14, ny, nz)],
    )
    local_t, cx_t, wx_t = call(
        local_kernel,
        (source, ivx, rx, cx, wx),
        [(fields, ny, nx, nz), along_y, along_y],
        scratch=[pltpu.VMEM((fields, nx * ny, nz), F32)],
        cost=8000000,
    )
    mine, theirs, saved = reduce_line("gx", message)
    solved, message_y = call(
        functools.partial(y_start_kernel, len(saved)),
        (mine, theirs, *saved, visc, y_even, y_odd, local_t, cx_t, wx_t, cy, wy),
        [(fields, ny, nx, nz), (14, nx, nz)],
        scratch=[pltpu.VMEM((fields, ny, nz), F32)] * 2,
    )
    (local_y,) = call(y_local_kernel, (solved, ivy, ry), [(fields, ny, nx, nz)], cost=8000000)
    mine, theirs, saved = reduce_line("gy", message_y)
    (out,) = call(
        functools.partial(finish_kernel, len(saved)),
        (mine, theirs, *saved, local_y, cy, wy),
        [(fields, nx, ny, nz)],
    )
    return out


def solution(mesh):
    placed = (P(None, "gx", "gy", None), P("gx", "gy", None))
    return jax.shard_map(
        per_device, mesh=mesh, in_specs=placed, out_specs=P(None, "gx", "gy", None), check_vma=False
    )
```

time: 163 us -> 45.4 us (0.28); the launches traced: 161 us -> 45.2 us
  starting transfers between devices: 61.5 us -> 17.6 us
  other arithmetic: 28.2 us -> 0 us
  waiting for transfers between devices: 43.9 us -> 19.2 us
  local copies, waits for them, and re-layouts: 25.5 us -> 2.18 us
  Pallas kernels: 0 us -> 6.1 us
    all_to_all x10 -> x0, waiting for transfers between devices: 39.9 us -> none  [the longest x1 5.82 us: solve_along_x(): lax.all_to_all(solution, 'gx', split_axis=0, concat_axis=1, tiled=True)]
    all_to_all x10 -> x0, starting transfers between devices: 39.5 us -> none  [the longest x1 5.71 us: solve_along_x(): lax.all_to_all(rows[0], 'gx', split_axis=1, concat_axis=0, tiled=True)]
    ppermute x8 -> x9, waiting for transfers between devices: 3.97 us -> 19.2 us  [the longest x5 19 us: reduce_line(): theirs = lax.ppermute(message, axis, [(i, i ^ bit) for i in range(count)])]
    mul x14 -> x0, other arithmetic: 10.4 us -> none  [the longest x5 4.55 us: sweep_down(): forward.append(running * inverse[k])]
    unnamed x54 -> x0, other arithmetic: 7.57 us -> none
    slice x9 -> x0, local copies, waits for them, and re-layouts: 6.36 us -> none  [the longest x2 3 us: advect(): along_z = 0.5 * (jnp.roll(flow_state, -1, 3) - jnp.roll(flow_state, 1, 3))]
    pallas_call x0 -> x10, Pallas kernels: none -> 6.1 us  [call(): pl.pallas_call(kernel, out_shape=[jax.ShapeDtypeStruct(shape, F32) for sh...]
    reshape x9 -> x0, local copies, waits for them, and re-layouts: 5.73 us -> none  [the longest x8 5.72 us: pack_rows(): jnp.transpose(stacked, (0, 2, 1, 3)).reshape(2, -1, stacked.shape[-1])]
  transfers between devices with their start and end apart: 18 -> 9, of which waited for: 12 -> 6; matrix products, arithmetic and copies ran while one was open for 15% -> 0% of each run, Pallas kernels for 0% -> 6%
where the time goes in v1:
time: 45.4 us; the launch traced here: 45.2 us
  waiting for transfers between devices  19.2 us (42%)
  starting transfers between devices  17.6 us (39%)
  Pallas kernels  6.1 us (13%)
  local copies, waits for them, and re-layouts  2.18 us (5%)
    ppermute x5, waiting for transfers between devices, reduce_line(): theirs = lax.ppermute(message, axis, [(i, i ^ bit) for i in range(count)])  19 us
    ppermute x5, starting transfers between devices, reduce_line(): theirs = lax.ppermute(message, axis, [(i, i ^ bit) for i in range(count)])  13.2 us
    pallas_call x10, Pallas kernels, call(): pl.pallas_call(kernel, out_shape=[jax.ShapeDtypeStruct(shape, F32) for sh...  6.1 us
    ppermute x1, starting transfers between devices, per_device(): x_even = lax.ppermute(edges[0], 'gx', [(i, i ^ 1) for i in range(mx)])  3 us
    unnamed x8, local copies, waits for them, and re-layouts  2.18 us
  transfers between devices with their start and end apart: 9, of which 6 were waited for; matrix products, arithmetic and copies ran while one was open for 0% of the time, Pallas kernels for 6%

profile of v1, /device:TPU:0, one launch (start us, length us, event | category | flops | bytes accessed | tf_op | source)
XLA Modules:
  0.0 45.2 jit_solution(2448560690837436246)
XLA Ops:
  0.0 1.2 %copy-done = f32[4,16,32,128]{3,2,1,0:T(8,128)S(1)} copy-done((f32[4,16,32,128]{3,2,1,0:T(8,128)S(1)}, f32[4,16,32,128]{3,2,1,0:T(8,128)}, u32[]{:S(2)}) %copy-start) | copy-done | bytes 1048600
  1.2 0.9 %copy-done.2 = f32[16,32,128]{2,1,0:T(8,128)S(1)} copy-done((f32[16,32,128]{2,1,0:T(8,128)S(1)}, f32[16,32,128]{2,1,0:T(8,128)}, u32[]{:S(2)}) %copy-start.2) | copy-done | bytes 262168
  2.2 0.3 shard_map.28
  2.4 3.0 %collective-permute-start = (f32[5,32,128]{2,1,0:T(8,128)S(1)}, f32[5,32,128]{2,1,0:T(8,128)S(1)}, u32[]{:S(2)}, u32[]{:S(2)}) collective-permute-start(f32[5,32,128]{2,1,0:T(8,128)S(1)} %get-tuple-element.30), channel_id=1, source_target_pairs={{0,4},{4,0},{8,12},{12,8},{16,20},{20,16},{24,28},{28,24},{1,5},{5... | collective-permute-start | bytes 245768 | tf_op jit(solution)/shard_map/ppermute | solution.py:338
  5.4 0.7 %collective-permute-start.1 = (f32[5,32,128]{2,1,0:T(8,128)S(1)}, f32[5,32,128]{2,1,0:T(8,128)S(1)}, u32[]{:S(2)}, u32[]{:S(2)}) collective-permute-start(f32[5,32,128]{2,1,0:T(8,128)S(1)} %get-tuple-element.31), channel_id=1, source_target_pairs={{4,8},{12,16},{20,24},{8,4},{16,12},{24,20},{5,9},{13,17},{21,25},... | collective-permute-start | bytes 245768 | tf_op jit(solution)/shard_map/ppermute | solution.py:341
  6.1 0.1 collective-permute-start.2
  6.2 0.7 %collective-permute-start.3 = (f32[5,16,128]{2,1,0:T(8,128)S(1)}, f32[5,16,128]{2,1,0:T(8,128)S(1)}, u32[]{:S(2)}, u32[]{:S(2)}) collective-permute-start(f32[5,16,128]{2,1,0:T(8,128)S(1)} %get-tuple-element.33), channel_id=1, source_target_pairs={{1,2},{2,1},{5,6},{6,5},{9,10},{10,9},{13,14},{14,13},{17,18},{18,... | collective-permute-start | bytes 122888 | tf_op jit(solution)/shard_map/ppermute | solution.py:342
  6.9 0.8 %shard_map.29 = (f32[2,16,32,128]{3,2,1,0:T(8,128)S(1)}, f32[2,16,32,128]{3,2,1,0:T(8,128)S(1)}, f32[2,16,32,128]{3,2,1,0:T(8,128)S(1)}, f32[2,16,32,128]{3,2,1,...) custom-call(f32[16,32,128]{2,1,0:T(8,128)S(1)} %copy-done.3), custom_call_target="tpu_custom_call" | custom-call | flops 8000000 | bytes 8000000 | tf_op jit(solution)/shard_map/pallas_call | solution.py:21
  7.7 0.2 collective-permute-done.x_even
  7.9 0.9 %shard_map.30 = (f32[4,16,32,128]{3,2,1,0:T(8,128)S(1)}, f32[14,32,128]{2,1,0:T(8,128)S(1)}) custom-call(f32[4,16,32,128]{3,2,1,0:T(8,128)S(1)} %copy-done.1, f32[16,32,128]{2,1,0:T(8,128)S(1)} %copy-done.3, f32[5,32,128]{2,1,0:T(8,128)S(1)} %collective-permute-done.x_even, f32[5,32,128]{2,1,0:T(8,128)S(1)} %collective-permute-done.1.x_odd, ...), custom_call_target="tpu_custom_call" | custom-call | flops 1000000 | bytes 1000000 | tf_op jit(solution)/shard_map/pallas_call | solution.py:21
  8.8 5.0 %collective-permute-start.4 = (f32[14,32,128]{2,1,0:T(8,128)S(1)}, f32[14,32,128]{2,1,0:T(8,128)S(1)}, u32[]{:S(2)}, u32[]{:S(2)}) collective-permute-start(f32[14,32,128]{2,1,0:T(8,128)S(1)} %get-tuple-element.36.mine), channel_id=1, source_target_pairs={{0,4},{4,0},{8,12},{12,8},{16,20},{20,16},{24,28},{28,24},{1,5},{5... | collective-permute-start | bytes 688136 | tf_op jit(solution)/shard_map/ppermute | solution.py:315
  13.8 4.0 %collective-permute-done.4.theirs = f32[14,32,128]{2,1,0:T(8,128)S(1)} collective-permute-done((f32[14,32,128]{2,1,0:T(8,128)S(1)}, f32[14,32,128]{2,1,0:T(8,128)S(1)}, u32[]{:S(2)}, u32[]{:S(2)}) %collective-permute-start.4) | collective-permute-done | bytes 229408 | tf_op jit(solution)/shard_map/ppermute | solution.py:315
  17.9 5.1 %collective-permute-start.5 = (f32[14,32,128]{2,1,0:T(8,128)S(1)}, f32[14,32,128]{2,1,0:T(8,128)S(1)}, u32[]{:S(2)}, u32[]{:S(2)}) collective-permute-start(f32[14,32,128]{2,1,0:T(8,128)S(1)} %get-tuple-element.37.mine), channel_id=1, source_target_pairs={{0,8},{4,12},{8,0},{12,4},{16,24},{20,28},{24,16},{28,20},{1,9},{5... | collective-permute-start | bytes 688136 | tf_op jit(solution)/shard_map/ppermute | solution.py:315
  22.9 6.4 %collective-permute-done.5.theirs = f32[14,32,128]{2,1,0:T(8,128)S(1)} collective-permute-done((f32[14,32,128]{2,1,0:T(8,128)S(1)}, f32[14,32,128]{2,1,0:T(8,128)S(1)}, u32[]{:S(2)}, u32[]{:S(2)}) %collective-permute-start.5) | collective-permute-done | bytes 229408 | tf_op jit(solution)/shard_map/ppermute | solution.py:315
  29.4 3.0 %collective-permute-start.6 = (f32[6,32,128]{2,1,0:T(8,128)S(1)}, f32[6,32,128]{2,1,0:T(8,128)S(1)}, u32[]{:S(2)}, u32[]{:S(2)}) collective-permute-start(f32[6,32,128]{2,1,0:T(8,128)S(1)} %get-tuple-element.38.refs_0_), channel_id=1, source_target_pairs={{0,16},{4,20},{8,24},{12,28},{16,0},{20,4},{24,8},{28,12},{1,17},{... | collective-permute-start | bytes 294920 | tf_op jit(solution)/shard_map/ppermute | solution.py:324
  32.4 1.4 %shard_map.33 = (f32[4,32,16,128]{3,2,1,0:T(8,128)S(1)}, f32[2,32,16,128]{3,2,1,0:T(8,128)S(1)}, f32[2,32,16,128]{3,2,1,0:T(8,128)S(1)}) custom-call(f32[4,16,32,128]{3,2,1,0:T(8,128)S(1)} %get-tuple-element.41.source, f32[2,16,32,128]{3,2,1,0:T(8,128)S(1)} %get-tuple-element.42.ivx, f32[2,16,32,128]{3,2,1,0:T(8,128)S(1)} %get-tuple-element.43.rx, ...), custom_call_target="tpu_custom_call" | custom-call | flops 8000000 | bytes 8000000 | tf_op jit(solution)/shard_map/pallas_call | solution.py:21
  33.8 3.5 %collective-permute-done.6.refs_1_ = f32[6,32,128]{2,1,0:T(8,128)S(1)} collective-permute-done((f32[6,32,128]{2,1,0:T(8,128)S(1)}, f32[6,32,128]{2,1,0:T(8,128)S(1)}, u32[]{:S(2)}, u32[]{:S(2)}) %collective-permute-start.6) | collective-permute-done | bytes 98336 | tf_op jit(solution)/shard_map/ppermute | solution.py:324
  37.3 0.3 shard_map.34
  37.7 0.1 collective-permute-start.7
  37.7 1.3 %collective-permute-done.7.theirs = f32[14,16,128]{2,1,0:T(8,128)S(1)} collective-permute-done((f32[14,16,128]{2,1,0:T(8,128)S(1)}, f32[14,16,128]{2,1,0:T(8,128)S(1)}, u32[]{:S(2)}, u32[]{:S(2)}) %collective-permute-start.7) | collective-permute-done | bytes 114720 | tf_op jit(solution)/shard_map/ppermute | solution.py:315
  39.1 0.1 collective-permute-start.8
  39.2 0.3 shard_map.36.refs_3_
  39.5 3.8 %collective-permute-done.8.refs_1_ = f32[6,16,128]{2,1,0:T(8,128)S(1)} collective-permute-done((f32[6,16,128]{2,1,0:T(8,128)S(1)}, f32[6,16,128]{2,1,0:T(8,128)S(1)}, u32[]{:S(2)}, u32[]{:S(2)}) %collective-permute-start.8) | collective-permute-done | bytes 49184 | tf_op jit(solution)/shard_map/ppermute | solution.py:324
  43.3 1.9 %shard_map.37 = f32[4,16,32,128]{3,2,1,0:T(8,128)} custom-call(f32[6,16,128]{2,1,0:T(8,128)S(1)} %get-tuple-element.50.refs_0_, f32[6,16,128]{2,1,0:T(8,128)S(1)} %collective-permute-done.8.refs_1_, f32[8,16,128]{2,1,0:T(8,128)S(1)} %get-tuple-element.51.refs_2_, f32[4,32,16,128]{3,2,1,0:T(8,128)S(1)} %shard_map.36.refs_3_, ...), custom_call_target="tpu_custom_call" | custom-call | flops 1000000 | bytes 1000000 | tf_op jit(solution)/shard_map/pallas_call | solution.py:21
  (12 shorter events, 0.2 us)
Async XLA Ops:
  0.0 1.2 %copy-start = (f32[4,16,32,128]{3,2,1,0:T(8,128)S(1)}, f32[4,16,32,128]{3,2,1,0:T(8,128)}, u32[]{:S(2)}) copy-start(f32[4,16,32,128]{3,2,1,0:T(8,128)} %flow.3) | copy-start | bytes 3145732
  1.2 0.9 %copy-start.2 = (f32[16,32,128]{2,1,0:T(8,128)S(1)}, f32[16,32,128]{2,1,0:T(8,128)}, u32[]{:S(2)}) copy-start(f32[16,32,128]{2,1,0:T(8,128)} %refs_4_.1) | copy-start | bytes 786436
  2.2 4.7 %copy-start.3 = (f32[16,32,128]{2,1,0:T(8,128)S(1)}, f32[16,32,128]{2,1,0:T(8,128)}, u32[]{:S(2)}) copy-start(f32[16,32,128]{2,1,0:T(8,128)} %refs_4_.1) | copy-start | bytes 786436
  2.2 5.7 %copy-start.1 = (f32[4,16,32,128]{3,2,1,0:T(8,128)S(1)}, f32[4,16,32,128]{3,2,1,0:T(8,128)}, u32[]{:S(2)}) copy-start(f32[4,16,32,128]{3,2,1,0:T(8,128)} %flow.3) | copy-start | bytes 3145732
  2.4 5.4 %collective-permute-start = (f32[5,32,128]{2,1,0:T(8,128)S(1)}, f32[5,32,128]{2,1,0:T(8,128)S(1)}, u32[]{:S(2)}, u32[]{:S(2)}) collective-permute-start(f32[5,32,128]{2,1,0:T(8,128)S(1)} %get-tuple-element.30), channel_id=1, source_target_pairs={{0,4},{4,0},{8,12},{12,8},{16,20},{20,16},{24,28},{28,24},{1,5},{5... | collective-permute-start | bytes 245768 | tf_op jit(solution)/shard_map/ppermute | solution.py:338
  5.4 2.4 %collective-permute-start.1 = (f32[5,32,128]{2,1,0:T(8,128)S(1)}, f32[5,32,128]{2,1,0:T(8,128)S(1)}, u32[]{:S(2)}, u32[]{:S(2)}) collective-permute-start(f32[5,32,128]{2,1,0:T(8,128)S(1)} %get-tuple-element.31), channel_id=1, source_target_pairs={{4,8},{12,16},{20,24},{8,4},{16,12},{24,20},{5,9},{13,17},{21,25},... | collective-permute-start | bytes 245768 | tf_op jit(solution)/shard_map/ppermute | solution.py:341
  6.1 1.6 %collective-permute-start.2 = (f32[5,16,128]{2,1,0:T(8,128)S(1)}, f32[5,16,128]{2,1,0:T(8,128)S(1)}, u32[]{:S(2)}, u32[]{:S(2)}) collective-permute-start(f32[5,16,128]{2,1,0:T(8,128)S(1)} %get-tuple-element.32), channel_id=1, source_target_pairs={{0,1},{1,0},{2,3},{3,2},{4,5},{5,4},{6,7},{7,6},{8,9},{9,8},{10,11... | collective-permute-start | bytes 122888 | tf_op jit(solution)/shard_map/ppermute | solution.py:339
  6.2 1.5 %collective-permute-start.3 = (f32[5,16,128]{2,1,0:T(8,128)S(1)}, f32[5,16,128]{2,1,0:T(8,128)S(1)}, u32[]{:S(2)}, u32[]{:S(2)}) collective-permute-start(f32[5,16,128]{2,1,0:T(8,128)S(1)} %get-tuple-element.33), channel_id=1, source_target_pairs={{1,2},{2,1},{5,6},{6,5},{9,10},{10,9},{13,14},{14,13},{17,18},{18,... | collective-permute-start | bytes 122888 | tf_op jit(solution)/shard_map/ppermute | solution.py:342
  8.8 9.0 %collective-permute-start.4 = (f32[14,32,128]{2,1,0:T(8,128)S(1)}, f32[14,32,128]{2,1,0:T(8,128)S(1)}, u32[]{:S(2)}, u32[]{:S(2)}) collective-permute-start(f32[14,32,128]{2,1,0:T(8,128)S(1)} %get-tuple-element.36.mine), channel_id=1, source_target_pairs={{0,4},{4,0},{8,12},{12,8},{16,20},{20,16},{24,28},{28,24},{1,5},{5... | collective-permute-start | bytes 688136 | tf_op jit(solution)/shard_map/ppermute | solution.py:315
  17.9 11.5 %collective-permute-start.5 = (f32[14,32,128]{2,1,0:T(8,128)S(1)}, f32[14,32,128]{2,1,0:T(8,128)S(1)}, u32[]{:S(2)}, u32[]{:S(2)}) collective-permute-start(f32[14,32,128]{2,1,0:T(8,128)S(1)} %get-tuple-element.37.mine), channel_id=1, source_target_pairs={{0,8},{4,12},{8,0},{12,4},{16,24},{20,28},{24,16},{28,20},{1,9},{5... | collective-permute-start | bytes 688136 | tf_op jit(solution)/shard_map/ppermute | solution.py:315
  29.4 7.9 %collective-permute-start.6 = (f32[6,32,128]{2,1,0:T(8,128)S(1)}, f32[6,32,128]{2,1,0:T(8,128)S(1)}, u32[]{:S(2)}, u32[]{:S(2)}) collective-permute-start(f32[6,32,128]{2,1,0:T(8,128)S(1)} %get-tuple-element.38.refs_0_), channel_id=1, source_target_pairs={{0,16},{4,20},{8,24},{12,28},{16,0},{20,4},{24,8},{28,12},{1,17},{... | collective-permute-start | bytes 294920 | tf_op jit(solution)/shard_map/ppermute | solution.py:324
  37.7 1.4 %collective-permute-start.7 = (f32[14,16,128]{2,1,0:T(8,128)S(1)}, f32[14,16,128]{2,1,0:T(8,128)S(1)}, u32[]{:S(2)}, u32[]{:S(2)}) collective-permute-start(f32[14,16,128]{2,1,0:T(8,128)S(1)} %get-tuple-element.49.mine), channel_id=1, source_target_pairs={{0,1},{1,0},{2,3},{3,2},{4,5},{5,4},{6,7},{7,6},{8,9},{9,8},{10,11... | collective-permute-start | bytes 344072 | tf_op jit(solution)/shard_map/ppermute | solution.py:315
  39.1 4.2 %collective-permute-start.8 = (f32[6,16,128]{2,1,0:T(8,128)S(1)}, f32[6,16,128]{2,1,0:T(8,128)S(1)}, u32[]{:S(2)}, u32[]{:S(2)}) collective-permute-start(f32[6,16,128]{2,1,0:T(8,128)S(1)} %get-tuple-element.50.refs_0_), channel_id=1, source_target_pairs={{0,2},{1,3},{2,0},{3,1},{4,6},{5,7},{6,4},{7,5},{8,10},{9,11},{10,... | collective-permute-start | bytes 147464 | tf_op jit(solution)/shard_map/ppermute | solution.py:324

commit v2 on v1

--- a/solution.py
+++ b/solution.py
@@ -13,16 +13,16 @@
 GROUPS = (0, 0, 0, 1)
 SCALES = (1.0, CONDUCT)
 VMEM = pl.BlockSpec(memory_space=pltpu.VMEM)
-ANY = pl.BlockSpec(memory_space=pl.ANY)
+HBM = pl.BlockSpec(memory_space=pltpu.HBM)
 F32 = jnp.float32
 
 
-def call(kernel, ins, outs, scratch=(), in_specs=None, cost=1000000):
+def call(kernel, ins, outs, scratch=(), in_specs=None, out_specs=None, cost=1000000):
     return pl.pallas_call(
         kernel,
         out_shape=[jax.ShapeDtypeStruct(shape, F32) for shape in outs],
         in_specs=in_specs or [VMEM] * len(ins),
-        out_specs=[VMEM] * len(outs),
+        out_specs=out_specs or [VMEM] * len(outs),
         scratch_shapes=list(scratch),
         compiler_params=pltpu.CompilerParams(vmem_limit_bytes=40 * 1024 * 1024),
         cost_estimate=pl.CostEstimate(flops=cost, bytes_accessed=cost, transcendentals=0),
@@ -101,8 +101,10 @@
 
 def source_kernel(flow, visc, x_even, x_odd, y_even, y_odd, cx, wx, source, message):
     _, nx, ny, nz = flow.shape
-    x_par = lax.rem(lax.axis_index("gx"), 2) == 0
-    y_par = lax.rem(lax.axis_index("gy"), 2) == 0
+    ix, iy = lax.axis_index("gx"), lax.axis_index("gy")
+    x_par, y_par = lax.rem(ix, 2) == 0, lax.rem(iy, 2) == 0
+    x_first, x_last = ix == 0, ix == lax.axis_size("gx") - 1
+    y_first, y_last = iy == 0, iy == lax.axis_size("gy") - 1
     row = lax.broadcasted_iota(jnp.int32, (ny, nz), 0)
     left = [None] * 4
     right = [None] * 4
@@ -112,15 +114,17 @@
         for c in (3, 0, 1, 2):
             f = flow[c, i]
             if i == 0:
-                down = pick(x_par, x_odd[c], x_even[c])
+                down = pick(x_first, 0.0, pick(x_par, x_odd[c], x_even[c]))
             else:
                 down = flow[c, i - 1]
             if i == nx - 1:
-                up = pick(x_par, x_even[c], x_odd[c])
+                up = pick(x_last, 0.0, pick(x_par, x_even[c], x_odd[c]))
             else:
                 up = flow[c, i + 1]
             y_low = pick(y_par, y_odd[c, pl.ds(i, 1)], y_even[c, pl.ds(i, 1)])
             y_high = pick(y_par, y_even[c, pl.ds(i, 1)], y_odd[c, pl.ds(i, 1)])
+            y_low = pick(y_first, 0.0, y_low)
+            y_high = pick(y_last, 0.0, y_high)
             below = pick(row == 0, y_low, pltpu.roll(f, 1, 0))
             above = pick(row == ny - 1, y_high, pltpu.roll(f, ny - 1, 0))
             z_low = pltpu.roll(f, 1, 1)
@@ -292,16 +296,21 @@
 def finish_kernel(stages, *refs):
     mine, theirs = refs[0], refs[1]
     saved = refs[2 : 2 + stages]
-    local, cy, wy, out = refs[2 + stages :]
+    local, cy, wy, out, buffer, sems = refs[2 + stages :]
     _, ny, nx, nz = local.shape
     ends = fluxes("gy", mine, theirs, saved)
+    copies = []
     for c in range(4):
         group = GROUPS[c]
         low, high = ends[c]
-        rows = out.at[c].reshape(nx * ny, nz)
+        rows = buffer.at[c].reshape(nx * ny, nz)
         for j in range(ny):
             value = local[c, j] + (wy[group, j] * high - cy[group, j] * low)
             rows[pl.ds(j, nx, stride=ny), :] = value
+        copies.append(pltpu.make_async_copy(buffer.at[c], out.at[c], sems.at[c]))
+        copies[-1].start()
+    for copy in copies:
+        copy.wait()
 
 
 def reduce_line(axis, message):
@@ -333,13 +342,18 @@
         (flow, visc),
         [(5, ny, nz), (5, ny, nz), (5, nx, nz), (5, nx, nz)],
         scratch=[pltpu.SemaphoreType.DMA((8,))],
-        in_specs=[ANY, ANY],
-    )
+        in_specs=[HBM, HBM],
+    )
+    pairs = []
+    for i in range(mx):
+        for j in range(my):
+            inner = 0 < i < mx - 1
+            partner = ((i - 1 ^ 1) + 1, j) if inner else (i, j ^ 1)
+            pairs.append((i * my + j, partner[0] * my + partner[1]))
+    x_odd = lax.ppermute(edges[1], ("gx", "gy"), pairs)
+    y_odd = lax.ppermute(edges[3], "gy", [(i, (i - 1 ^ 1) + 1) if 0 < i < my - 1 else (i, my - 1 - i) for i in range(my)])
     x_even = lax.ppermute(edges[0], "gx", [(i, i ^ 1) for i in range(mx)])
     y_even = lax.ppermute(edges[2], "gy", [(i, i ^ 1) for i in range(my)])
-    odd = lambda n: [(i, i + 1) for i in range(1, n - 1, 2)] + [(i + 1, i) for i in range(1, n - 1, 2)]
-    x_odd = lax.ppermute(edges[1], "gx", odd(mx))
-    y_odd = lax.ppermute(edges[3], "gy", odd(my))
 
     along_x, along_y = (2, nx, ny, nz), (2, ny, nx, nz)
     ivx, rx, cx, wx, ivy, ry, cy, wy = call(
@@ -370,6 +384,8 @@
         functools.partial(finish_kernel, len(saved)),
         (mine, theirs, *saved, local_y, cy, wy),
         [(fields, nx, ny, nz)],
+        scratch=[pltpu.VMEM((fields, nx, ny, nz), F32), pltpu.SemaphoreType.DMA((fields,))],
+        out_specs=[HBM],
     )
     return out
 

time: 45.4 us -> 41.3 us (0.910)
  starting transfers between devices: 17.6 us -> 12.1 us
  waiting for transfers between devices: 19.2 us -> 20.9 us
    ppermute x5, starting transfers between devices: 13.2 us -> 7.41 us  [reduce_line(): theirs = lax.ppermute(message, axis, [(i, i ^ bit) for i in range(count)])]
    ppermute x2, waiting for transfers between devices: 0.01 us -> 1.75 us  [the longest x1 1.75 us: per_device(): lax.ppermute(edges[3], 'gy', [(i, (i - 1 ^ 1) + 1) if 0 < i < my - 1 else...]
where the time goes in v2:
time: 41.3 us; the launch traced here: 41.1 us
  waiting for transfers between devices  20.9 us (51%)
  starting transfers between devices  12.1 us (29%)
  Pallas kernels  5.89 us (14%)
  local copies, waits for them, and re-layouts  2.18 us (5%)
    ppermute x5, waiting for transfers between devices, reduce_line(): theirs = lax.ppermute(message, axis, [(i, i ^ bit) for i in range(count)])  19.1 us
    ppermute x5, starting transfers between devices, reduce_line(): theirs = lax.ppermute(message, axis, [(i, i ^ bit) for i in range(count)])  7.41 us
    pallas_call x10, Pallas kernels, call(): pl.pallas_call(kernel, out_shape=[jax.ShapeDtypeStruct(shape, F32) for sh...  5.89 us
    ppermute x1, starting transfers between devices, per_device(): x_even = lax.ppermute(edges[0], 'gx', [(i, i ^ 1) for i in range(mx)])  3 us
    unnamed x8, local copies, waits for them, and re-layouts  2.18 us
    ppermute x1, waiting for transfers between devices, per_device(): lax.ppermute(edges[3], 'gy', [(i, (i - 1 ^ 1) + 1) if 0 < i < my - 1 else...  1.75 us
    ppermute x1, starting transfers between devices, per_device(): lax.ppermute(edges[3], 'gy', [(i, (i - 1 ^ 1) + 1) if 0 < i < my - 1 else...  1.13 us
  transfers between devices with their start and end apart: 9, of which 6 were waited for; matrix products, arithmetic and copies ran while one was open for 0% of the time, Pallas kernels for 6%

profile of v2, /device:TPU:0, one launch (start us, length us, event | category | flops | bytes accessed | tf_op | source)
XLA Modules:
  0.0 41.1 jit_solution(9351848616276459318)
XLA Ops:
  0.0 1.2 %copy-done = f32[4,16,32,128]{3,2,1,0:T(8,128)S(1)} copy-done((f32[4,16,32,128]{3,2,1,0:T(8,128)S(1)}, f32[4,16,32,128]{3,2,1,0:T(8,128)}, u32[]{:S(2)}) %copy-start) | copy-done | bytes 1048600
  1.2 0.9 %copy-done.2 = f32[16,32,128]{2,1,0:T(8,128)S(1)} copy-done((f32[16,32,128]{2,1,0:T(8,128)S(1)}, f32[16,32,128]{2,1,0:T(8,128)}, u32[]{:S(2)}) %copy-start.2) | copy-done | bytes 262168
  2.2 0.3 shard_map.28
  2.4 3.0 %collective-permute-start = (f32[5,32,128]{2,1,0:T(8,128)S(1)}, f32[5,32,128]{2,1,0:T(8,128)S(1)}, u32[]{:S(2)}, u32[]{:S(2)}) collective-permute-start(f32[5,32,128]{2,1,0:T(8,128)S(1)} %get-tuple-element.30), channel_id=1, source_target_pairs={{0,4},{4,0},{8,12},{12,8},{16,20},{20,16},{24,28},{28,24},{1,5},{5... | collective-permute-start | bytes 245768 | tf_op jit(solution)/shard_map/ppermute | solution.py:355
  5.4 0.5 %collective-permute-start.2 = (f32[5,16,128]{2,1,0:T(8,128)S(1)}, f32[5,16,128]{2,1,0:T(8,128)S(1)}, u32[]{:S(2)}, u32[]{:S(2)}) collective-permute-start(f32[5,16,128]{2,1,0:T(8,128)S(1)} %get-tuple-element.32), channel_id=1, source_target_pairs={{0,1},{1,0},{2,3},{3,2},{4,5},{5,4},{6,7},{7,6},{8,9},{9,8},{10,11... | collective-permute-start | bytes 122888 | tf_op jit(solution)/shard_map/ppermute | solution.py:356
  6.0 1.1 %collective-permute-start.3 = (f32[5,16,128]{2,1,0:T(8,128)S(1)}, f32[5,16,128]{2,1,0:T(8,128)S(1)}, u32[]{:S(2)}, u32[]{:S(2)}) collective-permute-start(f32[5,16,128]{2,1,0:T(8,128)S(1)} %get-tuple-element.33), channel_id=1, source_target_pairs={{0,3},{1,2},{2,1},{3,0},{4,7},{5,6},{6,5},{7,4},{8,11},{9,10},{10,... | collective-permute-start | bytes 122888 | tf_op jit(solution)/shard_map/ppermute | solution.py:354
  7.1 0.8 %shard_map.29 = (f32[2,16,32,128]{3,2,1,0:T(8,128)S(1)}, f32[2,16,32,128]{3,2,1,0:T(8,128)S(1)}, f32[2,16,32,128]{3,2,1,0:T(8,128)S(1)}, f32[2,16,32,128]{3,2,1,...) custom-call(f32[16,32,128]{2,1,0:T(8,128)S(1)} %copy-done.3), custom_call_target="tpu_custom_call" | custom-call | flops 8000000 | bytes 8000000 | tf_op jit(solution)/shard_map/pallas_call | solution.py:21
  7.9 1.7 %collective-permute-done.3.y_odd.refs_6_ = f32[5,16,128]{2,1,0:T(8,128)S(1)} collective-permute-done((f32[5,16,128]{2,1,0:T(8,128)S(1)}, f32[5,16,128]{2,1,0:T(8,128)S(1)}, u32[]{:S(2)}, u32[]{:S(2)}) %collective-permute-start.3) | collective-permute-done | bytes 40992 | tf_op jit(solution)/shard_map/ppermute | solution.py:354
  9.6 0.9 %shard_map.30 = (f32[4,16,32,128]{3,2,1,0:T(8,128)S(1)}, f32[14,32,128]{2,1,0:T(8,128)S(1)}) custom-call(f32[4,16,32,128]{3,2,1,0:T(8,128)S(1)} %copy-done.1, f32[16,32,128]{2,1,0:T(8,128)S(1)} %copy-done.3, f32[5,32,128]{2,1,0:T(8,128)S(1)} %collective-permute-done.x_even, f32[5,32,128]{2,1,0:T(8,128)S(1)} %collective-permute-done.1.x_odd, ...), custom_call_target="tpu_custom_call" | custom-call | flops 1000000 | bytes 1000000 | tf_op jit(solution)/shard_map/pallas_call | solution.py:21
  10.6 2.3 %collective-permute-start.4 = (f32[14,32,128]{2,1,0:T(8,128)S(1)}, f32[14,32,128]{2,1,0:T(8,128)S(1)}, u32[]{:S(2)}, u32[]{:S(2)}) collective-permute-start(f32[14,32,128]{2,1,0:T(8,128)S(1)} %get-tuple-element.36.mine), channel_id=1, source_target_pairs={{0,4},{4,0},{8,12},{12,8},{16,20},{20,16},{24,28},{28,24},{1,5},{5... | collective-permute-start | bytes 688136 | tf_op jit(solution)/shard_map/ppermute | solution.py:324
  12.9 6.3 %collective-permute-done.4.theirs = f32[14,32,128]{2,1,0:T(8,128)S(1)} collective-permute-done((f32[14,32,128]{2,1,0:T(8,128)S(1)}, f32[14,32,128]{2,1,0:T(8,128)S(1)}, u32[]{:S(2)}, u32[]{:S(2)}) %collective-permute-start.4) | collective-permute-done | bytes 229408 | tf_op jit(solution)/shard_map/ppermute | solution.py:324
  19.2 0.1 shard_map.31
  19.3 1.6 %collective-permute-start.5 = (f32[14,32,128]{2,1,0:T(8,128)S(1)}, f32[14,32,128]{2,1,0:T(8,128)S(1)}, u32[]{:S(2)}, u32[]{:S(2)}) collective-permute-start(f32[14,32,128]{2,1,0:T(8,128)S(1)} %get-tuple-element.37.mine), channel_id=1, source_target_pairs={{0,8},{4,12},{8,0},{12,4},{16,24},{20,28},{24,16},{28,20},{1,9},{5... | collective-permute-start | bytes 688136 | tf_op jit(solution)/shard_map/ppermute | solution.py:324
  20.9 5.9 %collective-permute-done.5.theirs = f32[14,32,128]{2,1,0:T(8,128)S(1)} collective-permute-done((f32[14,32,128]{2,1,0:T(8,128)S(1)}, f32[14,32,128]{2,1,0:T(8,128)S(1)}, u32[]{:S(2)}, u32[]{:S(2)}) %collective-permute-start.5) | collective-permute-done | bytes 229408 | tf_op jit(solution)/shard_map/ppermute | solution.py:324
  26.8 1.8 %collective-permute-start.6 = (f32[6,32,128]{2,1,0:T(8,128)S(1)}, f32[6,32,128]{2,1,0:T(8,128)S(1)}, u32[]{:S(2)}, u32[]{:S(2)}) collective-permute-start(f32[6,32,128]{2,1,0:T(8,128)S(1)} %get-tuple-element.38.refs_0_), channel_id=1, source_target_pairs={{0,16},{4,20},{8,24},{12,28},{16,0},{20,4},{24,8},{28,12},{1,17},{... | collective-permute-start | bytes 294920 | tf_op jit(solution)/shard_map/ppermute | solution.py:333
  28.6 1.4 %shard_map.33 = (f32[4,32,16,128]{3,2,1,0:T(8,128)S(1)}, f32[2,32,16,128]{3,2,1,0:T(8,128)S(1)}, f32[2,32,16,128]{3,2,1,0:T(8,128)S(1)}) custom-call(f32[4,16,32,128]{3,2,1,0:T(8,128)S(1)} %get-tuple-element.41.source, f32[2,16,32,128]{3,2,1,0:T(8,128)S(1)} %get-tuple-element.42.ivx, f32[2,16,32,128]{3,2,1,0:T(8,128)S(1)} %get-tuple-element.43.rx, ...), custom_call_target="tpu_custom_call" | custom-call | flops 8000000 | bytes 8000000 | tf_op jit(solution)/shard_map/pallas_call | solution.py:21
  30.1 3.4 %collective-permute-done.6.refs_1_ = f32[6,32,128]{2,1,0:T(8,128)S(1)} collective-permute-done((f32[6,32,128]{2,1,0:T(8,128)S(1)}, f32[6,32,128]{2,1,0:T(8,128)S(1)}, u32[]{:S(2)}, u32[]{:S(2)}) %collective-permute-start.6) | collective-permute-done | bytes 98336 | tf_op jit(solution)/shard_map/ppermute | solution.py:333
  33.5 0.3 shard_map.34
  33.8 0.1 collective-permute-start.7
  33.9 1.3 %collective-permute-done.7.theirs = f32[14,16,128]{2,1,0:T(8,128)S(1)} collective-permute-done((f32[14,16,128]{2,1,0:T(8,128)S(1)}, f32[14,16,128]{2,1,0:T(8,128)S(1)}, u32[]{:S(2)}, u32[]{:S(2)}) %collective-permute-start.7) | collective-permute-done | bytes 114720 | tf_op jit(solution)/shard_map/ppermute | solution.py:324
  35.2 1.6 %collective-permute-start.8 = (f32[6,16,128]{2,1,0:T(8,128)S(1)}, f32[6,16,128]{2,1,0:T(8,128)S(1)}, u32[]{:S(2)}, u32[]{:S(2)}) collective-permute-start(f32[6,16,128]{2,1,0:T(8,128)S(1)} %get-tuple-element.50.refs_0_), channel_id=1, source_target_pairs={{0,2},{1,3},{2,0},{3,1},{4,6},{5,7},{6,4},{7,5},{8,10},{9,11},{10,... | collective-permute-start | bytes 147464 | tf_op jit(solution)/shard_map/ppermute | solution.py:333
  36.8 0.3 shard_map.36.refs_3_
  37.1 2.3 %collective-permute-done.8.refs_1_ = f32[6,16,128]{2,1,0:T(8,128)S(1)} collective-permute-done((f32[6,16,128]{2,1,0:T(8,128)S(1)}, f32[6,16,128]{2,1,0:T(8,128)S(1)}, u32[]{:S(2)}, u32[]{:S(2)}) %collective-permute-start.8) | collective-permute-done | bytes 49184 | tf_op jit(solution)/shard_map/ppermute | solution.py:333
  39.4 1.7 %shard_map.37 = f32[4,16,32,128]{3,2,1,0:T(8,128)} custom-call(f32[6,16,128]{2,1,0:T(8,128)S(1)} %get-tuple-element.50.refs_0_, f32[6,16,128]{2,1,0:T(8,128)S(1)} %collective-permute-done.8.refs_1_, f32[8,16,128]{2,1,0:T(8,128)S(1)} %get-tuple-element.51.refs_2_, f32[4,32,16,128]{3,2,1,0:T(8,128)S(1)} %shard_map.36.refs_3_, ...), custom_call_target="tpu_custom_call" | custom-call | flops 1000000 | bytes 1000000 | tf_op jit(solution)/shard_map/pallas_call | solution.py:21
  (12 shorter events, 0.1 us)
Async XLA Ops:
  0.0 1.2 %copy-start = (f32[4,16,32,128]{3,2,1,0:T(8,128)S(1)}, f32[4,16,32,128]{3,2,1,0:T(8,128)}, u32[]{:S(2)}) copy-start(f32[4,16,32,128]{3,2,1,0:T(8,128)} %flow.3) | copy-start | bytes 3145732
  1.2 0.9 %copy-start.2 = (f32[16,32,128]{2,1,0:T(8,128)S(1)}, f32[16,32,128]{2,1,0:T(8,128)}, u32[]{:S(2)}) copy-start(f32[16,32,128]{2,1,0:T(8,128)} %refs_4_.1) | copy-start | bytes 786436
  2.2 4.9 %copy-start.3 = (f32[16,32,128]{2,1,0:T(8,128)S(1)}, f32[16,32,128]{2,1,0:T(8,128)}, u32[]{:S(2)}) copy-start(f32[16,32,128]{2,1,0:T(8,128)} %refs_4_.1) | copy-start | bytes 786436
  2.2 7.5 %copy-start.1 = (f32[4,16,32,128]{3,2,1,0:T(8,128)S(1)}, f32[4,16,32,128]{3,2,1,0:T(8,128)}, u32[]{:S(2)}) copy-start(f32[4,16,32,128]{3,2,1,0:T(8,128)} %flow.3) | copy-start | bytes 3145732
  2.4 7.2 %collective-permute-start = (f32[5,32,128]{2,1,0:T(8,128)S(1)}, f32[5,32,128]{2,1,0:T(8,128)S(1)}, u32[]{:S(2)}, u32[]{:S(2)}) collective-permute-start(f32[5,32,128]{2,1,0:T(8,128)S(1)} %get-tuple-element.30), channel_id=1, source_target_pairs={{0,4},{4,0},{8,12},{12,8},{16,20},{20,16},{24,28},{28,24},{1,5},{5... | collective-permute-start | bytes 245768 | tf_op jit(solution)/shard_map/ppermute | solution.py:355
  5.4 4.2 %collective-permute-start.1 = (f32[5,32,128]{2,1,0:T(8,128)S(1)}, f32[5,32,128]{2,1,0:T(8,128)S(1)}, u32[]{:S(2)}, u32[]{:S(2)}) collective-permute-start(f32[5,32,128]{2,1,0:T(8,128)S(1)} %get-tuple-element.31), channel_id=1, source_target_pairs={{0,1},{1,0},{2,3},{3,2},{4,8},{5,9},{6,10},{7,11},{8,4},{9,5},{10,... | collective-permute-start | bytes 245768 | tf_op jit(solution)/shard_map/ppermute | solution.py:353
  5.4 2.4 %collective-permute-start.2 = (f32[5,16,128]{2,1,0:T(8,128)S(1)}, f32[5,16,128]{2,1,0:T(8,128)S(1)}, u32[]{:S(2)}, u32[]{:S(2)}) collective-permute-start(f32[5,16,128]{2,1,0:T(8,128)S(1)} %get-tuple-element.32), channel_id=1, source_target_pairs={{0,1},{1,0},{2,3},{3,2},{4,5},{5,4},{6,7},{7,6},{8,9},{9,8},{10,11... | collective-permute-start | bytes 122888 | tf_op jit(solution)/shard_map/ppermute | solution.py:356
  6.0 3.7 %collective-permute-start.3 = (f32[5,16,128]{2,1,0:T(8,128)S(1)}, f32[5,16,128]{2,1,0:T(8,128)S(1)}, u32[]{:S(2)}, u32[]{:S(2)}) collective-permute-start(f32[5,16,128]{2,1,0:T(8,128)S(1)} %get-tuple-element.33), channel_id=1, source_target_pairs={{0,3},{1,2},{2,1},{3,0},{4,7},{5,6},{6,5},{7,4},{8,11},{9,10},{10,... | collective-permute-start | bytes 122888 | tf_op jit(solution)/shard_map/ppermute | solution.py:354
  10.6 8.6 %collective-permute-start.4 = (f32[14,32,128]{2,1,0:T(8,128)S(1)}, f32[14,32,128]{2,1,0:T(8,128)S(1)}, u32[]{:S(2)}, u32[]{:S(2)}) collective-permute-start(f32[14,32,128]{2,1,0:T(8,128)S(1)} %get-tuple-element.36.mine), channel_id=1, source_target_pairs={{0,4},{4,0},{8,12},{12,8},{16,20},{20,16},{24,28},{28,24},{1,5},{5... | collective-permute-start | bytes 688136 | tf_op jit(solution)/shard_map/ppermute | solution.py:324
  19.3 7.5 %collective-permute-start.5 = (f32[14,32,128]{2,1,0:T(8,128)S(1)}, f32[14,32,128]{2,1,0:T(8,128)S(1)}, u32[]{:S(2)}, u32[]{:S(2)}) collective-permute-start(f32[14,32,128]{2,1,0:T(8,128)S(1)} %get-tuple-element.37.mine), channel_id=1, source_target_pairs={{0,8},{4,12},{8,0},{12,4},{16,24},{20,28},{24,16},{28,20},{1,9},{5... | collective-permute-start | bytes 688136 | tf_op jit(solution)/shard_map/ppermute | solution.py:324
  26.8 6.6 %collective-permute-start.6 = (f32[6,32,128]{2,1,0:T(8,128)S(1)}, f32[6,32,128]{2,1,0:T(8,128)S(1)}, u32[]{:S(2)}, u32[]{:S(2)}) collective-permute-start(f32[6,32,128]{2,1,0:T(8,128)S(1)} %get-tuple-element.38.refs_0_), channel_id=1, source_target_pairs={{0,16},{4,20},{8,24},{12,28},{16,0},{20,4},{24,8},{28,12},{1,17},{... | collective-permute-start | bytes 294920 | tf_op jit(solution)/shard_map/ppermute | solution.py:333
  33.8 1.4 %collective-permute-start.7 = (f32[14,16,128]{2,1,0:T(8,128)S(1)}, f32[14,16,128]{2,1,0:T(8,128)S(1)}, u32[]{:S(2)}, u32[]{:S(2)}) collective-permute-start(f32[14,16,128]{2,1,0:T(8,128)S(1)} %get-tuple-element.49.mine), channel_id=1, source_target_pairs={{0,1},{1,0},{2,3},{3,2},{4,5},{5,4},{6,7},{7,6},{8,9},{9,8},{10,11... | collective-permute-start | bytes 344072 | tf_op jit(solution)/shard_map/ppermute | solution.py:324
  35.2 4.2 %collective-permute-start.8 = (f32[6,16,128]{2,1,0:T(8,128)S(1)}, f32[6,16,128]{2,1,0:T(8,128)S(1)}, u32[]{:S(2)}, u32[]{:S(2)}) collective-permute-start(f32[6,16,128]{2,1,0:T(8,128)S(1)} %get-tuple-element.50.refs_0_), channel_id=1, source_target_pairs={{0,2},{1,3},{2,0},{3,1},{4,6},{5,7},{6,4},{7,5},{8,10},{9,11},{10,... | collective-permute-start | bytes 147464 | tf_op jit(solution)/shard_map/ppermute | solution.py:333

commit v3 on v2

v3 whole, which is shorter than its diff:
```python
import functools

import jax
import jax.numpy as jnp
from jax import lax
from jax.experimental import pallas as pl
from jax.experimental.pallas import tpu as pltpu
from jax.sharding import PartitionSpec as P

ADVECT = 0.2
BUOYANT = 0.5
CONDUCT = 0.6
GROUPS = (0, 0, 0, 1)
SCALES = (1.0, CONDUCT)
VMEM = pl.BlockSpec(memory_space=pltpu.VMEM)
HBM = pl.BlockSpec(memory_space=pltpu.HBM)
F32 = jnp.float32


def call(kernel, ins, outs, scratch=(), in_specs=None, out_specs=None, cost=1000, vmem=40):
    return pl.pallas_call(
        kernel,
        out_shape=[jax.ShapeDtypeStruct(shape, F32) for shape in outs],
        in_specs=in_specs or [VMEM] * len(ins),
        out_specs=out_specs or [VMEM] * len(outs),
        scratch_shapes=list(scratch),
        compiler_params=pltpu.CompilerParams(vmem_limit_bytes=vmem * 1024 * 1024),
        cost_estimate=pl.CostEstimate(flops=cost, bytes_accessed=cost, transcendentals=0),
    )(*ins)


def pick(flag, a, b):
    return jnp.where(flag, a, b)


def factor_line(load, count, first, last, inv, ratio, left, right):
    for group, scale in enumerate(SCALES):
        here = load(0)
        excess = 1.0 + pick(first, scale * here, 0.0)
        column = None
        columns = []
        for i in range(count):
            if i < count - 1:
                beyond = load(i + 1)
                face = (0.5 * scale) * (here + beyond)
                inverse = 1.0 / (excess + face)
                portion = face * inverse
                ratio[group, i] = portion
                inv[group, i] = inverse
                columns.append(column)
                column = portion if column is None else column * portion
                excess = 1.0 + portion * excess
                here = beyond
            else:
                excess = excess + pick(last, scale * here, 0.0)
                inverse = 1.0 / excess
                inv[group, i] = inverse
                ratio[group, i] = inverse
                columns.append(column)
        response = inverse
        onward = column * inverse
        right[group, count - 1] = response
        left[group, count - 1] = onward
        for i in range(count - 2, -1, -1):
            portion = ratio[group, i]
            response = portion * response
            start = inv[group, i] if i == 0 else columns[i] * inv[group, i]
            onward = start + portion * onward
            right[group, i] = response
            left[group, i] = onward


def coef_rows(left, right, out, count):
    for group in range(2):
        out[group] = left[group, 0]
        out[2 + group] = left[group, count - 1]
        out[4 + group] = right[group, count - 1]


def first_kernel(flow, visc, x_odd, y_even, y_odd, ivx, rx, cx, wx, coef_x, cells, sems):
    nx, ny = flow.shape[1], flow.shape[2]
    ix, iy = lax.axis_index("gx"), lax.axis_index("gy")
    x_par, y_par = lax.rem(ix, 2), lax.rem(iy, 2)
    copies = (
        (visc, cells),
        (flow.at[:, x_par * (nx - 1)], x_odd),
        (flow.at[:, :, (1 - y_par) * (ny - 1)], y_even),
        (flow.at[:, :, y_par * (ny - 1)], y_odd),
    )
    started = [pltpu.make_async_copy(a, b, sems.at[i]) for i, (a, b) in enumerate(copies)]
    for copy in started:
        copy.start()
    started[0].wait()
    factor_line(lambda i: cells[i], nx, ix == 0, ix == lax.axis_size("gx") - 1, ivx, rx, cx, wx)
    coef_rows(cx, wx, coef_x, nx)
    coef_x[6] = cells[0]
    coef_x[7] = cells[nx - 1]
    for copy in started[1:]:
        copy.wait()


def factor_y_kernel(visc, ivy, ry, cy, wy, coef_y):
    nx, ny, nz = visc.shape
    iy = lax.axis_index("gy")
    rows = visc.reshape(nx * ny, nz)

    def row_y(j):
        return rows[pl.ds(j, nx, stride=ny), :]

    factor_line(row_y, ny, iy == 0, iy == lax.axis_size("gy") - 1, ivy, ry, cy, wy)
    coef_rows(cy, wy, coef_y, ny)
    coef_y[6] = row_y(0)
    coef_y[7] = row_y(ny - 1)


def source_kernel(flow, x_odd, y_even, y_odd, cx, wx, after, source, message):
    _, nx, ny, nz = flow.shape
    ix, iy = lax.axis_index("gx"), lax.axis_index("gy")
    x_par, y_par = lax.rem(ix, 2) == 0, lax.rem(iy, 2) == 0
    no_low = (ix == 0) | (lax.rem(ix, 2) == 1)
    no_high = (ix == lax.axis_size("gx") - 1) | x_par
    y_first, y_last = iy == 0, iy == lax.axis_size("gy") - 1
    row = lax.broadcasted_iota(jnp.int32, (ny, nz), 0)
    left = [None] * 4
    right = [None] * 4
    for i in range(nx):
        velocity = [ADVECT * 0.5 * flow[c, i] for c in range(3)]
        for c in range(4):
            f = flow[c, i]
            down = pick(no_low, 0.0, x_odd[c]) if i == 0 else flow[c, i - 1]
            up = pick(no_high, 0.0, x_odd[c]) if i == nx - 1 else flow[c, i + 1]
            y_low = pick(y_par, y_odd[c, pl.ds(i, 1)], y_even[c, pl.ds(i, 1)])
            y_high = pick(y_par, y_even[c, pl.ds(i, 1)], y_odd[c, pl.ds(i, 1)])
            y_low = pick(y_first, 0.0, y_low)
            y_high = pick(y_last, 0.0, y_high)
            below = pick(row == 0, y_low, pltpu.roll(f, 1, 0))
            above = pick(row == ny - 1, y_high, pltpu.roll(f, ny - 1, 0))
            z_low = pltpu.roll(f, 1, 1)
            z_high = pltpu.roll(f, nz - 1, 1)
            s = f - (
                velocity[0] * (up - down)
                + velocity[1] * (above - below)
                + velocity[2] * (z_high - z_low)
            )
            if c == 2:
                s = s + BUOYANT * flow[3, i]
            source[c, i] = s
            group = GROUPS[c]
            a, b = cx[group, i] * s, wx[group, i] * s
            left[c] = a if i == 0 else left[c] + a
            right[c] = b if i == 0 else right[c] + b
    for c in range(4):
        message[c] = left[c]
        message[4 + c] = right[c]
        message[8 + c] = pick(x_par, flow[c, nx - 1], flow[c, 0])


def coef_part(axis, bit, last, mine, theirs, at, union, union_at, weights):
    is_left = (lax.axis_index(axis) & bit) == 0
    next_left = (lax.axis_index(axis) & (2 * bit)) == 0

    def a(k):
        return pick(is_left, mine[at + k], theirs[at + k])

    def b(k):
        return pick(is_left, theirs[at + k], mine[at + k])

    face = 0.5 * (a(7) + b(6))
    for group, scale in enumerate(SCALES):
        a_lr, b_lr = a(2 + group), b(2 + group)
        m = 1.0 / (1.0 / (scale * face) + a(4 + group) + b(group))
        pa, pb = m * a_lr, m * b_lr
        weights[group] = m
        weights[2 + group] = pa
        weights[4 + group] = pb
        out_ll = a(group) - a_lr * pa
        out_rr = b(4 + group) - b_lr * pb
        if last:
            union[union_at + group] = pick(next_left, out_rr, out_ll)
        else:
            union[union_at + group] = out_ll
            union[union_at + 2 + group] = a_lr * pb
            union[union_at + 4 + group] = out_rr
    if last:
        union[union_at + 2] = pick(next_left, b(7), a(6))
    else:
        union[union_at + 6] = a(6)
        union[union_at + 7] = b(7)


def row_part(axis, bit, last, mine, theirs, weights, union, saved, edged=None):
    is_left = (lax.axis_index(axis) & bit) == 0
    next_left = (lax.axis_index(axis) & (2 * bit)) == 0

    def sides(x, y):
        return pick(is_left, x, y), pick(is_left, y, x)

    for c in range(4):
        group = GROUPS[c]
        a_l, b_l = sides(mine[c], theirs[c])
        a_r, b_r = sides(mine[4 + c], theirs[4 + c])
        if edged is not None:
            coef_mine, coef_theirs, missing = edged
            here = (ADVECT * 0.5) * mine[8] * theirs[8 + c]
            there = (ADVECT * 0.5) * theirs[8] * mine[8 + c]
            missing[c] = here
            a_gap, b_gap = sides(here, there)
            ll = pick(is_left, coef_theirs[group], coef_mine[group])
            rr = pick(is_left, coef_mine[4 + group], coef_theirs[4 + group])
            a_lr, b_lr = sides(coef_mine[2 + group], coef_theirs[2 + group])
            a_l = a_l - a_lr * a_gap
            a_r = a_r - rr * a_gap
            b_l = b_l + ll * b_gap
            b_r = b_r + b_lr * b_gap
        d = b_l - a_r
        saved[c] = weights[group] * d
        out_l = a_l + weights[2 + group] * d
        out_r = b_r - weights[4 + group] * d
        if last:
            union[c] = pick(next_left, out_r, out_l)
        else:
            union[c] = out_l
            union[4 + c] = out_r


def coef_kernel(axis, bit, last, mine, theirs, after, union, weights):
    coef_part(axis, bit, last, mine, theirs, 0, union, 0, weights)


def x_merge_kernel(axis, bit, last, edged, mine, theirs, weights, coef_mine, coef_theirs, near, union, saved, missing):
    row_part(
        axis, bit, last, mine, theirs, weights, union, saved,
        (coef_mine, coef_theirs, missing) if edged else None,
    )
    if last:
        union[pl.ds(4, 3)] = near[...]


def y_merge_kernel(axis, bit, last, mine, theirs, union, saved, weights):
    coef_part(axis, bit, last, mine, theirs, 8, union, 4 if last else 8, weights)
    row_part(axis, bit, last, mine, theirs, weights, union, saved)


def fluxes(axis, mine, theirs, saved, missing=None):
    index = lax.axis_index(axis)
    bit = lax.axis_size(axis) // 2
    is_left = (index & bit) == 0
    result = []
    face = 0.5 * (mine[6] + theirs[6])
    weight = [
        1.0 / (1.0 / (scale * face) + mine[4 + group] + theirs[4 + group])
        for group, scale in enumerate(SCALES)
    ]
    for c in range(4):
        group = GROUPS[c]
        d = theirs[c] - mine[c]
        flux = weight[group] * pick(is_left, d, -d)
        zero = jnp.zeros_like(flux)
        low = pick(is_left, zero, flux)
        high = pick(is_left, flux, zero)
        this = bit
        for part, weights in saved[::-1]:
            this = this // 2
            flux = part[c] + weights[4 + group] * high + weights[2 + group] * low
            if this == 1 and missing is not None:
                flux = flux - missing[c]
            side = (index & this) == 0
            low, high = pick(side, low, flux), pick(side, flux, high)
        result.append((low, high))
    return result


def local_kernel(source, ivx, rx, cx, wx, local_t, cx_t, wx_t, scratch):
    _, nx, ny, nz = source.shape
    for c in range(4):
        group = GROUPS[c]
        running = source[c, 0]
        forward = [running]
        for i in range(1, nx):
            running = source[c, i] + rx[group, i - 1] * running
            forward.append(running)
        value = running * ivx[group, nx - 1]
        scratch[c, pl.ds((nx - 1) * ny, ny)] = value
        for i in range(nx - 2, -1, -1):
            value = forward[i] * ivx[group, i] + rx[group, i] * value
            scratch[c, pl.ds(i * ny, ny)] = value
        for j in range(ny):
            local_t[c, j] = scratch[c, pl.ds(j, nx, stride=ny), :]
    for group in range(2):
        c_rows = cx.at[group].reshape(nx * ny, nz)
        w_rows = wx.at[group].reshape(nx * ny, nz)
        for j in range(ny):
            cx_t[group, j] = c_rows[pl.ds(j, nx, stride=ny), :]
            wx_t[group, j] = w_rows[pl.ds(j, nx, stride=ny), :]


def y_start_kernel(stages, *refs):
    mine, theirs, missing = refs[:3]
    parts = refs[3 : 3 + 2 * stages]
    local_t, cx_t, wx_t, cy, wy, coef_y, solved, message, flux_low, flux_high = refs[3 + 2 * stages :]
    _, ny, nx, nz = local_t.shape
    saved = list(zip(parts[::2], parts[1::2]))
    for c, (low, high) in enumerate(fluxes("gx", mine, theirs, saved, missing)):
        flux_low[c] = low
        flux_high[c] = high
    for c in range(4):
        group = GROUPS[c]
        left = right = None
        for j in range(ny):
            low = flux_low[c, pl.ds(j, 1)]
            high = flux_high[c, pl.ds(j, 1)]
            value = local_t[c, j] + (wx_t[group, j] * high - cx_t[group, j] * low)
            solved[c, j] = value
            a, b = cy[group, j] * value, wy[group, j] * value
            left = a if j == 0 else left + a
            right = b if j == 0 else right + b
        message[c] = left
        message[4 + c] = right
    message[pl.ds(8, 8)] = coef_y[...]


def y_local_kernel(solved, ivy, ry, local):
    _, ny, nx, nz = solved.shape
    for c in range(4):
        group = GROUPS[c]
        running = solved[c, 0]
        forward = [running]
        for j in range(1, ny):
            running = solved[c, j] + ry[group, j - 1] * running
            forward.append(running)
        value = running * ivy[group, ny - 1]
        local[c, ny - 1] = value
        for j in range(ny - 2, -1, -1):
            value = forward[j] * ivy[group, j] + ry[group, j] * value
            local[c, j] = value


def finish_kernel(stages, *refs):
    mine, theirs = refs[:2]
    parts = refs[2 : 2 + 2 * stages]
    local, cy, wy, out, buffer, sems = refs[2 + 2 * stages :]
    saved = list(zip(parts[::2], parts[1::2]))
    _, ny, nx, nz = local.shape
    ends = fluxes("gy", mine, theirs, saved)
    copies = []
    for c in range(4):
        group = GROUPS[c]
        low, high = ends[c]
        rows = buffer.at[c].reshape(nx * ny, nz)
        for j in range(ny):
            value = local[c, j] + (wy[group, j] * high - cy[group, j] * low)
            rows[pl.ds(j, nx, stride=ny), :] = value
        copies.append(pltpu.make_async_copy(buffer.at[c], out.at[c], sems.at[c]))
        copies[-1].start()
    for copy in copies:
        copy.wait()


def swap(array, axis, bit):
    return lax.ppermute(array, axis, [(i, i ^ bit) for i in range(lax.axis_size(axis))])


def after_all(spec_count):
    return [VMEM] * spec_count + [pl.BlockSpec(memory_space=pl.ANY)]


def per_device(flow, visc):
    fields, nx, ny, nz = flow.shape
    mx, my = lax.axis_size("gx"), lax.axis_size("gy")
    along_x, along_y = (2, nx, ny, nz), (2, ny, nx, nz)
    x_edge, y_edge_even, y_edge_odd, ivx, rx, cx, wx, coef_x = call(
        first_kernel,
        tuple(pltpu.with_memory_space_constraint(array, pltpu.HBM) for array in (flow, visc)),
        [(fields, ny, nz), (fields, nx, nz), (fields, nx, nz)] + [along_x] * 4 + [(8, ny, nz)],
        scratch=[pltpu.VMEM((nx, ny, nz), F32), pltpu.SemaphoreType.DMA((4,))],
        in_specs=[HBM, HBM],
    )
    pairs = []
    for i in range(mx):
        for j in range(my):
            inner = 0 < i < mx - 1
            partner = ((i - 1 ^ 1) + 1, j) if inner else (i, j ^ 1)
            pairs.append((i * my + j, partner[0] * my + partner[1]))
    x_odd = lax.ppermute(x_edge, ("gx", "gy"), pairs)
    y_odd = lax.ppermute(
        y_edge_odd, "gy", [(i, (i - 1 ^ 1) + 1) if 0 < i < my - 1 else (i, my - 1 - i) for i in range(my)]
    )
    y_even = swap(y_edge_even, "gy", 1)

    ivy, ry, cy, wy, coef_y = call(factor_y_kernel, (visc,), [along_y] * 4 + [(8, nx, nz)])
    coef_x_theirs = swap(coef_x, "gx", 1)
    source, message = call(
        source_kernel,
        (flow, x_odd, y_even, y_odd, cx, wx, coef_x_theirs),
        in_specs=after_all(6),
        outs=[(fields, nx, ny, nz), (12, ny, nz)],
    )
    local_t, cx_t, wx_t = call(
        local_kernel,
        (source, ivx, rx, cx, wx),
        [(fields, ny, nx, nz), along_y, along_y],
        scratch=[pltpu.VMEM((fields, nx * ny, nz), F32)],
        cost=1000,
    )

    saved = []
    coefs, coefs_theirs, rows = coef_x, coef_x_theirs, message
    shape = (ny, nz)
    bit = 1
    while 2 * bit < mx:
        last = 4 * bit == mx
        rows_theirs = swap(rows, "gx", bit)
        merged, weights = call(
            functools.partial(coef_kernel, "gx", bit, last),
            (coefs, coefs_theirs, rows),
            [(3 if last else 8,) + shape, (6,) + shape],
            in_specs=after_all(2),
        )
        merged_theirs = merged if last else swap(merged, "gx", 2 * bit)
        rows, part, gap = call(
            functools.partial(x_merge_kernel, "gx", bit, last, bit == 1),
            (rows, rows_theirs, weights, coefs, coefs_theirs, merged),
            [(7 if last else 8,) + shape, (4,) + shape, (4,) + shape],
        )
        if bit == 1:
            missing = gap
        saved += [part, weights]
        coefs, coefs_theirs = merged, merged_theirs
        bit *= 2
    rows_theirs = swap(rows, "gx", bit)

    solved, rows = call(
        functools.partial(y_start_kernel, len(saved) // 2),
        (rows, rows_theirs, missing, *saved, local_t, cx_t, wx_t, cy, wy, coef_y),
        [(fields, ny, nx, nz), (16, nx, nz)],
        scratch=[pltpu.VMEM((fields, ny, nz), F32)] * 2,
    )
    (local_y,) = call(y_local_kernel, (solved, ivy, ry), [(fields, ny, nx, nz)])
    saved = []
    shape = (nx, nz)
    bit = 1
    while 2 * bit < my:
        last = 4 * bit == my
        rows, part, weights = call(
            functools.partial(y_merge_kernel, "gy", bit, last),
            (rows, swap(rows, "gy", bit)),
            [(7 if last else 16,) + shape, (4,) + shape, (6,) + shape],
        )
        saved += [part, weights]
        bit *= 2
    rows_theirs = swap(rows, "gy", bit)
    (out,) = call(
        functools.partial(finish_kernel, len(saved) // 2),
        (rows, rows_theirs, *saved, local_y, cy, wy),
        [(fields, nx, ny, nz)],
        scratch=[pltpu.VMEM((fields, nx, ny, nz), F32), pltpu.SemaphoreType.DMA((fields,))],
        out_specs=[HBM],
    )
    return out


def solution(mesh):
    placed = (P(None, "gx", "gy", None), P("gx", "gy", None))
    return jax.shard_map(
        per_device, mesh=mesh, in_specs=placed, out_specs=P(None, "gx", "gy", None), check_vma=False
    )
```

time: 41.3 us -> 38.4 us (0.930)
  waiting for transfers between devices: 20.9 us -> 16.3 us
  starting transfers between devices: 12.1 us -> 14.5 us
  local copies, waits for them, and re-layouts: 2.18 us -> 0.01 us
  Pallas kernels: 5.89 us -> 7.39 us
    ppermute x9 -> x10, waiting for transfers between devices: 20.9 us -> 16.3 us  [the longest x8 13.9 us: swap(): lax.ppermute(array, axis, [(i, i ^ bit) for i in range(lax.axis_size(axis...]
    ppermute x9 -> x10, starting transfers between devices: 12.1 us -> 14.5 us  [the longest x8 13.4 us: swap(): lax.ppermute(array, axis, [(i, i ^ bit) for i in range(lax.axis_size(axis...]
    unnamed x8 -> x4, local copies, waits for them, and re-layouts: 2.18 us -> 0.01 us
    pallas_call x10 -> x12, Pallas kernels: 5.89 us -> 7.39 us  [call(): pl.pallas_call(kernel, out_shape=[jax.ShapeDtypeStruct(shape, F32) for sh...]
  transfers between devices with their start and end apart: 9 -> 10, of which waited for: 6 -> 7; matrix products, arithmetic and copies ran while one was open for 0% -> 0% of each run, Pallas kernels for 6% -> 6%
where the time goes in v3:
time: 38.4 us; the launch traced here: 38.2 us
  waiting for transfers between devices  16.3 us (42%)
  starting transfers between devices  14.5 us (38%)
  Pallas kernels  7.39 us (19%)
    ppermute x8, waiting for transfers between devices, swap(): lax.ppermute(array, axis, [(i, i ^ bit) for i in range(lax.axis_size(axis...  13.9 us
    ppermute x8, starting transfers between devices, swap(): lax.ppermute(array, axis, [(i, i ^ bit) for i in range(lax.axis_size(axis...  13.4 us
    pallas_call x12, Pallas kernels, call(): pl.pallas_call(kernel, out_shape=[jax.ShapeDtypeStruct(shape, F32) for sh...  7.39 us
    ppermute x1, waiting for transfers between devices, per_device(): lax.ppermute(y_edge_odd, 'gy', [(i, (i - 1 ^ 1) + 1) if 0 < i < my - 1 el...  2.37 us
    ppermute x1, starting transfers between devices, per_device(): lax.ppermute(y_edge_odd, 'gy', [(i, (i - 1 ^ 1) + 1) if 0 < i < my - 1 el...  1.13 us
  transfers between devices with their start and end apart: 10, of which 7 were waited for; matrix products, arithmetic and copies ran while one was open for 0% of the time, Pallas kernels for 6%

profile of v3, /device:TPU:0, one launch (start us, length us, event | category | flops | bytes accessed | tf_op | source)
XLA Modules:
  0.0 38.2 jit_solution(9811219275439352902)
XLA Ops:
  0.0 1.4 %shard_map.28 = (f32[4,32,128]{2,1,0:T(8,128)S(1)}, f32[4,16,128]{2,1,0:T(8,128)S(1)}, f32[4,16,128]{2,1,0:T(8,128)S(1)}, f32[2,16,32,128]{3,2,1,0:T(8,128)S(1)}...) custom-call(f32[4,16,32,128]{3,2,1,0:T(8,128)} %flow.3, ...), custom_call_target="tpu_custom_call" | custom-call | flops 1000 | bytes 1000 | tf_op jit(solution)/shard_map/pallas_call | solution.py:21
  1.4 3.0 %collective-permute-start.3 = (f32[8,32,128]{2,1,0:T(8,128)S(1)}, f32[8,32,128]{2,1,0:T(8,128)S(1)}, u32[]{:S(2)}, u32[]{:S(2)}) collective-permute-start(f32[8,32,128]{2,1,0:T(8,128)S(1)} %get-tuple-element.42.mine.coef_mine), channel_id=1, source_target_pairs={{0,4},{4,0},{8,12},{12,8},{16,20},{20,16},{24,28},{28,24},{1,5},{5... | collective-permute-start | bytes 393224 | tf_op jit(solution)/shard_map/ppermute | solution.py:360
  4.4 0.5 %collective-permute-start.1 = (f32[4,16,128]{2,1,0:T(8,128)S(1)}, f32[4,16,128]{2,1,0:T(8,128)S(1)}, u32[]{:S(2)}, u32[]{:S(2)}) collective-permute-start(f32[4,16,128]{2,1,0:T(8,128)S(1)} %get-tuple-element.38), channel_id=1, source_target_pairs={{0,1},{1,0},{2,3},{3,2},{4,5},{5,4},{6,7},{7,6},{8,9},{9,8},{10,11... | collective-permute-start | bytes 98312 | tf_op jit(solution)/shard_map/ppermute | solution.py:360
  4.9 1.1 %collective-permute-start.2 = (f32[4,16,128]{2,1,0:T(8,128)S(1)}, f32[4,16,128]{2,1,0:T(8,128)S(1)}, u32[]{:S(2)}, u32[]{:S(2)}) collective-permute-start(f32[4,16,128]{2,1,0:T(8,128)S(1)} %get-tuple-element.39), channel_id=1, source_target_pairs={{0,3},{1,2},{2,1},{3,0},{4,7},{5,6},{6,5},{7,4},{8,11},{9,10},{10,... | collective-permute-start | bytes 98312 | tf_op jit(solution)/shard_map/ppermute | solution.py:385
  6.0 2.4 %collective-permute-done.2.y_odd = f32[4,16,128]{2,1,0:T(8,128)S(1)} collective-permute-done((f32[4,16,128]{2,1,0:T(8,128)S(1)}, f32[4,16,128]{2,1,0:T(8,128)S(1)}, u32[]{:S(2)}, u32[]{:S(2)}) %collective-permute-start.2) | collective-permute-done | bytes 32800 | tf_op jit(solution)/shard_map/ppermute | solution.py:385
  8.4 0.1 collective-permute-done.3.after.theirs.coef_theirs
  8.5 0.9 %shard_map.29 = (f32[4,16,32,128]{3,2,1,0:T(8,128)S(1)}, f32[12,32,128]{2,1,0:T(8,128)S(1)}) custom-call(f32[4,16,32,128]{3,2,1,0:T(8,128)S(1)} %copy-done, f32[4,32,128]{2,1,0:T(8,128)S(1)} %collective-permute-done.x_odd, f32[4,16,128]{2,1,0:T(8,128)S(1)} %collective-permute-done.1.y_even, f32[4,16,128]{2,1,0:T(8,128)S(1)} %collective-permute-done.2.y_odd, ...), custom_call_target="tpu_custom_call" | custom-call | flops 1000 | bytes 1000 | tf_op jit(solution)/shard_map/pallas_call | solution.py:21
  9.5 2.5 %collective-permute-start.4 = (f32[12,32,128]{2,1,0:T(8,128)S(1)}, f32[12,32,128]{2,1,0:T(8,128)S(1)}, u32[]{:S(2)}, u32[]{:S(2)}) collective-permute-start(f32[12,32,128]{2,1,0:T(8,128)S(1)} %get-tuple-element.43.after.mine), channel_id=1, source_target_pairs={{0,4},{4,0},{8,12},{12,8},{16,20},{20,16},{24,28},{28,24},{1,5},{5... | collective-permute-start | bytes 589832 | tf_op jit(solution)/shard_map/ppermute | solution.py:360
  12.1 1.6 %collective-permute-start.6 = (f32[8,32,128]{2,1,0:T(8,128)S(1)}, f32[8,32,128]{2,1,0:T(8,128)S(1)}, u32[]{:S(2)}, u32[]{:S(2)}) collective-permute-start(f32[8,32,128]{2,1,0:T(8,128)S(1)} %get-tuple-element.45.near.mine.coef_mine), channel_id=1, source_target_pairs={{0,8},{4,12},{8,0},{12,4},{16,24},{20,28},{24,16},{28,20},{1,9},{5... | collective-permute-start | bytes 393224 | tf_op jit(solution)/shard_map/ppermute | solution.py:360
  13.7 3.6 %collective-permute-done.4.theirs = f32[12,32,128]{2,1,0:T(8,128)S(1)} collective-permute-done((f32[12,32,128]{2,1,0:T(8,128)S(1)}, f32[12,32,128]{2,1,0:T(8,128)S(1)}, u32[]{:S(2)}, u32[]{:S(2)}) %collective-permute-start.4) | collective-permute-done | bytes 196640 | tf_op jit(solution)/shard_map/ppermute | solution.py:360
  17.4 1.6 %collective-permute-start.5 = (f32[8,32,128]{2,1,0:T(8,128)S(1)}, f32[8,32,128]{2,1,0:T(8,128)S(1)}, u32[]{:S(2)}, u32[]{:S(2)}) collective-permute-start(f32[8,32,128]{2,1,0:T(8,128)S(1)} %get-tuple-element.46.after.mine), channel_id=1, source_target_pairs={{0,8},{4,12},{8,0},{12,4},{16,24},{20,28},{24,16},{28,20},{1,9},{5... | collective-permute-start | bytes 393224 | tf_op jit(solution)/shard_map/ppermute | solution.py:360
  19.1 3.5 %collective-permute-done.5.theirs = f32[8,32,128]{2,1,0:T(8,128)S(1)} collective-permute-done((f32[8,32,128]{2,1,0:T(8,128)S(1)}, f32[8,32,128]{2,1,0:T(8,128)S(1)}, u32[]{:S(2)}, u32[]{:S(2)}) %collective-permute-start.5) | collective-permute-done | bytes 131104 | tf_op jit(solution)/shard_map/ppermute | solution.py:360
  22.6 0.6 %shard_map.33 = (f32[7,32,128]{2,1,0:T(8,128)S(1)}, f32[4,32,128]{2,1,0:T(8,128)S(1)}, f32[4,32,128]{2,1,0:T(8,128)}) custom-call(f32[8,32,128]{2,1,0:T(8,128)S(1)} %get-tuple-element.46.after.mine, f32[8,32,128]{2,1,0:T(8,128)S(1)} %collective-permute-done.5.theirs, f32[6,32,128]{2,1,0:T(8,128)S(1)} %get-tuple-element.47.weights.refs_6_, ...), custom_call_target="tpu_custom_call" | custom-call | flops 1000 | bytes 1000 | tf_op jit(solution)/shard_map/pallas_call | solution.py:21
  23.3 2.4 %collective-permute-start.7 = (f32[7,32,128]{2,1,0:T(8,128)S(1)}, f32[7,32,128]{2,1,0:T(8,128)S(1)}, u32[]{:S(2)}, u32[]{:S(2)}) collective-permute-start(f32[7,32,128]{2,1,0:T(8,128)S(1)} %get-tuple-element.49.refs_0_), channel_id=1, source_target_pairs={{0,16},{4,20},{8,24},{12,28},{16,0},{20,4},{24,8},{28,12},{1,17},{... | collective-permute-start | bytes 344072 | tf_op jit(solution)/shard_map/ppermute | solution.py:360
  25.7 0.5 %shard_map.35 = (f32[2,32,16,128]{3,2,1,0:T(8,128)S(1)}, f32[2,32,16,128]{3,2,1,0:T(8,128)S(1)}, f32[2,32,16,128]{3,2,1,0:T(8,128)S(1)}, f32[2,32,16,128]{3,2,1,0:T(8,128)S(1)}, f32[8,16,128]{2,1,0:T(8,128)S(1)}) custom-call(f32[16,32,128]{2,1,0:T(8,128)S(1)} %copy-done.1), custom_call_target="tpu_custom_call" | custom-call | flops 1000 | bytes 1000 | tf_op jit(solution)/shard_map/pallas_call | solution.py:21
  26.2 1.4 %shard_map.34 = (f32[4,32,16,128]{3,2,1,0:T(8,128)S(1)}, f32[2,32,16,128]{3,2,1,0:T(8,128)S(1)}, f32[2,32,16,128]{3,2,1,0:T(8,128)S(1)}) custom-call(f32[4,16,32,128]{3,2,1,0:T(8,128)S(1)} %get-tuple-element.53.source, f32[2,16,32,128]{3,2,1,0:T(8,128)S(1)} %get-tuple-element.54.ivx, f32[2,16,32,128]{3,2,1,0:T(8,128)S(1)} %get-tuple-element.55.rx, ...), custom_call_target="tpu_custom_call" | custom-call | flops 1000 | bytes 1000 | tf_op jit(solution)/shard_map/pallas_call | solution.py:21
  27.7 2.8 %collective-permute-done.7.refs_1_ = f32[7,32,128]{2,1,0:T(8,128)S(1)} collective-permute-done((f32[7,32,128]{2,1,0:T(8,128)S(1)}, f32[7,32,128]{2,1,0:T(8,128)S(1)}, u32[]{:S(2)}, u32[]{:S(2)}) %collective-permute-start.7) | collective-permute-done | bytes 114720 | tf_op jit(solution)/shard_map/ppermute | solution.py:360
  30.5 0.3 shard_map.36
  30.8 0.1 collective-permute-start.8
  30.9 1.3 %collective-permute-done.8.theirs = f32[16,16,128]{2,1,0:T(8,128)S(1)} collective-permute-done((f32[16,16,128]{2,1,0:T(8,128)S(1)}, f32[16,16,128]{2,1,0:T(8,128)S(1)}, u32[]{:S(2)}, u32[]{:S(2)}) %collective-permute-start.8) | collective-permute-done | bytes 131104 | tf_op jit(solution)/shard_map/ppermute | solution.py:360
  32.3 1.6 %collective-permute-start.9 = (f32[7,16,128]{2,1,0:T(8,128)S(1)}, f32[7,16,128]{2,1,0:T(8,128)S(1)}, u32[]{:S(2)}, u32[]{:S(2)}) collective-permute-start(f32[7,16,128]{2,1,0:T(8,128)S(1)} %get-tuple-element.63.refs_0_), channel_id=1, source_target_pairs={{0,2},{1,3},{2,0},{3,1},{4,6},{5,7},{6,4},{7,5},{8,10},{9,11},{10,... | collective-permute-start | bytes 172040 | tf_op jit(solution)/shard_map/ppermute | solution.py:360
  33.9 0.3 shard_map.38.refs_4_
  34.2 2.4 %collective-permute-done.9.refs_1_ = f32[7,16,128]{2,1,0:T(8,128)S(1)} collective-permute-done((f32[7,16,128]{2,1,0:T(8,128)S(1)}, f32[7,16,128]{2,1,0:T(8,128)S(1)}, u32[]{:S(2)}, u32[]{:S(2)}) %collective-permute-start.9) | collective-permute-done | bytes 57376 | tf_op jit(solution)/shard_map/ppermute | solution.py:360
  36.5 1.7 %shard_map.39 = f32[4,16,32,128]{3,2,1,0:T(8,128)} custom-call(f32[7,16,128]{2,1,0:T(8,128)S(1)} %get-tuple-element.63.refs_0_, f32[7,16,128]{2,1,0:T(8,128)S(1)} %collective-permute-done.9.refs_1_, f32[4,16,128]{2,1,0:T(8,128)S(1)} %get-tuple-element.64.refs_2_, f32[6,16,128]{2,1,0:T(8,128)S(1)} %get-tuple-element.65.refs_3_, ...), custom_call_target="tpu_custom_call" | custom-call | flops 1000 | bytes 1000 | tf_op jit(solution)/shard_map/pallas_call | solution.py:21
  (12 shorter events, 0.2 us)
Async XLA Ops:
  0.0 8.5 %copy-start = (f32[4,16,32,128]{3,2,1,0:T(8,128)S(1)}, f32[4,16,32,128]{3,2,1,0:T(8,128)}, u32[]{:S(2)}) copy-start(f32[4,16,32,128]{3,2,1,0:T(8,128)} %flow.3) | copy-start | bytes 3145732
  1.4 7.2 %collective-permute-start.3 = (f32[8,32,128]{2,1,0:T(8,128)S(1)}, f32[8,32,128]{2,1,0:T(8,128)S(1)}, u32[]{:S(2)}, u32[]{:S(2)}) collective-permute-start(f32[8,32,128]{2,1,0:T(8,128)S(1)} %get-tuple-element.42.mine.coef_mine), channel_id=1, source_target_pairs={{0,4},{4,0},{8,12},{12,8},{16,20},{20,16},{24,28},{28,24},{1,5},{5... | collective-permute-start | bytes 393224 | tf_op jit(solution)/shard_map/ppermute | solution.py:360
  4.4 4.0 %collective-permute-start = (f32[4,32,128]{2,1,0:T(8,128)S(1)}, f32[4,32,128]{2,1,0:T(8,128)S(1)}, u32[]{:S(2)}, u32[]{:S(2)}) collective-permute-start(f32[4,32,128]{2,1,0:T(8,128)S(1)} %get-tuple-element.37), channel_id=1, source_target_pairs={{0,1},{1,0},{2,3},{3,2},{4,8},{5,9},{6,10},{7,11},{8,4},{9,5},{10,... | collective-permute-start | bytes 196616 | tf_op jit(solution)/shard_map/ppermute | solution.py:384
  4.4 1.6 %collective-permute-start.1 = (f32[4,16,128]{2,1,0:T(8,128)S(1)}, f32[4,16,128]{2,1,0:T(8,128)S(1)}, u32[]{:S(2)}, u32[]{:S(2)}) collective-permute-start(f32[4,16,128]{2,1,0:T(8,128)S(1)} %get-tuple-element.38), channel_id=1, source_target_pairs={{0,1},{1,0},{2,3},{3,2},{4,5},{5,4},{6,7},{7,6},{8,9},{9,8},{10,11... | collective-permute-start | bytes 98312 | tf_op jit(solution)/shard_map/ppermute | solution.py:360
  4.9 3.5 %collective-permute-start.2 = (f32[4,16,128]{2,1,0:T(8,128)S(1)}, f32[4,16,128]{2,1,0:T(8,128)S(1)}, u32[]{:S(2)}, u32[]{:S(2)}) collective-permute-start(f32[4,16,128]{2,1,0:T(8,128)S(1)} %get-tuple-element.39), channel_id=1, source_target_pairs={{0,3},{1,2},{2,1},{3,0},{4,7},{5,6},{6,5},{7,4},{8,11},{9,10},{10,... | collective-permute-start | bytes 98312 | tf_op jit(solution)/shard_map/ppermute | solution.py:385
  9.5 7.9 %collective-permute-start.4 = (f32[12,32,128]{2,1,0:T(8,128)S(1)}, f32[12,32,128]{2,1,0:T(8,128)S(1)}, u32[]{:S(2)}, u32[]{:S(2)}) collective-permute-start(f32[12,32,128]{2,1,0:T(8,128)S(1)} %get-tuple-element.43.after.mine), channel_id=1, source_target_pairs={{0,4},{4,0},{8,12},{12,8},{16,20},{20,16},{24,28},{28,24},{1,5},{5... | collective-permute-start | bytes 589832 | tf_op jit(solution)/shard_map/ppermute | solution.py:360
  12.1 7.0 %collective-permute-start.6 = (f32[8,32,128]{2,1,0:T(8,128)S(1)}, f32[8,32,128]{2,1,0:T(8,128)S(1)}, u32[]{:S(2)}, u32[]{:S(2)}) collective-permute-start(f32[8,32,128]{2,1,0:T(8,128)S(1)} %get-tuple-element.45.near.mine.coef_mine), channel_id=1, source_target_pairs={{0,8},{4,12},{8,0},{12,4},{16,24},{20,28},{24,16},{28,20},{1,9},{5... | collective-permute-start | bytes 393224 | tf_op jit(solution)/shard_map/ppermute | solution.py:360
  17.4 5.2 %collective-permute-start.5 = (f32[8,32,128]{2,1,0:T(8,128)S(1)}, f32[8,32,128]{2,1,0:T(8,128)S(1)}, u32[]{:S(2)}, u32[]{:S(2)}) collective-permute-start(f32[8,32,128]{2,1,0:T(8,128)S(1)} %get-tuple-element.46.after.mine), channel_id=1, source_target_pairs={{0,8},{4,12},{8,0},{12,4},{16,24},{20,28},{24,16},{28,20},{1,9},{5... | collective-permute-start | bytes 393224 | tf_op jit(solution)/shard_map/ppermute | solution.py:360
  22.6 3.0 %copy-start.1 = (f32[16,32,128]{2,1,0:T(8,128)S(1)}, f32[16,32,128]{2,1,0:T(8,128)}, u32[]{:S(2)}) copy-start(f32[16,32,128]{2,1,0:T(8,128)} %visc.3) | copy-start | bytes 786436
  23.3 7.2 %collective-permute-start.7 = (f32[7,32,128]{2,1,0:T(8,128)S(1)}, f32[7,32,128]{2,1,0:T(8,128)S(1)}, u32[]{:S(2)}, u32[]{:S(2)}) collective-permute-start(f32[7,32,128]{2,1,0:T(8,128)S(1)} %get-tuple-element.49.refs_0_), channel_id=1, source_target_pairs={{0,16},{4,20},{8,24},{12,28},{16,0},{20,4},{24,8},{28,12},{1,17},{... | collective-permute-start | bytes 344072 | tf_op jit(solution)/shard_map/ppermute | solution.py:360
  30.8 1.4 %collective-permute-start.8 = (f32[16,16,128]{2,1,0:T(8,128)S(1)}, f32[16,16,128]{2,1,0:T(8,128)S(1)}, u32[]{:S(2)}, u32[]{:S(2)}) collective-permute-start(f32[16,16,128]{2,1,0:T(8,128)S(1)} %get-tuple-element.62.mine), channel_id=1, source_target_pairs={{0,1},{1,0},{2,3},{3,2},{4,5},{5,4},{6,7},{7,6},{8,9},{9,8},{10,11... | collective-permute-start | bytes 393224 | tf_op jit(solution)/shard_map/ppermute | solution.py:360
  32.3 4.2 %collective-permute-start.9 = (f32[7,16,128]{2,1,0:T(8,128)S(1)}, f32[7,16,128]{2,1,0:T(8,128)S(1)}, u32[]{:S(2)}, u32[]{:S(2)}) collective-permute-start(f32[7,16,128]{2,1,0:T(8,128)S(1)} %get-tuple-element.63.refs_0_), channel_id=1, source_target_pairs={{0,2},{1,3},{2,0},{3,1},{4,6},{5,7},{6,4},{7,5},{8,10},{9,11},{10,... | collective-permute-start | bytes 172040 | tf_op jit(solution)/shard_map/ppermute | solution.py:360

commit v4 on v3

--- a/solution.py
+++ b/solution.py
@@ -99,7 +99,7 @@
         copy.wait()
 
 
-def factor_y_kernel(visc, ivy, ry, cy, wy, coef_y):
+def factor_y_kernel(visc, ivy, ry, cy, wy, coef_y, cy_t, wy_t):
     nx, ny, nz = visc.shape
     iy = lax.axis_index("gy")
     rows = visc.reshape(nx * ny, nz)
@@ -111,15 +111,16 @@
     coef_rows(cy, wy, coef_y, ny)
     coef_y[6] = row_y(0)
     coef_y[7] = row_y(ny - 1)
-
-
-def source_kernel(flow, x_odd, y_even, y_odd, cx, wx, after, source, message):
+    for part, turned in ((cy, cy_t), (wy, wy_t)):
+        for group in range(2):
+            out = turned.at[group].reshape(nx * ny, nz)
+            for j in range(ny):
+                out[pl.ds(j, nx, stride=ny), :] = part[group, j]
+
+
+def source_kernel(flow, cx, wx, source, message):
     _, nx, ny, nz = flow.shape
-    ix, iy = lax.axis_index("gx"), lax.axis_index("gy")
-    x_par, y_par = lax.rem(ix, 2) == 0, lax.rem(iy, 2) == 0
-    no_low = (ix == 0) | (lax.rem(ix, 2) == 1)
-    no_high = (ix == lax.axis_size("gx") - 1) | x_par
-    y_first, y_last = iy == 0, iy == lax.axis_size("gy") - 1
+    x_par = lax.rem(lax.axis_index("gx"), 2) == 0
     row = lax.broadcasted_iota(jnp.int32, (ny, nz), 0)
     left = [None] * 4
     right = [None] * 4
@@ -127,14 +128,10 @@
         velocity = [ADVECT * 0.5 * flow[c, i] for c in range(3)]
         for c in range(4):
             f = flow[c, i]
-            down = pick(no_low, 0.0, x_odd[c]) if i == 0 else flow[c, i - 1]
-            up = pick(no_high, 0.0, x_odd[c]) if i == nx - 1 else flow[c, i + 1]
-            y_low = pick(y_par, y_odd[c, pl.ds(i, 1)], y_even[c, pl.ds(i, 1)])
-            y_high = pick(y_par, y_even[c, pl.ds(i, 1)], y_odd[c, pl.ds(i, 1)])
-            y_low = pick(y_first, 0.0, y_low)
-            y_high = pick(y_last, 0.0, y_high)
-            below = pick(row == 0, y_low, pltpu.roll(f, 1, 0))
-            above = pick(row == ny - 1, y_high, pltpu.roll(f, ny - 1, 0))
+            down = 0.0 if i == 0 else flow[c, i - 1]
+            up = 0.0 if i == nx - 1 else flow[c, i + 1]
+            below = pick(row == 0, 0.0, pltpu.roll(f, 1, 0))
+            above = pick(row == ny - 1, 0.0, pltpu.roll(f, ny - 1, 0))
             z_low = pltpu.roll(f, 1, 1)
             z_high = pltpu.roll(f, nz - 1, 1)
             s = f - (
@@ -153,6 +150,37 @@
         message[c] = left[c]
         message[4 + c] = right[c]
         message[8 + c] = pick(x_par, flow[c, nx - 1], flow[c, 0])
+
+
+def edge_kernel(partial, x_edge, y_edge_even, y_edge_odd, x_odd, y_even, y_odd, cx, wx, after, message, gap_x, gap_y):
+    _, nx, ny, nz = cx.shape
+    ix, iy = lax.axis_index("gx"), lax.axis_index("gy")
+    x_par, y_par = lax.rem(ix, 2) == 0, lax.rem(iy, 2) == 0
+    x_none = (ix == 0) | (ix == lax.axis_size("gx") - 1)
+    y_first, y_last = iy == 0, iy == lax.axis_size("gy") - 1
+    half = 0.5 * ADVECT
+    message[pl.ds(8, 4)] = partial[pl.ds(8, 4)]
+    own_low = half * pick(y_par, y_edge_odd[1], y_edge_even[1])
+    own_high = half * pick(y_par, y_edge_even[1], y_edge_odd[1])
+    own_x = half * x_edge[0]
+    for c in range(4):
+        group = GROUPS[c]
+        low = own_low * pick(y_par, y_odd[c], y_even[c])
+        high = -own_high * pick(y_par, y_even[c], y_odd[c])
+        low = pick(y_first, 0.0, low)
+        high = pick(y_last, 0.0, high)
+        gap_y[c] = low
+        gap_y[4 + c] = high
+        across = own_x * x_odd[c]
+        across = pick(x_none, 0.0, pick(x_par, across, -across))
+        gap_x[c] = across
+        for k, part in ((c, cx), (4 + c, wx)):
+            edge = pick(x_par, part[group, 0], part[group, nx - 1])
+            message[k] = partial[k] + edge * across
+            rows = part.at[group].reshape(nx * ny, nz)
+            for j, gap in ((0, low), (ny - 1, high)):
+                line = jnp.sum(rows[pl.ds(j, nx, stride=ny), :] * gap, axis=0, keepdims=True)
+                message[k, pl.ds(j, 1)] = message[k, pl.ds(j, 1)] + line
 
 
 def coef_part(axis, bit, last, mine, theirs, at, union, union_at, weights):
@@ -227,7 +255,7 @@
     coef_part(axis, bit, last, mine, theirs, 0, union, 0, weights)
 
 
-def x_merge_kernel(axis, bit, last, edged, mine, theirs, weights, coef_mine, coef_theirs, near, union, saved, missing):
+def x_merge_kernel(axis, bit, last, edged, mine, theirs, weights, coef_mine, coef_theirs, near, union, saved, missing=None):
     row_part(
         axis, bit, last, mine, theirs, weights, union, saved,
         (coef_mine, coef_theirs, missing) if edged else None,
@@ -270,14 +298,27 @@
     return result
 
 
-def local_kernel(source, ivx, rx, cx, wx, local_t, cx_t, wx_t, scratch):
+def local_kernel(source, gap_x, gap_y, ivx, rx, cx, wx, local_t, cx_t, wx_t, scratch):
     _, nx, ny, nz = source.shape
-    for c in range(4):
-        group = GROUPS[c]
-        running = source[c, 0]
+    x_par = lax.rem(lax.axis_index("gx"), 2) == 0
+    row = lax.broadcasted_iota(jnp.int32, (ny, nz), 0)
+
+    def right_side(c, i):
+        s = source[c, i]
+        s = s + pick(row == 0, gap_y[c, pl.ds(i, 1)], 0.0)
+        s = s + pick(row == ny - 1, gap_y[4 + c, pl.ds(i, 1)], 0.0)
+        if i == 0:
+            s = s + pick(x_par, gap_x[c], 0.0)
+        if i == nx - 1:
+            s = s + pick(x_par, 0.0, gap_x[c])
+        return s
+
+    for c in range(4):
+        group = GROUPS[c]
+        running = right_side(c, 0)
         forward = [running]
         for i in range(1, nx):
-            running = source[c, i] + rx[group, i - 1] * running
+            running = right_side(c, i) + rx[group, i - 1] * running
             forward.append(running)
         value = running * ivx[group, nx - 1]
         scratch[c, pl.ds((nx - 1) * ny, ny)] = value
@@ -323,33 +364,35 @@
     _, ny, nx, nz = solved.shape
     for c in range(4):
         group = GROUPS[c]
+        rows = local.at[c].reshape(nx * ny, nz)
         running = solved[c, 0]
         forward = [running]
         for j in range(1, ny):
             running = solved[c, j] + ry[group, j - 1] * running
             forward.append(running)
         value = running * ivy[group, ny - 1]
-        local[c, ny - 1] = value
+        rows[pl.ds(ny - 1, nx, stride=ny), :] = value
         for j in range(ny - 2, -1, -1):
             value = forward[j] * ivy[group, j] + ry[group, j] * value
-            local[c, j] = value
+            rows[pl.ds(j, nx, stride=ny), :] = value
 
 
 def finish_kernel(stages, *refs):
     mine, theirs = refs[:2]
     parts = refs[2 : 2 + 2 * stages]
-    local, cy, wy, out, buffer, sems = refs[2 + 2 * stages :]
+    local, cy_t, wy_t, out, buffer, flux_low, flux_high, sems = refs[2 + 2 * stages :]
     saved = list(zip(parts[::2], parts[1::2]))
-    _, ny, nx, nz = local.shape
-    ends = fluxes("gy", mine, theirs, saved)
+    nx = local.shape[1]
+    for c, (low, high) in enumerate(fluxes("gy", mine, theirs, saved)):
+        flux_low[c] = low
+        flux_high[c] = high
     copies = []
     for c in range(4):
         group = GROUPS[c]
-        low, high = ends[c]
-        rows = buffer.at[c].reshape(nx * ny, nz)
-        for j in range(ny):
-            value = local[c, j] + (wy[group, j] * high - cy[group, j] * low)
-            rows[pl.ds(j, nx, stride=ny), :] = value
+        for i in range(nx):
+            low = flux_low[c, pl.ds(i, 1)]
+            high = flux_high[c, pl.ds(i, 1)]
+            buffer[c, i] = local[c, i] + (wy_t[group, i] * high - cy_t[group, i] * low)
         copies.append(pltpu.make_async_copy(buffer.at[c], out.at[c], sems.at[c]))
         copies[-1].start()
     for copy in copies:
@@ -387,17 +430,20 @@
     )
     y_even = swap(y_edge_even, "gy", 1)
 
-    ivy, ry, cy, wy, coef_y = call(factor_y_kernel, (visc,), [along_y] * 4 + [(8, nx, nz)])
+    ivy, ry, cy, wy, coef_y, cy_t, wy_t = call(
+        factor_y_kernel, (visc,), [along_y] * 4 + [(8, nx, nz)] + [along_x] * 2
+    )
     coef_x_theirs = swap(coef_x, "gx", 1)
-    source, message = call(
-        source_kernel,
-        (flow, x_odd, y_even, y_odd, cx, wx, coef_x_theirs),
-        in_specs=after_all(6),
-        outs=[(fields, nx, ny, nz), (12, ny, nz)],
+    source, partial = call(source_kernel, (flow, cx, wx), [(fields, nx, ny, nz), (12, ny, nz)])
+    message, gap_x, gap_y = call(
+        edge_kernel,
+        (partial, x_edge, y_edge_even, y_edge_odd, x_odd, y_even, y_odd, cx, wx, coef_x_theirs),
+        [(12, ny, nz), (fields, ny, nz), (2 * fields, nx, nz)],
+        in_specs=after_all(9),
     )
     local_t, cx_t, wx_t = call(
         local_kernel,
-        (source, ivx, rx, cx, wx),
+        (source, gap_x, gap_y, ivx, rx, cx, wx),
         [(fields, ny, nx, nz), along_y, along_y],
         scratch=[pltpu.VMEM((fields, nx * ny, nz), F32)],
         cost=1000,
@@ -417,13 +463,13 @@
             in_specs=after_all(2),
         )
         merged_theirs = merged if last else swap(merged, "gx", 2 * bit)
-        rows, part, gap = call(
+        rows, part, *gap = call(
             functools.partial(x_merge_kernel, "gx", bit, last, bit == 1),
             (rows, rows_theirs, weights, coefs, coefs_theirs, merged),
-            [(7 if last else 8,) + shape, (4,) + shape, (4,) + shape],
+            [(7 if last else 8,) + shape, (4,) + shape] + [(4,) + shape] * (bit == 1),
         )
-        if bit == 1:
-            missing = gap
+        if gap:
+            missing = gap[0]
         saved += [part, weights]
         coefs, coefs_theirs = merged, merged_theirs
         bit *= 2
@@ -435,7 +481,7 @@
         [(fields, ny, nx, nz), (16, nx, nz)],
         scratch=[pltpu.VMEM((fields, ny, nz), F32)] * 2,
     )
-    (local_y,) = call(y_local_kernel, (solved, ivy, ry), [(fields, ny, nx, nz)])
+    (local_y,) = call(y_local_kernel, (solved, ivy, ry), [(fields, nx, ny, nz)])
     saved = []
     shape = (nx, nz)
     bit = 1
@@ -451,9 +497,14 @@
     rows_theirs = swap(rows, "gy", bit)
     (out,) = call(
         functools.partial(finish_kernel, len(saved) // 2),
-        (rows, rows_theirs, *saved, local_y, cy, wy),
+        (rows, rows_theirs, *saved, local_y, cy_t, wy_t),
         [(fields, nx, ny, nz)],
-        scratch=[pltpu.VMEM((fields, nx, ny, nz), F32), pltpu.SemaphoreType.DMA((fields,))],
+        scratch=[
+            pltpu.VMEM((fields, nx, ny, nz), F32),
+            pltpu.VMEM((fields, nx, nz), F32),
+            pltpu.VMEM((fields, nx, nz), F32),
+            pltpu.SemaphoreType.DMA((fields,)),
+        ],
         out_specs=[HBM],
     )
     return out

time: 38.4 us -> 36.4 us (0.948)
  waiting for transfers between devices: 16.3 us -> 14.1 us
    ppermute x8, waiting for transfers between devices: 13.9 us -> 12.6 us  [swap(): lax.ppermute(array, axis, [(i, i ^ bit) for i in range(lax.axis_size(axis...]
    ppermute x1, waiting for transfers between devices: 2.37 us -> 1.5 us  [per_device(): lax.ppermute(y_edge_odd, 'gy', [(i, (i - 1 ^ 1) + 1) if 0 < i < my - 1 el...]
    pallas_call x12 -> x13, Pallas kernels: 7.39 us -> 7.51 us  [call(): pl.pallas_call(kernel, out_shape=[jax.ShapeDtypeStruct(shape, F32) for sh...]
  transfers between devices with their start and end apart: 10 -> 10, of which waited for: 7 -> 7; matrix products, arithmetic and copies ran while one was open for 0% -> 0% of each run, Pallas kernels for 6% -> 13%
where the time goes in v4:
time: 36.4 us; the launch traced here: 36.3 us
  starting transfers between devices  14.6 us (40%)
  waiting for transfers between devices  14.1 us (39%)
  Pallas kernels  7.51 us (21%)
    ppermute x8, starting transfers between devices, swap(): lax.ppermute(array, axis, [(i, i ^ bit) for i in range(lax.axis_size(axis...  13.5 us
    ppermute x8, waiting for transfers between devices, swap(): lax.ppermute(array, axis, [(i, i ^ bit) for i in range(lax.axis_size(axis...  12.6 us
    pallas_call x13, Pallas kernels, call(): pl.pallas_call(kernel, out_shape=[jax.ShapeDtypeStruct(shape, F32) for sh...  7.51 us
    ppermute x1, waiting for transfers between devices, per_device(): lax.ppermute(y_edge_odd, 'gy', [(i, (i - 1 ^ 1) + 1) if 0 < i < my - 1 el...  1.5 us
    ppermute x1, starting transfers between devices, per_device(): lax.ppermute(y_edge_odd, 'gy', [(i, (i - 1 ^ 1) + 1) if 0 < i < my - 1 el...  1.13 us
  transfers between devices with their start and end apart: 10, of which 7 were waited for; matrix products, arithmetic and copies ran while one was open for 0% of the time, Pallas kernels for 13%

profile of v4, /device:TPU:0, one launch (start us, length us, event | category | flops | bytes accessed | tf_op | source)
XLA Modules:
  0.0 36.3 jit_solution(11796666548962459173)
XLA Ops:
  0.0 1.4 %shard_map.28 = (f32[4,32,128]{2,1,0:T(8,128)S(1)}, f32[4,16,128]{2,1,0:T(8,128)S(1)}, f32[4,16,128]{2,1,0:T(8,128)S(1)}, f32[2,16,32,128]{3,2,1,0:T(8,128)S(1)}...) custom-call(f32[4,16,32,128]{3,2,1,0:T(8,128)} %flow.3, ...), custom_call_target="tpu_custom_call" | custom-call | flops 1000 | bytes 1000 | tf_op jit(solution)/shard_map/pallas_call | solution.py:21
  1.4 3.0 %collective-permute-start.3 = (f32[8,32,128]{2,1,0:T(8,128)S(1)}, f32[8,32,128]{2,1,0:T(8,128)S(1)}, u32[]{:S(2)}, u32[]{:S(2)}) collective-permute-start(f32[8,32,128]{2,1,0:T(8,128)S(1)} %get-tuple-element.48.mine.coef_mine), channel_id=1, source_target_pairs={{0,4},{4,0},{8,12},{12,8},{16,20},{20,16},{24,28},{28,24},{1,5},{5... | collective-permute-start | bytes 393224 | tf_op jit(solution)/shard_map/ppermute | solution.py:403
  4.4 0.5 %collective-permute-start.1 = (f32[4,16,128]{2,1,0:T(8,128)S(1)}, f32[4,16,128]{2,1,0:T(8,128)S(1)}, u32[]{:S(2)}, u32[]{:S(2)}) collective-permute-start(f32[4,16,128]{2,1,0:T(8,128)S(1)} %get-tuple-element.46.y_edge_even), channel_id=1, source_target_pairs={{0,1},{1,0},{2,3},{3,2},{4,5},{5,4},{6,7},{7,6},{8,9},{9,8},{10,11... | collective-permute-start | bytes 98312 | tf_op jit(solution)/shard_map/ppermute | solution.py:403
  4.9 1.1 %collective-permute-start.2 = (f32[4,16,128]{2,1,0:T(8,128)S(1)}, f32[4,16,128]{2,1,0:T(8,128)S(1)}, u32[]{:S(2)}, u32[]{:S(2)}) collective-permute-start(f32[4,16,128]{2,1,0:T(8,128)S(1)} %get-tuple-element.47.y_edge_odd), channel_id=1, source_target_pairs={{0,3},{1,2},{2,1},{3,0},{4,7},{5,6},{6,5},{7,4},{8,11},{9,10},{10,... | collective-permute-start | bytes 98312 | tf_op jit(solution)/shard_map/ppermute | solution.py:428
  6.0 0.9 %shard_map.29 = (f32[4,16,32,128]{3,2,1,0:T(8,128)S(1)}, f32[12,32,128]{2,1,0:T(8,128)S(1)}) custom-call(f32[4,16,32,128]{3,2,1,0:T(8,128)S(1)} %copy-done, f32[2,16,32,128]{3,2,1,0:T(8,128)S(1)} %get-tuple-element.42.cx, f32[2,16,32,128]{3,2,1,0:T(8,128)S(1)} %get-tuple-element.43.wx), custom_call_target="tpu_custom_call" | custom-call | flops 1000 | bytes 1000 | tf_op jit(solution)/shard_map/pallas_call | solution.py:21
  6.9 1.5 %collective-permute-done.2.y_odd = f32[4,16,128]{2,1,0:T(8,128)S(1)} collective-permute-done((f32[4,16,128]{2,1,0:T(8,128)S(1)}, f32[4,16,128]{2,1,0:T(8,128)S(1)}, u32[]{:S(2)}, u32[]{:S(2)}) %collective-permute-start.2) | collective-permute-done | bytes 32800 | tf_op jit(solution)/shard_map/ppermute | solution.py:428
  8.4 0.1 collective-permute-done.3.after.theirs.coef_theirs
  8.5 0.1 shard_map.30
  8.7 2.5 %collective-permute-start.4 = (f32[12,32,128]{2,1,0:T(8,128)S(1)}, f32[12,32,128]{2,1,0:T(8,128)S(1)}, u32[]{:S(2)}, u32[]{:S(2)}) collective-permute-start(f32[12,32,128]{2,1,0:T(8,128)S(1)} %get-tuple-element.49.after.mine), channel_id=1, source_target_pairs={{0,4},{4,0},{8,12},{12,8},{16,20},{20,16},{24,28},{28,24},{1,5},{5... | collective-permute-start | bytes 589832 | tf_op jit(solution)/shard_map/ppermute | solution.py:403
  11.2 1.6 %collective-permute-start.6 = (f32[8,32,128]{2,1,0:T(8,128)S(1)}, f32[8,32,128]{2,1,0:T(8,128)S(1)}, u32[]{:S(2)}, u32[]{:S(2)}) collective-permute-start(f32[8,32,128]{2,1,0:T(8,128)S(1)} %get-tuple-element.51.near.mine.coef_mine), channel_id=1, source_target_pairs={{0,8},{4,12},{8,0},{12,4},{16,24},{20,28},{24,16},{28,20},{1,9},{5... | collective-permute-start | bytes 393224 | tf_op jit(solution)/shard_map/ppermute | solution.py:403
  12.9 3.6 %collective-permute-done.4.theirs = f32[12,32,128]{2,1,0:T(8,128)S(1)} collective-permute-done((f32[12,32,128]{2,1,0:T(8,128)S(1)}, f32[12,32,128]{2,1,0:T(8,128)S(1)}, u32[]{:S(2)}, u32[]{:S(2)}) %collective-permute-start.4) | collective-permute-done | bytes 196640 | tf_op jit(solution)/shard_map/ppermute | solution.py:403
  16.6 1.6 %collective-permute-start.5 = (f32[8,32,128]{2,1,0:T(8,128)S(1)}, f32[8,32,128]{2,1,0:T(8,128)S(1)}, u32[]{:S(2)}, u32[]{:S(2)}) collective-permute-start(f32[8,32,128]{2,1,0:T(8,128)S(1)} %get-tuple-element.52.after.mine), channel_id=1, source_target_pairs={{0,8},{4,12},{8,0},{12,4},{16,24},{20,28},{24,16},{28,20},{1,9},{5... | collective-permute-start | bytes 393224 | tf_op jit(solution)/shard_map/ppermute | solution.py:403
  18.3 3.5 %collective-permute-done.5.theirs = f32[8,32,128]{2,1,0:T(8,128)S(1)} collective-permute-done((f32[8,32,128]{2,1,0:T(8,128)S(1)}, f32[8,32,128]{2,1,0:T(8,128)S(1)}, u32[]{:S(2)}, u32[]{:S(2)}) %collective-permute-start.5) | collective-permute-done | bytes 131104 | tf_op jit(solution)/shard_map/ppermute | solution.py:403
  21.9 2.5 %collective-permute-start.7 = (f32[7,32,128]{2,1,0:T(8,128)S(1)}, f32[7,32,128]{2,1,0:T(8,128)S(1)}, u32[]{:S(2)}, u32[]{:S(2)}) collective-permute-start(f32[7,32,128]{2,1,0:T(8,128)S(1)} %get-tuple-element.55.refs_0_), channel_id=1, source_target_pairs={{0,16},{4,20},{8,24},{12,28},{16,0},{20,4},{24,8},{28,12},{1,17},{... | collective-permute-start | bytes 344072 | tf_op jit(solution)/shard_map/ppermute | solution.py:403
  24.3 1.3 %shard_map.36 = (f32[2,32,16,128]{3,2,1,0:T(8,128)S(1)}, f32[2,32,16,128]{3,2,1,0:T(8,128)S(1)}, f32[2,32,16,128]{3,2,1,0:T(8,128)S(1)}, f32[2,32,16,128]{3,2,1,...) custom-call(f32[16,32,128]{2,1,0:T(8,128)S(1)} %copy-done.1), custom_call_target="tpu_custom_call" | custom-call | flops 1000 | bytes 1000 | tf_op jit(solution)/shard_map/pallas_call | solution.py:21
  25.6 1.5 %shard_map.35 = (f32[4,32,16,128]{3,2,1,0:T(8,128)S(1)}, f32[2,32,16,128]{3,2,1,0:T(8,128)S(1)}, f32[2,32,16,128]{3,2,1,0:T(8,128)S(1)}) custom-call(f32[4,16,32,128]{3,2,1,0:T(8,128)S(1)} %get-tuple-element.59.source, f32[4,32,128]{2,1,0:T(8,128)S(1)} %get-tuple-element.60.gap_x, f32[8,16,128]{2,1,0:T(8,128)S(1)} %get-tuple-element.61.gap_y, ...), custom_call_target="tpu_custom_call" | custom-call | flops 1000 | bytes 1000 | tf_op jit(solution)/shard_map/pallas_call | solution.py:21
  27.1 2.0 %collective-permute-done.7.refs_1_ = f32[7,32,128]{2,1,0:T(8,128)S(1)} collective-permute-done((f32[7,32,128]{2,1,0:T(8,128)S(1)}, f32[7,32,128]{2,1,0:T(8,128)S(1)}, u32[]{:S(2)}, u32[]{:S(2)}) %collective-permute-start.7) | collective-permute-done | bytes 114720 | tf_op jit(solution)/shard_map/ppermute | solution.py:403
  29.1 0.3 shard_map.37
  29.5 0.1 collective-permute-start.8
  29.6 1.3 %collective-permute-done.8.theirs = f32[16,16,128]{2,1,0:T(8,128)S(1)} collective-permute-done((f32[16,16,128]{2,1,0:T(8,128)S(1)}, f32[16,16,128]{2,1,0:T(8,128)S(1)}, u32[]{:S(2)}, u32[]{:S(2)}) %collective-permute-start.8) | collective-permute-done | bytes 131104 | tf_op jit(solution)/shard_map/ppermute | solution.py:403
  30.9 1.6 %collective-permute-start.9 = (f32[7,16,128]{2,1,0:T(8,128)S(1)}, f32[7,16,128]{2,1,0:T(8,128)S(1)}, u32[]{:S(2)}, u32[]{:S(2)}) collective-permute-start(f32[7,16,128]{2,1,0:T(8,128)S(1)} %get-tuple-element.71.refs_0_), channel_id=1, source_target_pairs={{0,2},{1,3},{2,0},{3,1},{4,6},{5,7},{6,4},{7,5},{8,10},{9,11},{10,... | collective-permute-start | bytes 172040 | tf_op jit(solution)/shard_map/ppermute | solution.py:403
  32.5 0.8 %shard_map.39.refs_4_ = f32[4,16,32,128]{3,2,1,0:T(8,128)S(1)} custom-call(f32[4,32,16,128]{3,2,1,0:T(8,128)S(1)} %get-tuple-element.74.solved, f32[2,32,16,128]{3,2,1,0:T(8,128)S(1)} %get-tuple-element.75.ivy, f32[2,32,16,128]{3,2,1,0:T(8,128)S(1)} %get-tuple-element.76.ry), custom_call_target="tpu_custom_call" | custom-call | flops 1000 | bytes 1000 | tf_op jit(solution)/shard_map/pallas_call | solution.py:21
  33.3 1.9 %collective-permute-done.9.refs_1_ = f32[7,16,128]{2,1,0:T(8,128)S(1)} collective-permute-done((f32[7,16,128]{2,1,0:T(8,128)S(1)}, f32[7,16,128]{2,1,0:T(8,128)S(1)}, u32[]{:S(2)}, u32[]{:S(2)}) %collective-permute-start.9) | collective-permute-done | bytes 57376 | tf_op jit(solution)/shard_map/ppermute | solution.py:403
  35.2 1.1 %shard_map.40 = f32[4,16,32,128]{3,2,1,0:T(8,128)} custom-call(f32[7,16,128]{2,1,0:T(8,128)S(1)} %get-tuple-element.71.refs_0_, f32[7,16,128]{2,1,0:T(8,128)S(1)} %collective-permute-done.9.refs_1_, f32[4,16,128]{2,1,0:T(8,128)S(1)} %get-tuple-element.72.refs_2_, f32[6,16,128]{2,1,0:T(8,128)S(1)} %get-tuple-element.73.refs_3_, ...), custom_call_target="tpu_custom_call" | custom-call | flops 1000 | bytes 1000 | tf_op jit(solution)/shard_map/pallas_call | solution.py:21
  (13 shorter events, 0.2 us)
Async XLA Ops:
  0.0 6.0 %copy-start = (f32[4,16,32,128]{3,2,1,0:T(8,128)S(1)}, f32[4,16,32,128]{3,2,1,0:T(8,128)}, u32[]{:S(2)}) copy-start(f32[4,16,32,128]{3,2,1,0:T(8,128)} %flow.3) | copy-start | bytes 3145732
  1.4 7.2 %collective-permute-start.3 = (f32[8,32,128]{2,1,0:T(8,128)S(1)}, f32[8,32,128]{2,1,0:T(8,128)S(1)}, u32[]{:S(2)}, u32[]{:S(2)}) collective-permute-start(f32[8,32,128]{2,1,0:T(8,128)S(1)} %get-tuple-element.48.mine.coef_mine), channel_id=1, source_target_pairs={{0,4},{4,0},{8,12},{12,8},{16,20},{20,16},{24,28},{28,24},{1,5},{5... | collective-permute-start | bytes 393224 | tf_op jit(solution)/shard_map/ppermute | solution.py:403
  4.4 4.0 %collective-permute-start = (f32[4,32,128]{2,1,0:T(8,128)S(1)}, f32[4,32,128]{2,1,0:T(8,128)S(1)}, u32[]{:S(2)}, u32[]{:S(2)}) collective-permute-start(f32[4,32,128]{2,1,0:T(8,128)S(1)} %get-tuple-element.45.x_edge), channel_id=1, source_target_pairs={{0,1},{1,0},{2,3},{3,2},{4,8},{5,9},{6,10},{7,11},{8,4},{9,5},{10,... | collective-permute-start | bytes 196616 | tf_op jit(solution)/shard_map/ppermute | solution.py:427
  4.4 2.5 %collective-permute-start.1 = (f32[4,16,128]{2,1,0:T(8,128)S(1)}, f32[4,16,128]{2,1,0:T(8,128)S(1)}, u32[]{:S(2)}, u32[]{:S(2)}) collective-permute-start(f32[4,16,128]{2,1,0:T(8,128)S(1)} %get-tuple-element.46.y_edge_even), channel_id=1, source_target_pairs={{0,1},{1,0},{2,3},{3,2},{4,5},{5,4},{6,7},{7,6},{8,9},{9,8},{10,11... | collective-permute-start | bytes 98312 | tf_op jit(solution)/shard_map/ppermute | solution.py:403
  4.9 3.5 %collective-permute-start.2 = (f32[4,16,128]{2,1,0:T(8,128)S(1)}, f32[4,16,128]{2,1,0:T(8,128)S(1)}, u32[]{:S(2)}, u32[]{:S(2)}) collective-permute-start(f32[4,16,128]{2,1,0:T(8,128)S(1)} %get-tuple-element.47.y_edge_odd), channel_id=1, source_target_pairs={{0,3},{1,2},{2,1},{3,0},{4,7},{5,6},{6,5},{7,4},{8,11},{9,10},{10,... | collective-permute-start | bytes 98312 | tf_op jit(solution)/shard_map/ppermute | solution.py:428
  8.7 7.9 %collective-permute-start.4 = (f32[12,32,128]{2,1,0:T(8,128)S(1)}, f32[12,32,128]{2,1,0:T(8,128)S(1)}, u32[]{:S(2)}, u32[]{:S(2)}) collective-permute-start(f32[12,32,128]{2,1,0:T(8,128)S(1)} %get-tuple-element.49.after.mine), channel_id=1, source_target_pairs={{0,4},{4,0},{8,12},{12,8},{16,20},{20,16},{24,28},{28,24},{1,5},{5... | collective-permute-start | bytes 589832 | tf_op jit(solution)/shard_map/ppermute | solution.py:403
  11.2 7.0 %collective-permute-start.6 = (f32[8,32,128]{2,1,0:T(8,128)S(1)}, f32[8,32,128]{2,1,0:T(8,128)S(1)}, u32[]{:S(2)}, u32[]{:S(2)}) collective-permute-start(f32[8,32,128]{2,1,0:T(8,128)S(1)} %get-tuple-element.51.near.mine.coef_mine), channel_id=1, source_target_pairs={{0,8},{4,12},{8,0},{12,4},{16,24},{20,28},{24,16},{28,20},{1,9},{5... | collective-permute-start | bytes 393224 | tf_op jit(solution)/shard_map/ppermute | solution.py:403
  16.6 5.2 %collective-permute-start.5 = (f32[8,32,128]{2,1,0:T(8,128)S(1)}, f32[8,32,128]{2,1,0:T(8,128)S(1)}, u32[]{:S(2)}, u32[]{:S(2)}) collective-permute-start(f32[8,32,128]{2,1,0:T(8,128)S(1)} %get-tuple-element.52.after.mine), channel_id=1, source_target_pairs={{0,8},{4,12},{8,0},{12,4},{16,24},{20,28},{24,16},{28,20},{1,9},{5... | collective-permute-start | bytes 393224 | tf_op jit(solution)/shard_map/ppermute | solution.py:403
  21.8 2.5 %copy-start.1 = (f32[16,32,128]{2,1,0:T(8,128)S(1)}, f32[16,32,128]{2,1,0:T(8,128)}, u32[]{:S(2)}) copy-start(f32[16,32,128]{2,1,0:T(8,128)} %visc.3) | copy-start | bytes 786436
  21.9 7.3 %collective-permute-start.7 = (f32[7,32,128]{2,1,0:T(8,128)S(1)}, f32[7,32,128]{2,1,0:T(8,128)S(1)}, u32[]{:S(2)}, u32[]{:S(2)}) collective-permute-start(f32[7,32,128]{2,1,0:T(8,128)S(1)} %get-tuple-element.55.refs_0_), channel_id=1, source_target_pairs={{0,16},{4,20},{8,24},{12,28},{16,0},{20,4},{24,8},{28,12},{1,17},{... | collective-permute-start | bytes 344072 | tf_op jit(solution)/shard_map/ppermute | solution.py:403
  29.5 1.4 %collective-permute-start.8 = (f32[16,16,128]{2,1,0:T(8,128)S(1)}, f32[16,16,128]{2,1,0:T(8,128)S(1)}, u32[]{:S(2)}, u32[]{:S(2)}) collective-permute-start(f32[16,16,128]{2,1,0:T(8,128)S(1)} %get-tuple-element.70.mine), channel_id=1, source_target_pairs={{0,1},{1,0},{2,3},{3,2},{4,5},{5,4},{6,7},{7,6},{8,9},{9,8},{10,11... | collective-permute-start | bytes 393224 | tf_op jit(solution)/shard_map/ppermute | solution.py:403
  30.9 4.2 %collective-permute-start.9 = (f32[7,16,128]{2,1,0:T(8,128)S(1)}, f32[7,16,128]{2,1,0:T(8,128)S(1)}, u32[]{:S(2)}, u32[]{:S(2)}) collective-permute-start(f32[7,16,128]{2,1,0:T(8,128)S(1)} %get-tuple-element.71.refs_0_), channel_id=1, source_target_pairs={{0,2},{1,3},{2,0},{3,1},{4,6},{5,7},{6,4},{7,5},{8,10},{9,11},{10,... | collective-permute-start | bytes 172040 | tf_op jit(solution)/shard_map/ppermute | solution.py:403

commit v5 on v4

--- a/solution.py
+++ b/solution.py
@@ -12,6 +12,7 @@
 CONDUCT = 0.6
 GROUPS = (0, 0, 0, 1)
 SCALES = (1.0, CONDUCT)
+EARLY = 3
 VMEM = pl.BlockSpec(memory_space=pltpu.VMEM)
 HBM = pl.BlockSpec(memory_space=pltpu.HBM)
 F32 = jnp.float32
@@ -77,29 +78,35 @@
         out[4 + group] = right[group, count - 1]
 
 
-def first_kernel(flow, visc, x_odd, y_even, y_odd, ivx, rx, cx, wx, coef_x, cells, sems):
+def pack_kernel(flow, visc, x_even, x_odd, y_even, y_odd, cells, sems):
     nx, ny = flow.shape[1], flow.shape[2]
-    ix, iy = lax.axis_index("gx"), lax.axis_index("gy")
-    x_par, y_par = lax.rem(ix, 2), lax.rem(iy, 2)
+    x_par = lax.rem(lax.axis_index("gx"), 2)
+    y_par = lax.rem(lax.axis_index("gy"), 2)
     copies = (
-        (visc, cells),
         (flow.at[:, x_par * (nx - 1)], x_odd),
         (flow.at[:, :, (1 - y_par) * (ny - 1)], y_even),
         (flow.at[:, :, y_par * (ny - 1)], y_odd),
+        (flow.at[:, (1 - x_par) * (nx - 1)], x_even),
+        (visc, cells),
     )
     started = [pltpu.make_async_copy(a, b, sems.at[i]) for i, (a, b) in enumerate(copies)]
     for copy in started:
         copy.start()
-    started[0].wait()
-    factor_line(lambda i: cells[i], nx, ix == 0, ix == lax.axis_size("gx") - 1, ivx, rx, cx, wx)
+    for copy in started:
+        copy.wait()
+
+
+def factor_x_kernel(visc, x_even, after, ivx, rx, cx, wx, coef_x):
+    nx = visc.shape[0]
+    ix = lax.axis_index("gx")
+    factor_line(lambda i: visc[i], nx, ix == 0, ix == lax.axis_size("gx") - 1, ivx, rx, cx, wx)
     coef_rows(cx, wx, coef_x, nx)
-    coef_x[6] = cells[0]
-    coef_x[7] = cells[nx - 1]
-    for copy in started[1:]:
-        copy.wait()
-
-
-def factor_y_kernel(visc, ivy, ry, cy, wy, coef_y, cy_t, wy_t):
+    coef_x[6] = visc[0]
+    coef_x[7] = visc[nx - 1]
+    coef_x[pl.ds(8, EARLY)] = x_even[pl.ds(0, EARLY)]
+
+
+def factor_y_kernel(visc, ivy, ry, cy, wy, coef_y):
     nx, ny, nz = visc.shape
     iy = lax.axis_index("gy")
     rows = visc.reshape(nx * ny, nz)
@@ -111,16 +118,10 @@
     coef_rows(cy, wy, coef_y, ny)
     coef_y[6] = row_y(0)
     coef_y[7] = row_y(ny - 1)
-    for part, turned in ((cy, cy_t), (wy, wy_t)):
-        for group in range(2):
-            out = turned.at[group].reshape(nx * ny, nz)
-            for j in range(ny):
-                out[pl.ds(j, nx, stride=ny), :] = part[group, j]
 
 
 def source_kernel(flow, cx, wx, source, message):
     _, nx, ny, nz = flow.shape
-    x_par = lax.rem(lax.axis_index("gx"), 2) == 0
     row = lax.broadcasted_iota(jnp.int32, (ny, nz), 0)
     left = [None] * 4
     right = [None] * 4
@@ -149,20 +150,19 @@
     for c in range(4):
         message[c] = left[c]
         message[4 + c] = right[c]
-        message[8 + c] = pick(x_par, flow[c, nx - 1], flow[c, 0])
-
-
-def edge_kernel(partial, x_edge, y_edge_even, y_edge_odd, x_odd, y_even, y_odd, cx, wx, after, message, gap_x, gap_y):
+
+
+def edge_kernel(partial, x_edge_even, x_edge, y_edge_even, y_edge_odd, x_odd, y_even, y_odd, cx, wx, message, gap_x, gap_y):
     _, nx, ny, nz = cx.shape
     ix, iy = lax.axis_index("gx"), lax.axis_index("gy")
     x_par, y_par = lax.rem(ix, 2) == 0, lax.rem(iy, 2) == 0
     x_none = (ix == 0) | (ix == lax.axis_size("gx") - 1)
     y_first, y_last = iy == 0, iy == lax.axis_size("gy") - 1
     half = 0.5 * ADVECT
-    message[pl.ds(8, 4)] = partial[pl.ds(8, 4)]
     own_low = half * pick(y_par, y_edge_odd[1], y_edge_even[1])
     own_high = half * pick(y_par, y_edge_even[1], y_edge_odd[1])
     own_x = half * x_edge[0]
+    message[pl.ds(8, 4 - EARLY)] = x_edge_even[pl.ds(EARLY, 4 - EARLY)]
     for c in range(4):
         group = GROUPS[c]
         low = own_low * pick(y_par, y_odd[c], y_even[c])
@@ -229,8 +229,10 @@
         a_r, b_r = sides(mine[4 + c], theirs[4 + c])
         if edged is not None:
             coef_mine, coef_theirs, missing = edged
-            here = (ADVECT * 0.5) * mine[8] * theirs[8 + c]
-            there = (ADVECT * 0.5) * theirs[8] * mine[8 + c]
+            k = 8 + c if c < EARLY else 8 + c - EARLY
+            facing_mine, facing_theirs = (coef_mine, coef_theirs) if c < EARLY else (mine, theirs)
+            here = (ADVECT * 0.5) * coef_mine[8] * facing_theirs[k]
+            there = (ADVECT * 0.5) * coef_theirs[8] * facing_mine[k]
             missing[c] = here
             a_gap, b_gap = sides(here, there)
             ll = pick(is_left, coef_theirs[group], coef_mine[group])
@@ -253,15 +255,28 @@
 
 def coef_kernel(axis, bit, last, mine, theirs, after, union, weights):
     coef_part(axis, bit, last, mine, theirs, 0, union, 0, weights)
-
-
-def x_merge_kernel(axis, bit, last, edged, mine, theirs, weights, coef_mine, coef_theirs, near, union, saved, missing=None):
+    if last:
+        union[3] = union[2]
+
+
+def x_merge_kernel(axis, bit, last, edged, mine, theirs, weights, coef_mine, coef_theirs, union, saved, missing=None):
     row_part(
         axis, bit, last, mine, theirs, weights, union, saved,
         (coef_mine, coef_theirs, missing) if edged else None,
     )
-    if last:
-        union[pl.ds(4, 3)] = near[...]
+
+
+def last_weight(mine, theirs, at):
+    face = 0.5 * (mine[at + 2] + theirs[at + 2])
+    return [
+        1.0 / (1.0 / (scale * face) + mine[at + group] + theirs[at + group])
+        for group, scale in enumerate(SCALES)
+    ]
+
+
+def last_coef_kernel(mine, theirs, weight):
+    for group, value in enumerate(last_weight(mine, theirs, 0)):
+        weight[group] = value
 
 
 def y_merge_kernel(axis, bit, last, mine, theirs, union, saved, weights):
@@ -269,16 +284,11 @@
     row_part(axis, bit, last, mine, theirs, weights, union, saved)
 
 
-def fluxes(axis, mine, theirs, saved, missing=None):
+def fluxes(axis, mine, theirs, weight, saved, missing=None):
     index = lax.axis_index(axis)
     bit = lax.axis_size(axis) // 2
     is_left = (index & bit) == 0
     result = []
-    face = 0.5 * (mine[6] + theirs[6])
-    weight = [
-        1.0 / (1.0 / (scale * face) + mine[4 + group] + theirs[4 + group])
-        for group, scale in enumerate(SCALES)
-    ]
     for c in range(4):
         group = GROUPS[c]
         d = theirs[c] - mine[c]
@@ -298,7 +308,7 @@
     return result
 
 
-def local_kernel(source, gap_x, gap_y, ivx, rx, cx, wx, local_t, cx_t, wx_t, scratch):
+def local_kernel(source, gap_x, gap_y, ivx, rx, cx, wx, after, local_t, cx_t, wx_t, scratch):
     _, nx, ny, nz = source.shape
     x_par = lax.rem(lax.axis_index("gx"), 2) == 0
     row = lax.broadcasted_iota(jnp.int32, (ny, nz), 0)
@@ -336,12 +346,12 @@
 
 
 def y_start_kernel(stages, *refs):
-    mine, theirs, missing = refs[:3]
-    parts = refs[3 : 3 + 2 * stages]
-    local_t, cx_t, wx_t, cy, wy, coef_y, solved, message, flux_low, flux_high = refs[3 + 2 * stages :]
+    mine, theirs, weight, missing = refs[:4]
+    parts = refs[4 : 4 + 2 * stages]
+    local_t, cx_t, wx_t, cy, wy, coef_y, solved, message, flux_low, flux_high = refs[4 + 2 * stages :]
     _, ny, nx, nz = local_t.shape
     saved = list(zip(parts[::2], parts[1::2]))
-    for c, (low, high) in enumerate(fluxes("gx", mine, theirs, saved, missing)):
+    for c, (low, high) in enumerate(fluxes("gx", mine, theirs, weight, saved, missing)):
         flux_low[c] = low
         flux_high[c] = high
     for c in range(4):
@@ -360,8 +370,13 @@
     message[pl.ds(8, 8)] = coef_y[...]
 
 
-def y_local_kernel(solved, ivy, ry, local):
+def y_local_kernel(solved, ivy, ry, cy, wy, local, cy_t, wy_t):
     _, ny, nx, nz = solved.shape
+    for part, turned in ((cy, cy_t), (wy, wy_t)):
+        for group in range(2):
+            out = turned.at[group].reshape(nx * ny, nz)
+            for j in range(ny):
+                out[pl.ds(j, nx, stride=ny), :] = part[group, j]
     for c in range(4):
         group = GROUPS[c]
         rows = local.at[c].reshape(nx * ny, nz)
@@ -383,7 +398,7 @@
     local, cy_t, wy_t, out, buffer, flux_low, flux_high, sems = refs[2 + 2 * stages :]
     saved = list(zip(parts[::2], parts[1::2]))
     nx = local.shape[1]
-    for c, (low, high) in enumerate(fluxes("gy", mine, theirs, saved)):
+    for c, (low, high) in enumerate(fluxes("gy", mine, theirs, last_weight(mine, theirs, 4), saved)):
         flux_low[c] = low
         flux_high[c] = high
     copies = []
@@ -411,11 +426,12 @@
     fields, nx, ny, nz = flow.shape
     mx, my = lax.axis_size("gx"), lax.axis_size("gy")
     along_x, along_y = (2, nx, ny, nz), (2, ny, nx, nz)
-    x_edge, y_edge_even, y_edge_odd, ivx, rx, cx, wx, coef_x = call(
-        first_kernel,
+    along_x, along_y = (2, nx, ny, nz), (2, ny, nx, nz)
+    x_edge_even, x_edge, y_edge_even, y_edge_odd, cells = call(
+        pack_kernel,
         tuple(pltpu.with_memory_space_constraint(array, pltpu.HBM) for array in (flow, visc)),
-        [(fields, ny, nz), (fields, nx, nz), (fields, nx, nz)] + [along_x] * 4 + [(8, ny, nz)],
-        scratch=[pltpu.VMEM((nx, ny, nz), F32), pltpu.SemaphoreType.DMA((4,))],
+        [(fields, ny, nz)] * 2 + [(fields, nx, nz)] * 2 + [(nx, ny, nz)],
+        scratch=[pltpu.SemaphoreType.DMA((5,))],
         in_specs=[HBM, HBM],
     )
     pairs = []
@@ -429,22 +445,26 @@
         y_edge_odd, "gy", [(i, (i - 1 ^ 1) + 1) if 0 < i < my - 1 else (i, my - 1 - i) for i in range(my)]
     )
     y_even = swap(y_edge_even, "gy", 1)
-
-    ivy, ry, cy, wy, coef_y, cy_t, wy_t = call(
-        factor_y_kernel, (visc,), [along_y] * 4 + [(8, nx, nz)] + [along_x] * 2
-    )
+    ivx, rx, cx, wx, coef_x = call(
+        factor_x_kernel,
+        (cells, x_edge_even, y_even),
+        [along_x] * 4 + [(8 + EARLY, ny, nz)],
+        in_specs=after_all(2),
+    )
+
+    ivy, ry, cy, wy, coef_y = call(factor_y_kernel, (cells,), [along_y] * 4 + [(8, nx, nz)])
     coef_x_theirs = swap(coef_x, "gx", 1)
-    source, partial = call(source_kernel, (flow, cx, wx), [(fields, nx, ny, nz), (12, ny, nz)])
+    source, partial = call(source_kernel, (flow, cx, wx), [(fields, nx, ny, nz), (8, ny, nz)])
     message, gap_x, gap_y = call(
         edge_kernel,
-        (partial, x_edge, y_edge_even, y_edge_odd, x_odd, y_even, y_odd, cx, wx, coef_x_theirs),
-        [(12, ny, nz), (fields, ny, nz), (2 * fields, nx, nz)],
-        in_specs=after_all(9),
+        (partial, x_edge_even, x_edge, y_edge_even, y_edge_odd, x_odd, y_even, y_odd, cx, wx),
+        [(12 - EARLY, ny, nz), (fields, ny, nz), (2 * fields, nx, nz)],
     )
     local_t, cx_t, wx_t = call(
         local_kernel,
-        (source, gap_x, gap_y, ivx, rx, cx, wx),
-        [(fields, ny, nx, nz), along_y, along_y],
+        (source, gap_x, gap_y, ivx, rx, cx, wx, ivy),
+        in_specs=after_all(7),
+        outs=[(fields, ny, nx, nz), along_y, along_y],
         scratch=[pltpu.VMEM((fields, nx * ny, nz), F32)],
         cost=1000,
     )
@@ -458,15 +478,15 @@
         rows_theirs = swap(rows, "gx", bit)
         merged, weights = call(
             functools.partial(coef_kernel, "gx", bit, last),
-            (coefs, coefs_theirs, rows),
-            [(3 if last else 8,) + shape, (6,) + shape],
+            (coefs, coefs_theirs, local_t if bit == 1 else rows),
+            [(4 if last else 8,) + shape, (6,) + shape],
             in_specs=after_all(2),
         )
-        merged_theirs = merged if last else swap(merged, "gx", 2 * bit)
+        merged_theirs = swap(merged, "gx", 2 * bit)
         rows, part, *gap = call(
             functools.partial(x_merge_kernel, "gx", bit, last, bit == 1),
-            (rows, rows_theirs, weights, coefs, coefs_theirs, merged),
-            [(7 if last else 8,) + shape, (4,) + shape] + [(4,) + shape] * (bit == 1),
+            (rows, rows_theirs, weights, coefs, coefs_theirs),
+            [(4 if last else 8,) + shape, (4,) + shape] + [(4,) + shape] * (bit == 1),
         )
         if gap:
             missing = gap[0]
@@ -475,13 +495,16 @@
         bit *= 2
     rows_theirs = swap(rows, "gx", bit)
 
+    (weight,) = call(last_coef_kernel, (coefs, coefs_theirs), [(2, ny, nz)])
     solved, rows = call(
         functools.partial(y_start_kernel, len(saved) // 2),
-        (rows, rows_theirs, missing, *saved, local_t, cx_t, wx_t, cy, wy, coef_y),
+        (rows, rows_theirs, weight, missing, *saved, local_t, cx_t, wx_t, cy, wy, coef_y),
         [(fields, ny, nx, nz), (16, nx, nz)],
         scratch=[pltpu.VMEM((fields, ny, nz), F32)] * 2,
     )
-    (local_y,) = call(y_local_kernel, (solved, ivy, ry), [(fields, nx, ny, nz)])
+    local_y, cy_t, wy_t = call(
+        y_local_kernel, (solved, ivy, ry, cy, wy), [(fields, nx, ny, nz), along_x, along_x]
+    )
     saved = []
     shape = (nx, nz)
     bit = 1

time: 36.4 us -> 34.2 us (0.940)
  waiting for transfers between devices: 14.1 us -> 8.42 us
  starting transfers between devices: 14.6 us -> 17.8 us
    ppermute x8 -> x9, waiting for transfers between devices: 12.6 us -> 8.41 us  [swap(): lax.ppermute(array, axis, [(i, i ^ bit) for i in range(lax.axis_size(axis...]
    ppermute x8 -> x9, starting transfers between devices: 13.5 us -> 15.1 us  [swap(): lax.ppermute(array, axis, [(i, i ^ bit) for i in range(lax.axis_size(axis...]
    ppermute x1, starting transfers between devices: 1.13 us -> 2.63 us  [per_device(): lax.ppermute(y_edge_odd, 'gy', [(i, (i - 1 ^ 1) + 1) if 0 < i < my - 1 el...]
    ppermute x1, waiting for transfers between devices: 1.5 us -> 0.01 us  [per_device(): lax.ppermute(y_edge_odd, 'gy', [(i, (i - 1 ^ 1) + 1) if 0 < i < my - 1 el...]
    pallas_call x13 -> x15, Pallas kernels: 7.51 us -> 7.72 us  [call(): pl.pallas_call(kernel, out_shape=[jax.ShapeDtypeStruct(shape, F32) for sh...]
  transfers between devices with their start and end apart: 10 -> 11, of which waited for: 7 -> 7; matrix products, arithmetic and copies ran while one was open for 0% -> 0% of each run, Pallas kernels for 13% -> 15%
where the time goes in v5:
time: 34.2 us; the launch traced here: 34.1 us
  starting transfers between devices  17.8 us (52%)
  waiting for transfers between devices  8.42 us (25%)
  Pallas kernels  7.72 us (23%)
    ppermute x9, starting transfers between devices, swap(): lax.ppermute(array, axis, [(i, i ^ bit) for i in range(lax.axis_size(axis...  15.1 us
    ppermute x9, waiting for transfers between devices, swap(): lax.ppermute(array, axis, [(i, i ^ bit) for i in range(lax.axis_size(axis...  8.41 us
    pallas_call x15, Pallas kernels, call(): pl.pallas_call(kernel, out_shape=[jax.ShapeDtypeStruct(shape, F32) for sh...  7.72 us
    ppermute x1, starting transfers between devices, per_device(): lax.ppermute(y_edge_odd, 'gy', [(i, (i - 1 ^ 1) + 1) if 0 < i < my - 1 el...  2.63 us
  transfers between devices with their start and end apart: 11, of which 7 were waited for; matrix products, arithmetic and copies ran while one was open for 0% of the time, Pallas kernels for 15%

profile of v5, /device:TPU:0, one launch (start us, length us, event | category | flops | bytes accessed | tf_op | source)
XLA Modules:
  0.0 34.1 jit_solution(5199009765552990075)
XLA Ops:
  0.0 1.2 %shard_map.28 = (f32[4,32,128]{2,1,0:T(8,128)S(1)}, f32[4,32,128]{2,1,0:T(8,128)S(1)}, f32[4,16,128]{2,1,0:T(8,128)S(1)}, f32[4,16,128]{2,1,0:T(8,128)S(1)}, f32[16,32,128]{2,1,0:T(8,128)S(1)}) custom-call(f32[4,16,32,128]{3,2,1,0:T(8,128)} %flow.3, f32[16,32,128]{2,1,0:T(8,128)} %visc.1), custom_call_target="tpu_custom_call" | custom-call | flops 1000 | bytes 1000 | tf_op jit(solution)/shard_map/pallas_call | solution.py:22
  1.2 0.5 %collective-permute-start = (f32[4,16,128]{2,1,0:T(8,128)S(1)}, f32[4,16,128]{2,1,0:T(8,128)S(1)}, u32[]{:S(2)}, u32[]{:S(2)}) collective-permute-start(f32[4,16,128]{2,1,0:T(8,128)S(1)} %get-tuple-element.47.y_edge_even), channel_id=1, source_target_pairs={{0,1},{1,0},{2,3},{3,2},{4,5},{5,4},{6,7},{7,6},{8,9},{9,8},{10,11... | collective-permute-start | bytes 98312 | tf_op jit(solution)/shard_map/ppermute | solution.py:418
  1.8 2.6 %collective-permute-start.2 = (f32[4,16,128]{2,1,0:T(8,128)S(1)}, f32[4,16,128]{2,1,0:T(8,128)S(1)}, u32[]{:S(2)}, u32[]{:S(2)}) collective-permute-start(f32[4,16,128]{2,1,0:T(8,128)S(1)} %get-tuple-element.52.y_edge_odd), channel_id=1, source_target_pairs={{0,3},{1,2},{2,1},{3,0},{4,7},{5,6},{6,5},{7,4},{8,11},{9,10},{10,... | collective-permute-start | bytes 98312 | tf_op jit(solution)/shard_map/ppermute | solution.py:444
  4.4 0.3 shard_map.29
  4.7 2.8 %collective-permute-start.4 = (f32[11,32,128]{2,1,0:T(8,128)S(1)}, f32[11,32,128]{2,1,0:T(8,128)S(1)}, u32[]{:S(2)}, u32[]{:S(2)}) collective-permute-start(f32[11,32,128]{2,1,0:T(8,128)S(1)} %get-tuple-element.54.mine.coef_mine), channel_id=1, source_target_pairs={{0,4},{4,0},{8,12},{12,8},{16,20},{20,16},{24,28},{28,24},{1,5},{5... | collective-permute-start | bytes 540680 | tf_op jit(solution)/shard_map/ppermute | solution.py:418
  7.5 0.9 %shard_map.30 = (f32[4,16,32,128]{3,2,1,0:T(8,128)S(1)}, f32[8,32,128]{2,1,0:T(8,128)S(1)}) custom-call(f32[4,16,32,128]{3,2,1,0:T(8,128)S(1)} %copy-done, f32[2,16,32,128]{3,2,1,0:T(8,128)S(1)} %get-tuple-element.48.cx, f32[2,16,32,128]{3,2,1,0:T(8,128)S(1)} %get-tuple-element.49.wx), custom_call_target="tpu_custom_call" | custom-call | flops 1000 | bytes 1000 | tf_op jit(solution)/shard_map/pallas_call | solution.py:22
  8.5 1.3 %collective-permute-start.3 = (f32[9,32,128]{2,1,0:T(8,128)S(1)}, f32[9,32,128]{2,1,0:T(8,128)S(1)}, u32[]{:S(2)}, u32[]{:S(2)}) collective-permute-start(f32[9,32,128]{2,1,0:T(8,128)S(1)} %get-tuple-element.53.mine), channel_id=1, source_target_pairs={{0,4},{4,0},{8,12},{12,8},{16,20},{20,16},{24,28},{28,24},{1,5},{5... | collective-permute-start | bytes 442376 | tf_op jit(solution)/shard_map/ppermute | solution.py:418
  9.8 0.5 %shard_map.32 = (f32[2,32,16,128]{3,2,1,0:T(8,128)S(1)}, f32[2,32,16,128]{3,2,1,0:T(8,128)S(1)}, f32[2,32,16,128]{3,2,1,0:T(8,128)S(1)}, f32[2,32,16,128]{3,2,1,0:T(8,128)S(1)}, f32[8,16,128]{2,1,0:T(8,128)S(1)}) custom-call(f32[16,32,128]{2,1,0:T(8,128)S(1)} %get-tuple-element.45.visc), custom_call_target="tpu_custom_call" | custom-call | flops 1000 | bytes 1000 | tf_op jit(solution)/shard_map/pallas_call | solution.py:22
  10.3 1.5 %shard_map.33 = (f32[4,32,16,128]{3,2,1,0:T(8,128)S(1)}, f32[2,32,16,128]{3,2,1,0:T(8,128)S(1)}, f32[2,32,16,128]{3,2,1,0:T(8,128)S(1)}) custom-call(f32[4,16,32,128]{3,2,1,0:T(8,128)S(1)} %get-tuple-element.55.source, f32[4,32,128]{2,1,0:T(8,128)S(1)} %get-tuple-element.56.gap_x, f32[8,16,128]{2,1,0:T(8,128)S(1)} %get-tuple-element.57.gap_y, ...), custom_call_target="tpu_custom_call" | custom-call | flops 1000 | bytes 1000 | tf_op jit(solution)/shard_map/pallas_call | solution.py:22
  11.8 1.1 %collective-permute-done.4.theirs.coef_theirs = f32[11,32,128]{2,1,0:T(8,128)S(1)} collective-permute-done((f32[11,32,128]{2,1,0:T(8,128)S(1)}, f32[11,32,128]{2,1,0:T(8,128)S(1)}, u32[]{:S(2)}, u32[]{:S(2)}) %collective-permute-start.4) | collective-permute-done | bytes 180256 | tf_op jit(solution)/shard_map/ppermute | solution.py:418
  12.9 1.9 %collective-permute-start.6 = (f32[8,32,128]{2,1,0:T(8,128)S(1)}, f32[8,32,128]{2,1,0:T(8,128)S(1)}, u32[]{:S(2)}, u32[]{:S(2)}) collective-permute-start(f32[8,32,128]{2,1,0:T(8,128)S(1)} %get-tuple-element.64.mine.coef_mine), channel_id=1, source_target_pairs={{0,8},{4,12},{8,0},{12,4},{16,24},{20,28},{24,16},{28,20},{1,9},{5... | collective-permute-start | bytes 393224 | tf_op jit(solution)/shard_map/ppermute | solution.py:418
  14.9 0.8 %collective-permute-done.3.theirs = f32[9,32,128]{2,1,0:T(8,128)S(1)} collective-permute-done((f32[9,32,128]{2,1,0:T(8,128)S(1)}, f32[9,32,128]{2,1,0:T(8,128)S(1)}, u32[]{:S(2)}, u32[]{:S(2)}) %collective-permute-start.3) | collective-permute-done | bytes 147488 | tf_op jit(solution)/shard_map/ppermute | solution.py:418
  15.8 1.7 %collective-permute-start.5 = (f32[8,32,128]{2,1,0:T(8,128)S(1)}, f32[8,32,128]{2,1,0:T(8,128)S(1)}, u32[]{:S(2)}, u32[]{:S(2)}) collective-permute-start(f32[8,32,128]{2,1,0:T(8,128)S(1)} %get-tuple-element.63.after.mine), channel_id=1, source_target_pairs={{0,8},{4,12},{8,0},{12,4},{16,24},{20,28},{24,16},{28,20},{1,9},{5... | collective-permute-start | bytes 393224 | tf_op jit(solution)/shard_map/ppermute | solution.py:418
  17.5 0.5 %collective-permute-done.6.theirs.coef_theirs = f32[8,32,128]{2,1,0:T(8,128)S(1)} collective-permute-done((f32[8,32,128]{2,1,0:T(8,128)S(1)}, f32[8,32,128]{2,1,0:T(8,128)S(1)}, u32[]{:S(2)}, u32[]{:S(2)}) %collective-permute-start.6) | collective-permute-done | bytes 131104 | tf_op jit(solution)/shard_map/ppermute | solution.py:418
  18.0 3.1 %collective-permute-start.8 = (f32[4,32,128]{2,1,0:T(8,128)S(1)}, f32[4,32,128]{2,1,0:T(8,128)S(1)}, u32[]{:S(2)}, u32[]{:S(2)}) collective-permute-start(f32[4,32,128]{2,1,0:T(8,128)S(1)} %get-tuple-element.67.mine), channel_id=1, source_target_pairs={{0,16},{4,20},{8,24},{12,28},{16,0},{20,4},{24,8},{28,12},{1,17},{... | collective-permute-start | bytes 196616 | tf_op jit(solution)/shard_map/ppermute | solution.py:418
  21.1 0.6 %collective-permute-done.5.theirs = f32[8,32,128]{2,1,0:T(8,128)S(1)} collective-permute-done((f32[8,32,128]{2,1,0:T(8,128)S(1)}, f32[8,32,128]{2,1,0:T(8,128)S(1)}, u32[]{:S(2)}, u32[]{:S(2)}) %collective-permute-start.5) | collective-permute-done | bytes 131104 | tf_op jit(solution)/shard_map/ppermute | solution.py:418
  21.8 2.7 %collective-permute-start.7 = (f32[4,32,128]{2,1,0:T(8,128)S(1)}, f32[4,32,128]{2,1,0:T(8,128)S(1)}, u32[]{:S(2)}, u32[]{:S(2)}) collective-permute-start(f32[4,32,128]{2,1,0:T(8,128)S(1)} %get-tuple-element.66.refs_0_), channel_id=1, source_target_pairs={{0,16},{4,20},{8,24},{12,28},{16,0},{20,4},{24,8},{28,12},{1,17},{... | collective-permute-start | bytes 196616 | tf_op jit(solution)/shard_map/ppermute | solution.py:418
  24.5 2.5 %collective-permute-done.7.refs_1_ = f32[4,32,128]{2,1,0:T(8,128)S(1)} collective-permute-done((f32[4,32,128]{2,1,0:T(8,128)S(1)}, f32[4,32,128]{2,1,0:T(8,128)S(1)}, u32[]{:S(2)}, u32[]{:S(2)}) %collective-permute-start.7) | collective-permute-done | bytes 65568 | tf_op jit(solution)/shard_map/ppermute | solution.py:418
  27.0 0.3 shard_map.39
  27.4 1.3 %collective-permute-done.9.theirs = f32[16,16,128]{2,1,0:T(8,128)S(1)} collective-permute-done((f32[16,16,128]{2,1,0:T(8,128)S(1)}, f32[16,16,128]{2,1,0:T(8,128)S(1)}, u32[]{:S(2)}, u32[]{:S(2)}) %collective-permute-start.9) | collective-permute-done | bytes 131104 | tf_op jit(solution)/shard_map/ppermute | solution.py:418
  28.8 1.0 %collective-permute-start.10 = (f32[7,16,128]{2,1,0:T(8,128)S(1)}, f32[7,16,128]{2,1,0:T(8,128)S(1)}, u32[]{:S(2)}, u32[]{:S(2)}) collective-permute-start(f32[7,16,128]{2,1,0:T(8,128)S(1)} %get-tuple-element.77.refs_0_), channel_id=1, source_target_pairs={{0,2},{1,3},{2,0},{3,1},{4,6},{5,7},{6,4},{7,5},{8,10},{9,11},{10,... | collective-permute-start | bytes 172040 | tf_op jit(solution)/shard_map/ppermute | solution.py:418
  29.7 1.6 %shard_map.41 = (f32[4,16,32,128]{3,2,1,0:T(8,128)S(1)}, f32[2,16,32,128]{3,2,1,0:T(8,128)S(1)}, f32[2,16,32,128]{3,2,1,0:T(8,128)S(1)}) custom-call(f32[4,32,16,128]{3,2,1,0:T(8,128)S(1)} %get-tuple-element.80.solved, f32[2,32,16,128]{3,2,1,0:T(8,128)S(1)} %get-tuple-element.60.after.ivy, f32[2,32,16,128]{3,2,1,0:T(8,128)S(1)} %get-tuple-element.81.ry, ...), custom_call_target="tpu_custom_call" | custom-call | flops 1000 | bytes 1000 | tf_op jit(solution)/shard_map/pallas_call | solution.py:22
  31.4 1.6 %collective-permute-done.10.refs_1_ = f32[7,16,128]{2,1,0:T(8,128)S(1)} collective-permute-done((f32[7,16,128]{2,1,0:T(8,128)S(1)}, f32[7,16,128]{2,1,0:T(8,128)S(1)}, u32[]{:S(2)}, u32[]{:S(2)}) %collective-permute-start.10) | collective-permute-done | bytes 57376 | tf_op jit(solution)/shard_map/ppermute | solution.py:418
  33.0 1.1 %shard_map.42 = f32[4,16,32,128]{3,2,1,0:T(8,128)} custom-call(f32[7,16,128]{2,1,0:T(8,128)S(1)} %get-tuple-element.77.refs_0_, f32[7,16,128]{2,1,0:T(8,128)S(1)} %collective-permute-done.10.refs_1_, f32[4,16,128]{2,1,0:T(8,128)S(1)} %get-tuple-element.78.refs_2_, f32[6,16,128]{2,1,0:T(8,128)S(1)} %get-tuple-element.79.refs_3_, ...), custom_call_target="tpu_custom_call" | custom-call | flops 1000 | bytes 1000 | tf_op jit(solution)/shard_map/pallas_call | solution.py:22
  (15 shorter events, 0.5 us)
Async XLA Ops:
  0.0 7.5 %copy-start = (f32[4,16,32,128]{3,2,1,0:T(8,128)S(1)}, f32[4,16,32,128]{3,2,1,0:T(8,128)}, u32[]{:S(2)}) copy-start(f32[4,16,32,128]{3,2,1,0:T(8,128)} %flow.3) | copy-start | bytes 3145732
  1.2 3.2 %collective-permute-start = (f32[4,16,128]{2,1,0:T(8,128)S(1)}, f32[4,16,128]{2,1,0:T(8,128)S(1)}, u32[]{:S(2)}, u32[]{:S(2)}) collective-permute-start(f32[4,16,128]{2,1,0:T(8,128)S(1)} %get-tuple-element.47.y_edge_even), channel_id=1, source_target_pairs={{0,1},{1,0},{2,3},{3,2},{4,5},{5,4},{6,7},{7,6},{8,9},{9,8},{10,11... | collective-permute-start | bytes 98312 | tf_op jit(solution)/shard_map/ppermute | solution.py:418
  1.7 6.7 %collective-permute-start.1 = (f32[4,32,128]{2,1,0:T(8,128)S(1)}, f32[4,32,128]{2,1,0:T(8,128)S(1)}, u32[]{:S(2)}, u32[]{:S(2)}) collective-permute-start(f32[4,32,128]{2,1,0:T(8,128)S(1)} %get-tuple-element.51.x_edge), channel_id=1, source_target_pairs={{0,1},{1,0},{2,3},{3,2},{4,8},{5,9},{6,10},{7,11},{8,4},{9,5},{10,... | collective-permute-start | bytes 196616 | tf_op jit(solution)/shard_map/ppermute | solution.py:443
  1.8 6.6 %collective-permute-start.2 = (f32[4,16,128]{2,1,0:T(8,128)S(1)}, f32[4,16,128]{2,1,0:T(8,128)S(1)}, u32[]{:S(2)}, u32[]{:S(2)}) collective-permute-start(f32[4,16,128]{2,1,0:T(8,128)S(1)} %get-tuple-element.52.y_edge_odd), channel_id=1, source_target_pairs={{0,3},{1,2},{2,1},{3,0},{4,7},{5,6},{6,5},{7,4},{8,11},{9,10},{10,... | collective-permute-start | bytes 98312 | tf_op jit(solution)/shard_map/ppermute | solution.py:444
  4.7 8.2 %collective-permute-start.4 = (f32[11,32,128]{2,1,0:T(8,128)S(1)}, f32[11,32,128]{2,1,0:T(8,128)S(1)}, u32[]{:S(2)}, u32[]{:S(2)}) collective-permute-start(f32[11,32,128]{2,1,0:T(8,128)S(1)} %get-tuple-element.54.mine.coef_mine), channel_id=1, source_target_pairs={{0,4},{4,0},{8,12},{12,8},{16,20},{20,16},{24,28},{28,24},{1,5},{5... | collective-permute-start | bytes 540680 | tf_op jit(solution)/shard_map/ppermute | solution.py:418
  8.5 7.2 %collective-permute-start.3 = (f32[9,32,128]{2,1,0:T(8,128)S(1)}, f32[9,32,128]{2,1,0:T(8,128)S(1)}, u32[]{:S(2)}, u32[]{:S(2)}) collective-permute-start(f32[9,32,128]{2,1,0:T(8,128)S(1)} %get-tuple-element.53.mine), channel_id=1, source_target_pairs={{0,4},{4,0},{8,12},{12,8},{16,20},{20,16},{24,28},{28,24},{1,5},{5... | collective-permute-start | bytes 442376 | tf_op jit(solution)/shard_map/ppermute | solution.py:418
  12.9 5.0 %collective-permute-start.6 = (f32[8,32,128]{2,1,0:T(8,128)S(1)}, f32[8,32,128]{2,1,0:T(8,128)S(1)}, u32[]{:S(2)}, u32[]{:S(2)}) collective-permute-start(f32[8,32,128]{2,1,0:T(8,128)S(1)} %get-tuple-element.64.mine.coef_mine), channel_id=1, source_target_pairs={{0,8},{4,12},{8,0},{12,4},{16,24},{20,28},{24,16},{28,20},{1,9},{5... | collective-permute-start | bytes 393224 | tf_op jit(solution)/shard_map/ppermute | solution.py:418
  15.8 5.9 %collective-permute-start.5 = (f32[8,32,128]{2,1,0:T(8,128)S(1)}, f32[8,32,128]{2,1,0:T(8,128)S(1)}, u32[]{:S(2)}, u32[]{:S(2)}) collective-permute-start(f32[8,32,128]{2,1,0:T(8,128)S(1)} %get-tuple-element.63.after.mine), channel_id=1, source_target_pairs={{0,8},{4,12},{8,0},{12,4},{16,24},{20,28},{24,16},{28,20},{1,9},{5... | collective-permute-start | bytes 393224 | tf_op jit(solution)/shard_map/ppermute | solution.py:418
  18.0 6.5 %collective-permute-start.8 = (f32[4,32,128]{2,1,0:T(8,128)S(1)}, f32[4,32,128]{2,1,0:T(8,128)S(1)}, u32[]{:S(2)}, u32[]{:S(2)}) collective-permute-start(f32[4,32,128]{2,1,0:T(8,128)S(1)} %get-tuple-element.67.mine), channel_id=1, source_target_pairs={{0,16},{4,20},{8,24},{12,28},{16,0},{20,4},{24,8},{28,12},{1,17},{... | collective-permute-start | bytes 196616 | tf_op jit(solution)/shard_map/ppermute | solution.py:418
  21.8 5.2 %collective-permute-start.7 = (f32[4,32,128]{2,1,0:T(8,128)S(1)}, f32[4,32,128]{2,1,0:T(8,128)S(1)}, u32[]{:S(2)}, u32[]{:S(2)}) collective-permute-start(f32[4,32,128]{2,1,0:T(8,128)S(1)} %get-tuple-element.66.refs_0_), channel_id=1, source_target_pairs={{0,16},{4,20},{8,24},{12,28},{16,0},{20,4},{24,8},{28,12},{1,17},{... | collective-permute-start | bytes 196616 | tf_op jit(solution)/shard_map/ppermute | solution.py:418
  27.3 1.4 %collective-permute-start.9 = (f32[16,16,128]{2,1,0:T(8,128)S(1)}, f32[16,16,128]{2,1,0:T(8,128)S(1)}, u32[]{:S(2)}, u32[]{:S(2)}) collective-permute-start(f32[16,16,128]{2,1,0:T(8,128)S(1)} %get-tuple-element.76.mine), channel_id=1, source_target_pairs={{0,1},{1,0},{2,3},{3,2},{4,5},{5,4},{6,7},{7,6},{8,9},{9,8},{10,11... | collective-permute-start | bytes 393224 | tf_op jit(solution)/shard_map/ppermute | solution.py:418
  28.8 4.2 %collective-permute-start.10 = (f32[7,16,128]{2,1,0:T(8,128)S(1)}, f32[7,16,128]{2,1,0:T(8,128)S(1)}, u32[]{:S(2)}, u32[]{:S(2)}) collective-permute-start(f32[7,16,128]{2,1,0:T(8,128)S(1)} %get-tuple-element.77.refs_0_), channel_id=1, source_target_pairs={{0,2},{1,3},{2,0},{3,1},{4,6},{5,7},{6,4},{7,5},{8,10},{9,11},{10,... | collective-permute-start | bytes 172040 | tf_op jit(solution)/shard_map/ppermute | solution.py:418

commit v6 on v5

--- a/solution.py
+++ b/solution.py
@@ -78,7 +78,7 @@
         out[4 + group] = right[group, count - 1]
 
 
-def pack_kernel(flow, visc, x_even, x_odd, y_even, y_odd, cells, sems):
+def pack_kernel(flow, visc, x_odd, y_even, y_odd, cells, sems):
     nx, ny = flow.shape[1], flow.shape[2]
     x_par = lax.rem(lax.axis_index("gx"), 2)
     y_par = lax.rem(lax.axis_index("gy"), 2)
@@ -86,7 +86,6 @@
         (flow.at[:, x_par * (nx - 1)], x_odd),
         (flow.at[:, :, (1 - y_par) * (ny - 1)], y_even),
         (flow.at[:, :, y_par * (ny - 1)], y_odd),
-        (flow.at[:, (1 - x_par) * (nx - 1)], x_even),
         (visc, cells),
     )
     started = [pltpu.make_async_copy(a, b, sems.at[i]) for i, (a, b) in enumerate(copies)]
@@ -96,14 +95,18 @@
         copy.wait()
 
 
-def factor_x_kernel(visc, x_even, after, ivx, rx, cx, wx, coef_x):
+def factor_x_kernel(visc, flow, after, ivx, rx, cx, wx, coef_x, x_even):
     nx = visc.shape[0]
     ix = lax.axis_index("gx")
     factor_line(lambda i: visc[i], nx, ix == 0, ix == lax.axis_size("gx") - 1, ivx, rx, cx, wx)
     coef_rows(cx, wx, coef_x, nx)
     coef_x[6] = visc[0]
     coef_x[7] = visc[nx - 1]
-    coef_x[pl.ds(8, EARLY)] = x_even[pl.ds(0, EARLY)]
+    for c in range(4):
+        facing = pick(lax.rem(ix, 2) == 0, flow[c, nx - 1], flow[c, 0])
+        if c < EARLY:
+            coef_x[8 + c] = facing
+        x_even[c] = facing
 
 
 def factor_y_kernel(visc, ivy, ry, cy, wy, coef_y):
@@ -152,7 +155,7 @@
         message[4 + c] = right[c]
 
 
-def edge_kernel(partial, x_edge_even, x_edge, y_edge_even, y_edge_odd, x_odd, y_even, y_odd, cx, wx, message, gap_x, gap_y):
+def edge_kernel(partial, x_edge_even, x_edge, y_edge_even, y_edge_odd, x_odd, y_even, y_odd, cx, wx, after, message, gap_x, gap_y):
     _, nx, ny, nz = cx.shape
     ix, iy = lax.axis_index("gx"), lax.axis_index("gy")
     x_par, y_par = lax.rem(ix, 2) == 0, lax.rem(iy, 2) == 0
@@ -308,7 +311,7 @@
     return result
 
 
-def local_kernel(source, gap_x, gap_y, ivx, rx, cx, wx, after, local_t, cx_t, wx_t, scratch):
+def local_kernel(source, gap_x, gap_y, ivx, rx, cx, wx, local_t, cx_t, wx_t, scratch):
     _, nx, ny, nz = source.shape
     x_par = lax.rem(lax.axis_index("gx"), 2) == 0
     row = lax.broadcasted_iota(jnp.int32, (ny, nz), 0)
@@ -427,11 +430,11 @@
     mx, my = lax.axis_size("gx"), lax.axis_size("gy")
     along_x, along_y = (2, nx, ny, nz), (2, ny, nx, nz)
     along_x, along_y = (2, nx, ny, nz), (2, ny, nx, nz)
-    x_edge_even, x_edge, y_edge_even, y_edge_odd, cells = call(
+    x_edge, y_edge_even, y_edge_odd, cells = call(
         pack_kernel,
         tuple(pltpu.with_memory_space_constraint(array, pltpu.HBM) for array in (flow, visc)),
-        [(fields, ny, nz)] * 2 + [(fields, nx, nz)] * 2 + [(nx, ny, nz)],
-        scratch=[pltpu.SemaphoreType.DMA((5,))],
+        [(fields, ny, nz)] + [(fields, nx, nz)] * 2 + [(nx, ny, nz)],
+        scratch=[pltpu.SemaphoreType.DMA((4,))],
         in_specs=[HBM, HBM],
     )
     pairs = []
@@ -445,10 +448,10 @@
         y_edge_odd, "gy", [(i, (i - 1 ^ 1) + 1) if 0 < i < my - 1 else (i, my - 1 - i) for i in range(my)]
     )
     y_even = swap(y_edge_even, "gy", 1)
-    ivx, rx, cx, wx, coef_x = call(
+    ivx, rx, cx, wx, coef_x, x_edge_even = call(
         factor_x_kernel,
-        (cells, x_edge_even, y_even),
-        [along_x] * 4 + [(8 + EARLY, ny, nz)],
+        (cells, flow, y_even),
+        [along_x] * 4 + [(8 + EARLY, ny, nz), (fields, ny, nz)],
         in_specs=after_all(2),
     )
 
@@ -457,13 +460,13 @@
     source, partial = call(source_kernel, (flow, cx, wx), [(fields, nx, ny, nz), (8, ny, nz)])
     message, gap_x, gap_y = call(
         edge_kernel,
-        (partial, x_edge_even, x_edge, y_edge_even, y_edge_odd, x_odd, y_even, y_odd, cx, wx),
+        (partial, x_edge_even, x_edge, y_edge_even, y_edge_odd, x_odd, y_even, y_odd, cx, wx, ivy),
         [(12 - EARLY, ny, nz), (fields, ny, nz), (2 * fields, nx, nz)],
+        in_specs=after_all(10),
     )
     local_t, cx_t, wx_t = call(
         local_kernel,
-        (source, gap_x, gap_y, ivx, rx, cx, wx, ivy),
-        in_specs=after_all(7),
+        (source, gap_x, gap_y, ivx, rx, cx, wx),
         outs=[(fields, ny, nx, nz), along_y, along_y],
         scratch=[pltpu.VMEM((fields, nx * ny, nz), F32)],
         cost=1000,

time: 34.2 us -> 34.2 us (level)
  waiting for transfers between devices: 8.42 us -> 8.96 us
  starting transfers between devices: 17.8 us -> 17.3 us
    ppermute x9, waiting for transfers between devices: 8.41 us -> 8.96 us  [swap(): lax.ppermute(array, axis, [(i, i ^ bit) for i in range(lax.axis_size(axis...]
    ppermute x9, starting transfers between devices: 15.1 us -> 14.6 us  [swap(): lax.ppermute(array, axis, [(i, i ^ bit) for i in range(lax.axis_size(axis...]
where the time goes in v6:
time: 34.2 us; the launch traced here: 34.1 us
  starting transfers between devices  17.3 us (51%)
  waiting for transfers between devices  8.96 us (26%)
  Pallas kernels  7.68 us (22%)
    ppermute x9, starting transfers between devices, swap(): lax.ppermute(array, axis, [(i, i ^ bit) for i in range(lax.axis_size(axis...  14.6 us
    ppermute x9, waiting for transfers between devices, swap(): lax.ppermute(array, axis, [(i, i ^ bit) for i in range(lax.axis_size(axis...  8.96 us
    pallas_call x15, Pallas kernels, call(): pl.pallas_call(kernel, out_shape=[jax.ShapeDtypeStruct(shape, F32) for sh...  7.68 us
    ppermute x1, starting transfers between devices, per_device(): lax.ppermute(y_edge_odd, 'gy', [(i, (i - 1 ^ 1) + 1) if 0 < i < my - 1 el...  2.63 us
  transfers between devices with their start and end apart: 11, of which 7 were waited for; matrix products, arithmetic and copies ran while one was open for 0% of the time, Pallas kernels for 15%

profile of v6, /device:TPU:0, one launch (start us, length us, event | category | flops | bytes accessed | tf_op | source)
XLA Modules:
  0.0 34.1 jit_solution(15954708974467328989)
XLA Ops:
  0.0 1.1 %shard_map.28 = (f32[4,32,128]{2,1,0:T(8,128)S(1)}, f32[4,16,128]{2,1,0:T(8,128)S(1)}, f32[4,16,128]{2,1,0:T(8,128)S(1)}, f32[16,32,128]{2,1,0:T(8,128)S(1)}) custom-call(f32[4,16,32,128]{3,2,1,0:T(8,128)} %flow.5, f32[16,32,128]{2,1,0:T(8,128)} %visc.1), custom_call_target="tpu_custom_call" | custom-call | flops 1000 | bytes 1000 | tf_op jit(solution)/shard_map/pallas_call | solution.py:22
  1.2 0.5 %collective-permute-start = (f32[4,16,128]{2,1,0:T(8,128)S(1)}, f32[4,16,128]{2,1,0:T(8,128)S(1)}, u32[]{:S(2)}, u32[]{:S(2)}) collective-permute-start(f32[4,16,128]{2,1,0:T(8,128)S(1)} %get-tuple-element.46.y_edge_even), channel_id=1, source_target_pairs={{0,1},{1,0},{2,3},{3,2},{4,5},{5,4},{6,7},{7,6},{8,9},{9,8},{10,11... | collective-permute-start | bytes 98312 | tf_op jit(solution)/shard_map/ppermute | solution.py:421
  1.8 2.6 %collective-permute-start.2 = (f32[4,16,128]{2,1,0:T(8,128)S(1)}, f32[4,16,128]{2,1,0:T(8,128)S(1)}, u32[]{:S(2)}, u32[]{:S(2)}) collective-permute-start(f32[4,16,128]{2,1,0:T(8,128)S(1)} %get-tuple-element.52.y_edge_odd), channel_id=1, source_target_pairs={{0,3},{1,2},{2,1},{3,0},{4,7},{5,6},{6,5},{7,4},{8,11},{9,10},{10,... | collective-permute-start | bytes 98312 | tf_op jit(solution)/shard_map/ppermute | solution.py:447
  4.4 0.3 shard_map.29
  4.7 2.8 %collective-permute-start.4 = (f32[11,32,128]{2,1,0:T(8,128)S(1)}, f32[11,32,128]{2,1,0:T(8,128)S(1)}, u32[]{:S(2)}, u32[]{:S(2)}) collective-permute-start(f32[11,32,128]{2,1,0:T(8,128)S(1)} %get-tuple-element.55.mine.coef_mine), channel_id=1, source_target_pairs={{0,4},{4,0},{8,12},{12,8},{16,20},{20,16},{24,28},{28,24},{1,5},{5... | collective-permute-start | bytes 540680 | tf_op jit(solution)/shard_map/ppermute | solution.py:421
  7.4 0.5 %shard_map.31 = (f32[2,32,16,128]{3,2,1,0:T(8,128)S(1)}, f32[2,32,16,128]{3,2,1,0:T(8,128)S(1)}, f32[2,32,16,128]{3,2,1,0:T(8,128)S(1)}, f32[2,32,16,128]{3,2,1,0:T(8,128)S(1)}, f32[8,16,128]{2,1,0:T(8,128)S(1)}) custom-call(f32[16,32,128]{2,1,0:T(8,128)S(1)} %get-tuple-element.45.visc), custom_call_target="tpu_custom_call" | custom-call | flops 1000 | bytes 1000 | tf_op jit(solution)/shard_map/pallas_call | solution.py:22
  8.0 0.9 %shard_map.30 = (f32[4,16,32,128]{3,2,1,0:T(8,128)S(1)}, f32[8,32,128]{2,1,0:T(8,128)S(1)}) custom-call(f32[4,16,32,128]{3,2,1,0:T(8,128)S(1)} %copy-done, f32[2,16,32,128]{3,2,1,0:T(8,128)S(1)} %get-tuple-element.47.cx, f32[2,16,32,128]{3,2,1,0:T(8,128)S(1)} %get-tuple-element.48.wx), custom_call_target="tpu_custom_call" | custom-call | flops 1000 | bytes 1000 | tf_op jit(solution)/shard_map/pallas_call | solution.py:22
  9.0 0.8 %collective-permute-start.3 = (f32[9,32,128]{2,1,0:T(8,128)S(1)}, f32[9,32,128]{2,1,0:T(8,128)S(1)}, u32[]{:S(2)}, u32[]{:S(2)}) collective-permute-start(f32[9,32,128]{2,1,0:T(8,128)S(1)} %get-tuple-element.54.mine), channel_id=1, source_target_pairs={{0,4},{4,0},{8,12},{12,8},{16,20},{20,16},{24,28},{28,24},{1,5},{5... | collective-permute-start | bytes 442376 | tf_op jit(solution)/shard_map/ppermute | solution.py:421
  9.8 1.5 %shard_map.33 = (f32[4,32,16,128]{3,2,1,0:T(8,128)S(1)}, f32[2,32,16,128]{3,2,1,0:T(8,128)S(1)}, f32[2,32,16,128]{3,2,1,0:T(8,128)S(1)}) custom-call(f32[4,16,32,128]{3,2,1,0:T(8,128)S(1)} %get-tuple-element.56.source, f32[4,32,128]{2,1,0:T(8,128)S(1)} %get-tuple-element.57.gap_x, f32[8,16,128]{2,1,0:T(8,128)S(1)} %get-tuple-element.58.gap_y, ...), custom_call_target="tpu_custom_call" | custom-call | flops 1000 | bytes 1000 | tf_op jit(solution)/shard_map/pallas_call | solution.py:22
  11.2 1.6 %collective-permute-done.4.theirs.coef_theirs = f32[11,32,128]{2,1,0:T(8,128)S(1)} collective-permute-done((f32[11,32,128]{2,1,0:T(8,128)S(1)}, f32[11,32,128]{2,1,0:T(8,128)S(1)}, u32[]{:S(2)}, u32[]{:S(2)}) %collective-permute-start.4) | collective-permute-done | bytes 180256 | tf_op jit(solution)/shard_map/ppermute | solution.py:421
  12.9 1.9 %collective-permute-start.6 = (f32[8,32,128]{2,1,0:T(8,128)S(1)}, f32[8,32,128]{2,1,0:T(8,128)S(1)}, u32[]{:S(2)}, u32[]{:S(2)}) collective-permute-start(f32[8,32,128]{2,1,0:T(8,128)S(1)} %get-tuple-element.64.mine.coef_mine), channel_id=1, source_target_pairs={{0,8},{4,12},{8,0},{12,4},{16,24},{20,28},{24,16},{28,20},{1,9},{5... | collective-permute-start | bytes 393224 | tf_op jit(solution)/shard_map/ppermute | solution.py:421
  14.8 0.8 %collective-permute-done.3.theirs = f32[9,32,128]{2,1,0:T(8,128)S(1)} collective-permute-done((f32[9,32,128]{2,1,0:T(8,128)S(1)}, f32[9,32,128]{2,1,0:T(8,128)S(1)}, u32[]{:S(2)}, u32[]{:S(2)}) %collective-permute-start.3) | collective-permute-done | bytes 147488 | tf_op jit(solution)/shard_map/ppermute | solution.py:421
  15.7 1.7 %collective-permute-start.5 = (f32[8,32,128]{2,1,0:T(8,128)S(1)}, f32[8,32,128]{2,1,0:T(8,128)S(1)}, u32[]{:S(2)}, u32[]{:S(2)}) collective-permute-start(f32[8,32,128]{2,1,0:T(8,128)S(1)} %get-tuple-element.63.after.mine), channel_id=1, source_target_pairs={{0,8},{4,12},{8,0},{12,4},{16,24},{20,28},{24,16},{28,20},{1,9},{5... | collective-permute-start | bytes 393224 | tf_op jit(solution)/shard_map/ppermute | solution.py:421
  17.5 0.5 %collective-permute-done.6.theirs.coef_theirs = f32[8,32,128]{2,1,0:T(8,128)S(1)} collective-permute-done((f32[8,32,128]{2,1,0:T(8,128)S(1)}, f32[8,32,128]{2,1,0:T(8,128)S(1)}, u32[]{:S(2)}, u32[]{:S(2)}) %collective-permute-start.6) | collective-permute-done | bytes 131104 | tf_op jit(solution)/shard_map/ppermute | solution.py:421
  18.0 3.1 %collective-permute-start.8 = (f32[4,32,128]{2,1,0:T(8,128)S(1)}, f32[4,32,128]{2,1,0:T(8,128)S(1)}, u32[]{:S(2)}, u32[]{:S(2)}) collective-permute-start(f32[4,32,128]{2,1,0:T(8,128)S(1)} %get-tuple-element.67.mine), channel_id=1, source_target_pairs={{0,16},{4,20},{8,24},{12,28},{16,0},{20,4},{24,8},{28,12},{1,17},{... | collective-permute-start | bytes 196616 | tf_op jit(solution)/shard_map/ppermute | solution.py:421
  21.1 0.6 %collective-permute-done.5.theirs = f32[8,32,128]{2,1,0:T(8,128)S(1)} collective-permute-done((f32[8,32,128]{2,1,0:T(8,128)S(1)}, f32[8,32,128]{2,1,0:T(8,128)S(1)}, u32[]{:S(2)}, u32[]{:S(2)}) %collective-permute-start.5) | collective-permute-done | bytes 131104 | tf_op jit(solution)/shard_map/ppermute | solution.py:421
  21.7 2.7 %collective-permute-start.7 = (f32[4,32,128]{2,1,0:T(8,128)S(1)}, f32[4,32,128]{2,1,0:T(8,128)S(1)}, u32[]{:S(2)}, u32[]{:S(2)}) collective-permute-start(f32[4,32,128]{2,1,0:T(8,128)S(1)} %get-tuple-element.66.refs_0_), channel_id=1, source_target_pairs={{0,16},{4,20},{8,24},{12,28},{16,0},{20,4},{24,8},{28,12},{1,17},{... | collective-permute-start | bytes 196616 | tf_op jit(solution)/shard_map/ppermute | solution.py:421
  24.5 2.5 %collective-permute-done.7.refs_1_ = f32[4,32,128]{2,1,0:T(8,128)S(1)} collective-permute-done((f32[4,32,128]{2,1,0:T(8,128)S(1)}, f32[4,32,128]{2,1,0:T(8,128)S(1)}, u32[]{:S(2)}, u32[]{:S(2)}) %collective-permute-start.7) | collective-permute-done | bytes 65568 | tf_op jit(solution)/shard_map/ppermute | solution.py:421
  26.9 0.3 shard_map.39
  27.4 1.3 %collective-permute-done.9.theirs = f32[16,16,128]{2,1,0:T(8,128)S(1)} collective-permute-done((f32[16,16,128]{2,1,0:T(8,128)S(1)}, f32[16,16,128]{2,1,0:T(8,128)S(1)}, u32[]{:S(2)}, u32[]{:S(2)}) %collective-permute-start.9) | collective-permute-done | bytes 131104 | tf_op jit(solution)/shard_map/ppermute | solution.py:421
  28.7 1.0 %collective-permute-start.10 = (f32[7,16,128]{2,1,0:T(8,128)S(1)}, f32[7,16,128]{2,1,0:T(8,128)S(1)}, u32[]{:S(2)}, u32[]{:S(2)}) collective-permute-start(f32[7,16,128]{2,1,0:T(8,128)S(1)} %get-tuple-element.77.refs_0_), channel_id=1, source_target_pairs={{0,2},{1,3},{2,0},{3,1},{4,6},{5,7},{6,4},{7,5},{8,10},{9,11},{10,... | collective-permute-start | bytes 172040 | tf_op jit(solution)/shard_map/ppermute | solution.py:421
  29.7 1.6 %shard_map.41 = (f32[4,16,32,128]{3,2,1,0:T(8,128)S(1)}, f32[2,16,32,128]{3,2,1,0:T(8,128)S(1)}, f32[2,16,32,128]{3,2,1,0:T(8,128)S(1)}) custom-call(f32[4,32,16,128]{3,2,1,0:T(8,128)S(1)} %get-tuple-element.80.solved, f32[2,32,16,128]{3,2,1,0:T(8,128)S(1)} %get-tuple-element.53.after.ivy, f32[2,32,16,128]{3,2,1,0:T(8,128)S(1)} %get-tuple-element.81.ry, ...), custom_call_target="tpu_custom_call" | custom-call | flops 1000 | bytes 1000 | tf_op jit(solution)/shard_map/pallas_call | solution.py:22
  31.3 1.6 %collective-permute-done.10.refs_1_ = f32[7,16,128]{2,1,0:T(8,128)S(1)} collective-permute-done((f32[7,16,128]{2,1,0:T(8,128)S(1)}, f32[7,16,128]{2,1,0:T(8,128)S(1)}, u32[]{:S(2)}, u32[]{:S(2)}) %collective-permute-start.10) | collective-permute-done | bytes 57376 | tf_op jit(solution)/shard_map/ppermute | solution.py:421
  33.0 1.1 %shard_map.42 = f32[4,16,32,128]{3,2,1,0:T(8,128)} custom-call(f32[7,16,128]{2,1,0:T(8,128)S(1)} %get-tuple-element.77.refs_0_, f32[7,16,128]{2,1,0:T(8,128)S(1)} %collective-permute-done.10.refs_1_, f32[4,16,128]{2,1,0:T(8,128)S(1)} %get-tuple-element.78.refs_2_, f32[6,16,128]{2,1,0:T(8,128)S(1)} %get-tuple-element.79.refs_3_, ...), custom_call_target="tpu_custom_call" | custom-call | flops 1000 | bytes 1000 | tf_op jit(solution)/shard_map/pallas_call | solution.py:22
  (15 shorter events, 0.5 us)
Async XLA Ops:
  0.0 4.4 %copy-start = (f32[4,16,32,128]{3,2,1,0:T(8,128)S(1)}, f32[4,16,32,128]{3,2,1,0:T(8,128)}, u32[]{:S(2)}) copy-start(f32[4,16,32,128]{3,2,1,0:T(8,128)} %flow.5) | copy-start | bytes 3145732
  1.2 3.2 %collective-permute-start = (f32[4,16,128]{2,1,0:T(8,128)S(1)}, f32[4,16,128]{2,1,0:T(8,128)S(1)}, u32[]{:S(2)}, u32[]{:S(2)}) collective-permute-start(f32[4,16,128]{2,1,0:T(8,128)S(1)} %get-tuple-element.46.y_edge_even), channel_id=1, source_target_pairs={{0,1},{1,0},{2,3},{3,2},{4,5},{5,4},{6,7},{7,6},{8,9},{9,8},{10,11... | collective-permute-start | bytes 98312 | tf_op jit(solution)/shard_map/ppermute | solution.py:421
  1.7 7.2 %collective-permute-start.1 = (f32[4,32,128]{2,1,0:T(8,128)S(1)}, f32[4,32,128]{2,1,0:T(8,128)S(1)}, u32[]{:S(2)}, u32[]{:S(2)}) collective-permute-start(f32[4,32,128]{2,1,0:T(8,128)S(1)} %get-tuple-element.51.x_edge), channel_id=1, source_target_pairs={{0,1},{1,0},{2,3},{3,2},{4,8},{5,9},{6,10},{7,11},{8,4},{9,5},{10,... | collective-permute-start | bytes 196616 | tf_op jit(solution)/shard_map/ppermute | solution.py:446
  1.8 7.1 %collective-permute-start.2 = (f32[4,16,128]{2,1,0:T(8,128)S(1)}, f32[4,16,128]{2,1,0:T(8,128)S(1)}, u32[]{:S(2)}, u32[]{:S(2)}) collective-permute-start(f32[4,16,128]{2,1,0:T(8,128)S(1)} %get-tuple-element.52.y_edge_odd), channel_id=1, source_target_pairs={{0,3},{1,2},{2,1},{3,0},{4,7},{5,6},{6,5},{7,4},{8,11},{9,10},{10,... | collective-permute-start | bytes 98312 | tf_op jit(solution)/shard_map/ppermute | solution.py:447
  4.7 8.2 %collective-permute-start.4 = (f32[11,32,128]{2,1,0:T(8,128)S(1)}, f32[11,32,128]{2,1,0:T(8,128)S(1)}, u32[]{:S(2)}, u32[]{:S(2)}) collective-permute-start(f32[11,32,128]{2,1,0:T(8,128)S(1)} %get-tuple-element.55.mine.coef_mine), channel_id=1, source_target_pairs={{0,4},{4,0},{8,12},{12,8},{16,20},{20,16},{24,28},{28,24},{1,5},{5... | collective-permute-start | bytes 540680 | tf_op jit(solution)/shard_map/ppermute | solution.py:421
  9.0 6.7 %collective-permute-start.3 = (f32[9,32,128]{2,1,0:T(8,128)S(1)}, f32[9,32,128]{2,1,0:T(8,128)S(1)}, u32[]{:S(2)}, u32[]{:S(2)}) collective-permute-start(f32[9,32,128]{2,1,0:T(8,128)S(1)} %get-tuple-element.54.mine), channel_id=1, source_target_pairs={{0,4},{4,0},{8,12},{12,8},{16,20},{20,16},{24,28},{28,24},{1,5},{5... | collective-permute-start | bytes 442376 | tf_op jit(solution)/shard_map/ppermute | solution.py:421
  12.9 5.0 %collective-permute-start.6 = (f32[8,32,128]{2,1,0:T(8,128)S(1)}, f32[8,32,128]{2,1,0:T(8,128)S(1)}, u32[]{:S(2)}, u32[]{:S(2)}) collective-permute-start(f32[8,32,128]{2,1,0:T(8,128)S(1)} %get-tuple-element.64.mine.coef_mine), channel_id=1, source_target_pairs={{0,8},{4,12},{8,0},{12,4},{16,24},{20,28},{24,16},{28,20},{1,9},{5... | collective-permute-start | bytes 393224 | tf_op jit(solution)/shard_map/ppermute | solution.py:421
  15.7 5.9 %collective-permute-start.5 = (f32[8,32,128]{2,1,0:T(8,128)S(1)}, f32[8,32,128]{2,1,0:T(8,128)S(1)}, u32[]{:S(2)}, u32[]{:S(2)}) collective-permute-start(f32[8,32,128]{2,1,0:T(8,128)S(1)} %get-tuple-element.63.after.mine), channel_id=1, source_target_pairs={{0,8},{4,12},{8,0},{12,4},{16,24},{20,28},{24,16},{28,20},{1,9},{5... | collective-permute-start | bytes 393224 | tf_op jit(solution)/shard_map/ppermute | solution.py:421
  18.0 6.5 %collective-permute-start.8 = (f32[4,32,128]{2,1,0:T(8,128)S(1)}, f32[4,32,128]{2,1,0:T(8,128)S(1)}, u32[]{:S(2)}, u32[]{:S(2)}) collective-permute-start(f32[4,32,128]{2,1,0:T(8,128)S(1)} %get-tuple-element.67.mine), channel_id=1, source_target_pairs={{0,16},{4,20},{8,24},{12,28},{16,0},{20,4},{24,8},{28,12},{1,17},{... | collective-permute-start | bytes 196616 | tf_op jit(solution)/shard_map/ppermute | solution.py:421
  21.7 5.2 %collective-permute-start.7 = (f32[4,32,128]{2,1,0:T(8,128)S(1)}, f32[4,32,128]{2,1,0:T(8,128)S(1)}, u32[]{:S(2)}, u32[]{:S(2)}) collective-permute-start(f32[4,32,128]{2,1,0:T(8,128)S(1)} %get-tuple-element.66.refs_0_), channel_id=1, source_target_pairs={{0,16},{4,20},{8,24},{12,28},{16,0},{20,4},{24,8},{28,12},{1,17},{... | collective-permute-start | bytes 196616 | tf_op jit(solution)/shard_map/ppermute | solution.py:421
  27.3 1.4 %collective-permute-start.9 = (f32[16,16,128]{2,1,0:T(8,128)S(1)}, f32[16,16,128]{2,1,0:T(8,128)S(1)}, u32[]{:S(2)}, u32[]{:S(2)}) collective-permute-start(f32[16,16,128]{2,1,0:T(8,128)S(1)} %get-tuple-element.76.mine), channel_id=1, source_target_pairs={{0,1},{1,0},{2,3},{3,2},{4,5},{5,4},{6,7},{7,6},{8,9},{9,8},{10,11... | collective-permute-start | bytes 393224 | tf_op jit(solution)/shard_map/ppermute | solution.py:421
  28.7 4.2 %collective-permute-start.10 = (f32[7,16,128]{2,1,0:T(8,128)S(1)}, f32[7,16,128]{2,1,0:T(8,128)S(1)}, u32[]{:S(2)}, u32[]{:S(2)}) collective-permute-start(f32[7,16,128]{2,1,0:T(8,128)S(1)} %get-tuple-element.77.refs_0_), channel_id=1, source_target_pairs={{0,2},{1,3},{2,0},{3,1},{4,6},{5,7},{6,4},{7,5},{8,10},{9,11},{10,... | collective-permute-start | bytes 172040 | tf_op jit(solution)/shard_map/ppermute | solution.py:421

commit v7 on v6

--- a/solution.py
+++ b/solution.py
@@ -186,15 +186,15 @@
                 message[k, pl.ds(j, 1)] = message[k, pl.ds(j, 1)] + line
 
 
-def coef_part(axis, bit, last, mine, theirs, at, union, union_at, weights):
+def coef_part(axis, bit, last, mine, theirs, union, weights):
     is_left = (lax.axis_index(axis) & bit) == 0
     next_left = (lax.axis_index(axis) & (2 * bit)) == 0
 
     def a(k):
-        return pick(is_left, mine[at + k], theirs[at + k])
+        return pick(is_left, mine[k], theirs[k])
 
     def b(k):
-        return pick(is_left, theirs[at + k], mine[at + k])
+        return pick(is_left, theirs[k], mine[k])
 
     face = 0.5 * (a(7) + b(6))
     for group, scale in enumerate(SCALES):
@@ -207,16 +207,16 @@
         out_ll = a(group) - a_lr * pa
         out_rr = b(4 + group) - b_lr * pb
         if last:
-            union[union_at + group] = pick(next_left, out_rr, out_ll)
+            union[group] = pick(next_left, out_rr, out_ll)
         else:
-            union[union_at + group] = out_ll
-            union[union_at + 2 + group] = a_lr * pb
-            union[union_at + 4 + group] = out_rr
+            union[group] = out_ll
+            union[2 + group] = a_lr * pb
+            union[4 + group] = out_rr
     if last:
-        union[union_at + 2] = pick(next_left, b(7), a(6))
+        union[2] = pick(next_left, b(7), a(6))
     else:
-        union[union_at + 6] = a(6)
-        union[union_at + 7] = b(7)
+        union[6] = a(6)
+        union[7] = b(7)
 
 
 def row_part(axis, bit, last, mine, theirs, weights, union, saved, edged=None):
@@ -256,35 +256,28 @@
             union[4 + c] = out_r
 
 
-def coef_kernel(axis, bit, last, mine, theirs, after, union, weights):
-    coef_part(axis, bit, last, mine, theirs, 0, union, 0, weights)
+def coef_kernel(axis, bit, last, waits, mine, theirs, *refs):
+    union, weights = refs[waits:]
+    coef_part(axis, bit, last, mine, theirs, union, weights)
     if last:
         union[3] = union[2]
 
 
-def x_merge_kernel(axis, bit, last, edged, mine, theirs, weights, coef_mine, coef_theirs, union, saved, missing=None):
-    row_part(
-        axis, bit, last, mine, theirs, weights, union, saved,
-        (coef_mine, coef_theirs, missing) if edged else None,
-    )
-
-
-def last_weight(mine, theirs, at):
-    face = 0.5 * (mine[at + 2] + theirs[at + 2])
-    return [
-        1.0 / (1.0 / (scale * face) + mine[at + group] + theirs[at + group])
-        for group, scale in enumerate(SCALES)
-    ]
-
-
-def last_coef_kernel(mine, theirs, weight):
-    for group, value in enumerate(last_weight(mine, theirs, 0)):
-        weight[group] = value
-
-
-def y_merge_kernel(axis, bit, last, mine, theirs, union, saved, weights):
-    coef_part(axis, bit, last, mine, theirs, 8, union, 4 if last else 8, weights)
-    row_part(axis, bit, last, mine, theirs, weights, union, saved)
+def merge_kernel(axis, bit, last, edged, *refs):
+    if edged:
+        mine, theirs, weights, coef_mine, coef_theirs, union, saved, missing = refs
+        edge = (coef_mine, coef_theirs, missing)
+    else:
+        mine, theirs, weights, union, saved = refs
+        edge = None
+    row_part(axis, bit, last, mine, theirs, weights, union, saved, edge)
+
+
+def last_coef_kernel(mine, theirs, *refs):
+    weight = refs[-1]
+    face = 0.5 * (mine[2] + theirs[2])
+    for group, scale in enumerate(SCALES):
+        weight[group] = 1.0 / (1.0 / (scale * face) + mine[group] + theirs[group])
 
 
 def fluxes(axis, mine, theirs, weight, saved, missing=None):
@@ -351,7 +344,7 @@
 def y_start_kernel(stages, *refs):
     mine, theirs, weight, missing = refs[:4]
     parts = refs[4 : 4 + 2 * stages]
-    local_t, cx_t, wx_t, cy, wy, coef_y, solved, message, flux_low, flux_high = refs[4 + 2 * stages :]
+    local_t, cx_t, wx_t, cy, wy, solved, message, flux_low, flux_high = refs[4 + 2 * stages :]
     _, ny, nx, nz = local_t.shape
     saved = list(zip(parts[::2], parts[1::2]))
     for c, (low, high) in enumerate(fluxes("gx", mine, theirs, weight, saved, missing)):
@@ -370,7 +363,6 @@
             right = b if j == 0 else right + b
         message[c] = left
         message[4 + c] = right
-    message[pl.ds(8, 8)] = coef_y[...]
 
 
 def y_local_kernel(solved, ivy, ry, cy, wy, local, cy_t, wy_t):
@@ -396,12 +388,12 @@
 
 
 def finish_kernel(stages, *refs):
-    mine, theirs = refs[:2]
-    parts = refs[2 : 2 + 2 * stages]
-    local, cy_t, wy_t, out, buffer, flux_low, flux_high, sems = refs[2 + 2 * stages :]
+    mine, theirs, weight = refs[:3]
+    parts = refs[3 : 3 + 2 * stages]
+    local, cy_t, wy_t, out, buffer, flux_low, flux_high, sems = refs[3 + 2 * stages :]
     saved = list(zip(parts[::2], parts[1::2]))
     nx = local.shape[1]
-    for c, (low, high) in enumerate(fluxes("gy", mine, theirs, last_weight(mine, theirs, 4), saved)):
+    for c, (low, high) in enumerate(fluxes("gy", mine, theirs, weight, saved)):
         flux_low[c] = low
         flux_high[c] = high
     copies = []
@@ -421,8 +413,29 @@
     return lax.ppermute(array, axis, [(i, i ^ bit) for i in range(lax.axis_size(axis))])
 
 
-def after_all(spec_count):
-    return [VMEM] * spec_count + [pl.BlockSpec(memory_space=pl.ANY)]
+def after_all(spec_count, waits=1):
+    return [VMEM] * spec_count + [pl.BlockSpec(memory_space=pl.ANY)] * waits
+
+
+def merge_coefs(axis, bit, mine, theirs, after=()):
+    last = 4 * bit == lax.axis_size(axis)
+    shape = mine.shape[1:]
+    return call(
+        functools.partial(coef_kernel, axis, bit, last, len(after)),
+        (mine, theirs, *after),
+        [(4 if last else 8,) + shape, (6,) + shape],
+        in_specs=after_all(2, len(after)),
+    )
+
+
+def merge_rows(axis, bit, mine, theirs, weights, coefs=()):
+    last = 4 * bit == lax.axis_size(axis)
+    shape = mine.shape[1:]
+    return call(
+        functools.partial(merge_kernel, axis, bit, last, bool(coefs)),
+        (mine, theirs, weights, *coefs),
+        [(4 if last else 8,) + shape, (4,) + shape] + [(4,) + shape] * bool(coefs),
+    )
 
 
 def per_device(flow, visc):
@@ -472,58 +485,53 @@
         cost=1000,
     )
 
+    y_coefs, y_coefs_theirs, y_weights = coef_y, swap(coef_y, "gy", 1), []
+    bit = 1
+    while 2 * bit < my:
+        y_coefs, weights = merge_coefs("gy", bit, y_coefs, y_coefs_theirs)
+        y_weights.append(weights)
+        y_coefs_theirs = swap(y_coefs, "gy", 2 * bit)
+        bit *= 2
+
     saved = []
     coefs, coefs_theirs, rows = coef_x, coef_x_theirs, message
-    shape = (ny, nz)
     bit = 1
     while 2 * bit < mx:
-        last = 4 * bit == mx
         rows_theirs = swap(rows, "gx", bit)
-        merged, weights = call(
-            functools.partial(coef_kernel, "gx", bit, last),
-            (coefs, coefs_theirs, local_t if bit == 1 else rows),
-            [(4 if last else 8,) + shape, (6,) + shape],
-            in_specs=after_all(2),
-        )
+        after = (local_t, y_weights[0]) if bit == 1 else (rows,)
+        merged, weights = merge_coefs("gx", bit, coefs, coefs_theirs, after)
         merged_theirs = swap(merged, "gx", 2 * bit)
-        rows, part, *gap = call(
-            functools.partial(x_merge_kernel, "gx", bit, last, bit == 1),
-            (rows, rows_theirs, weights, coefs, coefs_theirs),
-            [(4 if last else 8,) + shape, (4,) + shape] + [(4,) + shape] * (bit == 1),
-        )
+        extra = (coefs, coefs_theirs) if bit == 1 else ()
+        rows, part, *gap = merge_rows("gx", bit, rows, rows_theirs, weights, extra)
         if gap:
             missing = gap[0]
         saved += [part, weights]
         coefs, coefs_theirs = merged, merged_theirs
         bit *= 2
     rows_theirs = swap(rows, "gx", bit)
-
     (weight,) = call(last_coef_kernel, (coefs, coefs_theirs), [(2, ny, nz)])
+
     solved, rows = call(
         functools.partial(y_start_kernel, len(saved) // 2),
-        (rows, rows_theirs, weight, missing, *saved, local_t, cx_t, wx_t, cy, wy, coef_y),
-        [(fields, ny, nx, nz), (16, nx, nz)],
+        (rows, rows_theirs, weight, missing, *saved, local_t, cx_t, wx_t, cy, wy),
+        [(fields, ny, nx, nz), (8, nx, nz)],
         scratch=[pltpu.VMEM((fields, ny, nz), F32)] * 2,
     )
     local_y, cy_t, wy_t = call(
         y_local_kernel, (solved, ivy, ry, cy, wy), [(fields, nx, ny, nz), along_x, along_x]
     )
+    (y_weight,) = call(
+        last_coef_kernel, (y_coefs, y_coefs_theirs, local_y), [(2, nx, nz)], in_specs=after_all(2)
+    )
     saved = []
-    shape = (nx, nz)
-    bit = 1
-    while 2 * bit < my:
-        last = 4 * bit == my
-        rows, part, weights = call(
-            functools.partial(y_merge_kernel, "gy", bit, last),
-            (rows, swap(rows, "gy", bit)),
-            [(7 if last else 16,) + shape, (4,) + shape, (6,) + shape],
-        )
+    for step, weights in enumerate(y_weights):
+        bit = 1 << step
+        rows, part = merge_rows("gy", bit, rows, swap(rows, "gy", bit), weights)
         saved += [part, weights]
-        bit *= 2
-    rows_theirs = swap(rows, "gy", bit)
+    rows_theirs = swap(rows, "gy", my // 2)
     (out,) = call(
         functools.partial(finish_kernel, len(saved) // 2),
-        (rows, rows_theirs, *saved, local_y, cy_t, wy_t),
+        (rows, rows_theirs, y_weight, *saved, local_y, cy_t, wy_t),
         [(fields, nx, ny, nz)],
         scratch=[
             pltpu.VMEM((fields, nx, ny, nz), F32),

time: 34.2 us -> 33.8 us (0.988)
  waiting for transfers between devices: 8.96 us -> 7.58 us
  starting transfers between devices: 17.3 us -> 18.3 us
    ppermute x9 -> x11, waiting for transfers between devices: 8.96 us -> 7.58 us  [swap(): lax.ppermute(array, axis, [(i, i ^ bit) for i in range(lax.axis_size(axis...]
    ppermute x9 -> x11, starting transfers between devices: 14.6 us -> 15.6 us  [swap(): lax.ppermute(array, axis, [(i, i ^ bit) for i in range(lax.axis_size(axis...]
    pallas_call x15 -> x17, Pallas kernels: 7.68 us -> 7.68 us  [call(): pl.pallas_call(kernel, out_shape=[jax.ShapeDtypeStruct(shape, F32) for sh...]
  transfers between devices with their start and end apart: 11 -> 13, of which waited for: 7 -> 8; matrix products, arithmetic and copies ran while one was open for 0% -> 0% of each run, Pallas kernels for 15% -> 15%
where the time goes in v7:
time: 33.8 us; the launch traced here: 33.7 us
  starting transfers between devices  18.3 us (54%)
  Pallas kernels  7.68 us (23%)
  waiting for transfers between devices  7.58 us (22%)
    ppermute x11, starting transfers between devices, swap(): lax.ppermute(array, axis, [(i, i ^ bit) for i in range(lax.axis_size(axis...  15.6 us
    pallas_call x17, Pallas kernels, call(): pl.pallas_call(kernel, out_shape=[jax.ShapeDtypeStruct(shape, F32) for sh...  7.68 us
    ppermute x11, waiting for transfers between devices, swap(): lax.ppermute(array, axis, [(i, i ^ bit) for i in range(lax.axis_size(axis...  7.58 us
    ppermute x1, starting transfers between devices, per_device(): lax.ppermute(y_edge_odd, 'gy', [(i, (i - 1 ^ 1) + 1) if 0 < i < my - 1 el...  2.63 us
  transfers between devices with their start and end apart: 13, of which 8 were waited for; matrix products, arithmetic and copies ran while one was open for 0% of the time, Pallas kernels for 15%

profile of v7, /device:TPU:0, one launch (start us, length us, event | category | flops | bytes accessed | tf_op | source)
XLA Modules:
  0.0 33.7 jit_solution(13775273384726769624)
XLA Ops:
  0.0 1.1 %shard_map.28 = (f32[4,32,128]{2,1,0:T(8,128)S(1)}, f32[4,16,128]{2,1,0:T(8,128)S(1)}, f32[4,16,128]{2,1,0:T(8,128)S(1)}, f32[16,32,128]{2,1,0:T(8,128)S(1)}) custom-call(f32[4,16,32,128]{3,2,1,0:T(8,128)} %flow.5, f32[16,32,128]{2,1,0:T(8,128)} %visc.1), custom_call_target="tpu_custom_call" | custom-call | flops 1000 | bytes 1000 | tf_op jit(solution)/shard_map/pallas_call | solution.py:22
  1.2 0.5 %collective-permute-start = (f32[4,16,128]{2,1,0:T(8,128)S(1)}, f32[4,16,128]{2,1,0:T(8,128)S(1)}, u32[]{:S(2)}, u32[]{:S(2)}) collective-permute-start(f32[4,16,128]{2,1,0:T(8,128)S(1)} %get-tuple-element.47.y_edge_even), channel_id=1, source_target_pairs={{0,1},{1,0},{2,3},{3,2},{4,5},{5,4},{6,7},{7,6},{8,9},{9,8},{10,11... | collective-permute-start | bytes 98312 | tf_op jit(solution)/shard_map/ppermute | solution.py:413
  1.8 2.6 %collective-permute-start.2 = (f32[4,16,128]{2,1,0:T(8,128)S(1)}, f32[4,16,128]{2,1,0:T(8,128)S(1)}, u32[]{:S(2)}, u32[]{:S(2)}) collective-permute-start(f32[4,16,128]{2,1,0:T(8,128)S(1)} %get-tuple-element.53.y_edge_odd), channel_id=1, source_target_pairs={{0,3},{1,2},{2,1},{3,0},{4,7},{5,6},{6,5},{7,4},{8,11},{9,10},{10,... | collective-permute-start | bytes 98312 | tf_op jit(solution)/shard_map/ppermute | solution.py:460
  4.4 0.3 shard_map.29
  4.7 2.8 %collective-permute-start.4 = (f32[11,32,128]{2,1,0:T(8,128)S(1)}, f32[11,32,128]{2,1,0:T(8,128)S(1)}, u32[]{:S(2)}, u32[]{:S(2)}) collective-permute-start(f32[11,32,128]{2,1,0:T(8,128)S(1)} %get-tuple-element.56.mine.refs_3_), channel_id=1, source_target_pairs={{0,4},{4,0},{8,12},{12,8},{16,20},{20,16},{24,28},{28,24},{1,5},{5... | collective-permute-start | bytes 540680 | tf_op jit(solution)/shard_map/ppermute | solution.py:413
  7.4 0.5 %shard_map.31 = (f32[2,32,16,128]{3,2,1,0:T(8,128)S(1)}, f32[2,32,16,128]{3,2,1,0:T(8,128)S(1)}, f32[2,32,16,128]{3,2,1,0:T(8,128)S(1)}, f32[2,32,16,128]{3,2,1,0:T(8,128)S(1)}, f32[8,16,128]{2,1,0:T(8,128)S(1)}) custom-call(f32[16,32,128]{2,1,0:T(8,128)S(1)} %get-tuple-element.46.visc), custom_call_target="tpu_custom_call" | custom-call | flops 1000 | bytes 1000 | tf_op jit(solution)/shard_map/pallas_call | solution.py:22
  8.0 0.9 %shard_map.30 = (f32[4,16,32,128]{3,2,1,0:T(8,128)S(1)}, f32[8,32,128]{2,1,0:T(8,128)S(1)}) custom-call(f32[4,16,32,128]{3,2,1,0:T(8,128)S(1)} %copy-done, f32[2,16,32,128]{3,2,1,0:T(8,128)S(1)} %get-tuple-element.48.cx, f32[2,16,32,128]{3,2,1,0:T(8,128)S(1)} %get-tuple-element.49.wx), custom_call_target="tpu_custom_call" | custom-call | flops 1000 | bytes 1000 | tf_op jit(solution)/shard_map/pallas_call | solution.py:22
  9.0 0.8 %collective-permute-start.3 = (f32[9,32,128]{2,1,0:T(8,128)S(1)}, f32[9,32,128]{2,1,0:T(8,128)S(1)}, u32[]{:S(2)}, u32[]{:S(2)}) collective-permute-start(f32[9,32,128]{2,1,0:T(8,128)S(1)} %get-tuple-element.55.refs_0_), channel_id=1, source_target_pairs={{0,4},{4,0},{8,12},{12,8},{16,20},{20,16},{24,28},{28,24},{1,5},{5... | collective-permute-start | bytes 442376 | tf_op jit(solution)/shard_map/ppermute | solution.py:413
  9.8 1.5 %shard_map.33 = (f32[4,32,16,128]{3,2,1,0:T(8,128)S(1)}, f32[2,32,16,128]{3,2,1,0:T(8,128)S(1)}, f32[2,32,16,128]{3,2,1,0:T(8,128)S(1)}) custom-call(f32[4,16,32,128]{3,2,1,0:T(8,128)S(1)} %get-tuple-element.57.source, f32[4,32,128]{2,1,0:T(8,128)S(1)} %get-tuple-element.58.gap_x, f32[8,16,128]{2,1,0:T(8,128)S(1)} %get-tuple-element.59.gap_y, ...), custom_call_target="tpu_custom_call" | custom-call | flops 1000 | bytes 1000 | tf_op jit(solution)/shard_map/pallas_call | solution.py:22
  11.3 1.6 %collective-permute-done.4.theirs.refs_4_ = f32[11,32,128]{2,1,0:T(8,128)S(1)} collective-permute-done((f32[11,32,128]{2,1,0:T(8,128)S(1)}, f32[11,32,128]{2,1,0:T(8,128)S(1)}, u32[]{:S(2)}, u32[]{:S(2)}) %collective-permute-start.4) | collective-permute-done | bytes 180256 | tf_op jit(solution)/shard_map/ppermute | solution.py:413
  12.9 1.9 %collective-permute-start.7 = (f32[8,32,128]{2,1,0:T(8,128)S(1)}, f32[8,32,128]{2,1,0:T(8,128)S(1)}, u32[]{:S(2)}, u32[]{:S(2)}) collective-permute-start(f32[8,32,128]{2,1,0:T(8,128)S(1)} %get-tuple-element.67.mine), channel_id=1, source_target_pairs={{0,8},{4,12},{8,0},{12,4},{16,24},{20,28},{24,16},{28,20},{1,9},{5... | collective-permute-start | bytes 393224 | tf_op jit(solution)/shard_map/ppermute | solution.py:413
  14.8 0.8 %collective-permute-done.3.refs_1_ = f32[9,32,128]{2,1,0:T(8,128)S(1)} collective-permute-done((f32[9,32,128]{2,1,0:T(8,128)S(1)}, f32[9,32,128]{2,1,0:T(8,128)S(1)}, u32[]{:S(2)}, u32[]{:S(2)}) %collective-permute-start.3) | collective-permute-done | bytes 147488 | tf_op jit(solution)/shard_map/ppermute | solution.py:413
  15.7 1.7 %collective-permute-start.6 = (f32[8,32,128]{2,1,0:T(8,128)S(1)}, f32[8,32,128]{2,1,0:T(8,128)S(1)}, u32[]{:S(2)}, u32[]{:S(2)}) collective-permute-start(f32[8,32,128]{2,1,0:T(8,128)S(1)} %get-tuple-element.66.refs_0_), channel_id=1, source_target_pairs={{0,8},{4,12},{8,0},{12,4},{16,24},{20,28},{24,16},{28,20},{1,9},{5... | collective-permute-start | bytes 393224 | tf_op jit(solution)/shard_map/ppermute | solution.py:413
  17.5 0.5 %collective-permute-done.7.theirs = f32[8,32,128]{2,1,0:T(8,128)S(1)} collective-permute-done((f32[8,32,128]{2,1,0:T(8,128)S(1)}, f32[8,32,128]{2,1,0:T(8,128)S(1)}, u32[]{:S(2)}, u32[]{:S(2)}) %collective-permute-start.7) | collective-permute-done | bytes 131104 | tf_op jit(solution)/shard_map/ppermute | solution.py:413
  18.0 3.1 %collective-permute-start.9 = (f32[4,32,128]{2,1,0:T(8,128)S(1)}, f32[4,32,128]{2,1,0:T(8,128)S(1)}, u32[]{:S(2)}, u32[]{:S(2)}) collective-permute-start(f32[4,32,128]{2,1,0:T(8,128)S(1)} %get-tuple-element.70.mine), channel_id=1, source_target_pairs={{0,16},{4,20},{8,24},{12,28},{16,0},{20,4},{24,8},{28,12},{1,17},{... | collective-permute-start | bytes 196616 | tf_op jit(solution)/shard_map/ppermute | solution.py:413
  21.1 0.6 %collective-permute-done.6.refs_1_ = f32[8,32,128]{2,1,0:T(8,128)S(1)} collective-permute-done((f32[8,32,128]{2,1,0:T(8,128)S(1)}, f32[8,32,128]{2,1,0:T(8,128)S(1)}, u32[]{:S(2)}, u32[]{:S(2)}) %collective-permute-start.6) | collective-permute-done | bytes 131104 | tf_op jit(solution)/shard_map/ppermute | solution.py:413
  21.7 2.7 %collective-permute-start.8 = (f32[4,32,128]{2,1,0:T(8,128)S(1)}, f32[4,32,128]{2,1,0:T(8,128)S(1)}, u32[]{:S(2)}, u32[]{:S(2)}) collective-permute-start(f32[4,32,128]{2,1,0:T(8,128)S(1)} %get-tuple-element.69.refs_0_), channel_id=1, source_target_pairs={{0,16},{4,20},{8,24},{12,28},{16,0},{20,4},{24,8},{28,12},{1,17},{... | collective-permute-start | bytes 196616 | tf_op jit(solution)/shard_map/ppermute | solution.py:413
  24.5 2.5 %collective-permute-done.8.refs_1_ = f32[4,32,128]{2,1,0:T(8,128)S(1)} collective-permute-done((f32[4,32,128]{2,1,0:T(8,128)S(1)}, f32[4,32,128]{2,1,0:T(8,128)S(1)}, u32[]{:S(2)}, u32[]{:S(2)}) %collective-permute-start.8) | collective-permute-done | bytes 65568 | tf_op jit(solution)/shard_map/ppermute | solution.py:413
  26.9 0.3 shard_map.40
  27.4 1.0 %collective-permute-start.12 = (f32[4,16,128]{2,1,0:T(8,128)S(1)}, f32[4,16,128]{2,1,0:T(8,128)S(1)}, u32[]{:S(2)}, u32[]{:S(2)}) collective-permute-start(f32[4,16,128]{2,1,0:T(8,128)S(1)} %get-tuple-element.80.mine), channel_id=1, source_target_pairs={{0,2},{1,3},{2,0},{3,1},{4,6},{5,7},{6,4},{7,5},{8,10},{9,11},{10,... | collective-permute-start | bytes 98312 | tf_op jit(solution)/shard_map/ppermute | solution.py:413
  28.6 1.0 %collective-permute-start.11 = (f32[4,16,128]{2,1,0:T(8,128)S(1)}, f32[4,16,128]{2,1,0:T(8,128)S(1)}, u32[]{:S(2)}, u32[]{:S(2)}) collective-permute-start(f32[4,16,128]{2,1,0:T(8,128)S(1)} %get-tuple-element.79.refs_0_), channel_id=1, source_target_pairs={{0,2},{1,3},{2,0},{3,1},{4,6},{5,7},{6,4},{7,5},{8,10},{9,11},{10,... | collective-permute-start | bytes 98312 | tf_op jit(solution)/shard_map/ppermute | solution.py:413
  29.6 1.6 %shard_map.42 = (f32[4,16,32,128]{3,2,1,0:T(8,128)S(1)}, f32[2,16,32,128]{3,2,1,0:T(8,128)S(1)}, f32[2,16,32,128]{3,2,1,0:T(8,128)S(1)}) custom-call(f32[4,32,16,128]{3,2,1,0:T(8,128)S(1)} %get-tuple-element.81.solved, f32[2,32,16,128]{3,2,1,0:T(8,128)S(1)} %get-tuple-element.54.after.ivy, f32[2,32,16,128]{3,2,1,0:T(8,128)S(1)} %get-tuple-element.82.ry, ...), custom_call_target="tpu_custom_call" | custom-call | flops 1000 | bytes 1000 | tf_op jit(solution)/shard_map/pallas_call | solution.py:22
  31.4 1.2 %collective-permute-done.11.refs_1_ = f32[4,16,128]{2,1,0:T(8,128)S(1)} collective-permute-done((f32[4,16,128]{2,1,0:T(8,128)S(1)}, f32[4,16,128]{2,1,0:T(8,128)S(1)}, u32[]{:S(2)}, u32[]{:S(2)}) %collective-permute-start.11) | collective-permute-done | bytes 32800 | tf_op jit(solution)/shard_map/ppermute | solution.py:413
  32.6 1.1 %shard_map.44 = f32[4,16,32,128]{3,2,1,0:T(8,128)} custom-call(f32[4,16,128]{2,1,0:T(8,128)S(1)} %get-tuple-element.79.refs_0_, f32[4,16,128]{2,1,0:T(8,128)S(1)} %collective-permute-done.11.refs_1_, f32[2,16,128]{2,1,0:T(8,128)S(1)} %shard_map.43.refs_2_, f32[4,16,128]{2,1,0:T(8,128)S(1)} %get-tuple-element.84.refs_3_, ...), custom_call_target="tpu_custom_call" | custom-call | flops 1000 | bytes 1000 | tf_op jit(solution)/shard_map/pallas_call | solution.py:22
  (21 shorter events, 0.9 us)
Async XLA Ops:
  0.0 4.4 %copy-start = (f32[4,16,32,128]{3,2,1,0:T(8,128)S(1)}, f32[4,16,32,128]{3,2,1,0:T(8,128)}, u32[]{:S(2)}) copy-start(f32[4,16,32,128]{3,2,1,0:T(8,128)} %flow.5) | copy-start | bytes 3145732
  1.2 3.2 %collective-permute-start = (f32[4,16,128]{2,1,0:T(8,128)S(1)}, f32[4,16,128]{2,1,0:T(8,128)S(1)}, u32[]{:S(2)}, u32[]{:S(2)}) collective-permute-start(f32[4,16,128]{2,1,0:T(8,128)S(1)} %get-tuple-element.47.y_edge_even), channel_id=1, source_target_pairs={{0,1},{1,0},{2,3},{3,2},{4,5},{5,4},{6,7},{7,6},{8,9},{9,8},{10,11... | collective-permute-start | bytes 98312 | tf_op jit(solution)/shard_map/ppermute | solution.py:413
  1.7 7.2 %collective-permute-start.1 = (f32[4,32,128]{2,1,0:T(8,128)S(1)}, f32[4,32,128]{2,1,0:T(8,128)S(1)}, u32[]{:S(2)}, u32[]{:S(2)}) collective-permute-start(f32[4,32,128]{2,1,0:T(8,128)S(1)} %get-tuple-element.52.x_edge), channel_id=1, source_target_pairs={{0,1},{1,0},{2,3},{3,2},{4,8},{5,9},{6,10},{7,11},{8,4},{9,5},{10,... | collective-permute-start | bytes 196616 | tf_op jit(solution)/shard_map/ppermute | solution.py:459
  1.8 7.1 %collective-permute-start.2 = (f32[4,16,128]{2,1,0:T(8,128)S(1)}, f32[4,16,128]{2,1,0:T(8,128)S(1)}, u32[]{:S(2)}, u32[]{:S(2)}) collective-permute-start(f32[4,16,128]{2,1,0:T(8,128)S(1)} %get-tuple-element.53.y_edge_odd), channel_id=1, source_target_pairs={{0,3},{1,2},{2,1},{3,0},{4,7},{5,6},{6,5},{7,4},{8,11},{9,10},{10,... | collective-permute-start | bytes 98312 | tf_op jit(solution)/shard_map/ppermute | solution.py:460
  4.7 8.2 %collective-permute-start.4 = (f32[11,32,128]{2,1,0:T(8,128)S(1)}, f32[11,32,128]{2,1,0:T(8,128)S(1)}, u32[]{:S(2)}, u32[]{:S(2)}) collective-permute-start(f32[11,32,128]{2,1,0:T(8,128)S(1)} %get-tuple-element.56.mine.refs_3_), channel_id=1, source_target_pairs={{0,4},{4,0},{8,12},{12,8},{16,20},{20,16},{24,28},{28,24},{1,5},{5... | collective-permute-start | bytes 540680 | tf_op jit(solution)/shard_map/ppermute | solution.py:413
  9.0 6.7 %collective-permute-start.3 = (f32[9,32,128]{2,1,0:T(8,128)S(1)}, f32[9,32,128]{2,1,0:T(8,128)S(1)}, u32[]{:S(2)}, u32[]{:S(2)}) collective-permute-start(f32[9,32,128]{2,1,0:T(8,128)S(1)} %get-tuple-element.55.refs_0_), channel_id=1, source_target_pairs={{0,4},{4,0},{8,12},{12,8},{16,20},{20,16},{24,28},{28,24},{1,5},{5... | collective-permute-start | bytes 442376 | tf_op jit(solution)/shard_map/ppermute | solution.py:413
  9.8 1.5 %collective-permute-start.5 = (f32[8,16,128]{2,1,0:T(8,128)S(1)}, f32[8,16,128]{2,1,0:T(8,128)S(1)}, u32[]{:S(2)}, u32[]{:S(2)}) collective-permute-start(f32[8,16,128]{2,1,0:T(8,128)S(1)} %get-tuple-element.63.mine), channel_id=1, source_target_pairs={{0,1},{1,0},{2,3},{3,2},{4,5},{5,4},{6,7},{7,6},{8,9},{9,8},{10,11... | collective-permute-start | bytes 196616 | tf_op jit(solution)/shard_map/ppermute | solution.py:413
  12.9 5.0 %collective-permute-start.7 = (f32[8,32,128]{2,1,0:T(8,128)S(1)}, f32[8,32,128]{2,1,0:T(8,128)S(1)}, u32[]{:S(2)}, u32[]{:S(2)}) collective-permute-start(f32[8,32,128]{2,1,0:T(8,128)S(1)} %get-tuple-element.67.mine), channel_id=1, source_target_pairs={{0,8},{4,12},{8,0},{12,4},{16,24},{20,28},{24,16},{28,20},{1,9},{5... | collective-permute-start | bytes 393224 | tf_op jit(solution)/shard_map/ppermute | solution.py:413
  15.7 5.9 %collective-permute-start.6 = (f32[8,32,128]{2,1,0:T(8,128)S(1)}, f32[8,32,128]{2,1,0:T(8,128)S(1)}, u32[]{:S(2)}, u32[]{:S(2)}) collective-permute-start(f32[8,32,128]{2,1,0:T(8,128)S(1)} %get-tuple-element.66.refs_0_), channel_id=1, source_target_pairs={{0,8},{4,12},{8,0},{12,4},{16,24},{20,28},{24,16},{28,20},{1,9},{5... | collective-permute-start | bytes 393224 | tf_op jit(solution)/shard_map/ppermute | solution.py:413
  18.0 6.5 %collective-permute-start.9 = (f32[4,32,128]{2,1,0:T(8,128)S(1)}, f32[4,32,128]{2,1,0:T(8,128)S(1)}, u32[]{:S(2)}, u32[]{:S(2)}) collective-permute-start(f32[4,32,128]{2,1,0:T(8,128)S(1)} %get-tuple-element.70.mine), channel_id=1, source_target_pairs={{0,16},{4,20},{8,24},{12,28},{16,0},{20,4},{24,8},{28,12},{1,17},{... | collective-permute-start | bytes 196616 | tf_op jit(solution)/shard_map/ppermute | solution.py:413
  21.7 5.2 %collective-permute-start.8 = (f32[4,32,128]{2,1,0:T(8,128)S(1)}, f32[4,32,128]{2,1,0:T(8,128)S(1)}, u32[]{:S(2)}, u32[]{:S(2)}) collective-permute-start(f32[4,32,128]{2,1,0:T(8,128)S(1)} %get-tuple-element.69.refs_0_), channel_id=1, source_target_pairs={{0,16},{4,20},{8,24},{12,28},{16,0},{20,4},{24,8},{28,12},{1,17},{... | collective-permute-start | bytes 196616 | tf_op jit(solution)/shard_map/ppermute | solution.py:413
  27.3 1.3 %collective-permute-start.10 = (f32[8,16,128]{2,1,0:T(8,128)S(1)}, f32[8,16,128]{2,1,0:T(8,128)S(1)}, u32[]{:S(2)}, u32[]{:S(2)}) collective-permute-start(f32[8,16,128]{2,1,0:T(8,128)S(1)} %get-tuple-element.78.refs_0_), channel_id=1, source_target_pairs={{0,1},{1,0},{2,3},{3,2},{4,5},{5,4},{6,7},{7,6},{8,9},{9,8},{10,11... | collective-permute-start | bytes 196616 | tf_op jit(solution)/shard_map/ppermute | solution.py:413
  27.4 4.0 %collective-permute-start.12 = (f32[4,16,128]{2,1,0:T(8,128)S(1)}, f32[4,16,128]{2,1,0:T(8,128)S(1)}, u32[]{:S(2)}, u32[]{:S(2)}) collective-permute-start(f32[4,16,128]{2,1,0:T(8,128)S(1)} %get-tuple-element.80.mine), channel_id=1, source_target_pairs={{0,2},{1,3},{2,0},{3,1},{4,6},{5,7},{6,4},{7,5},{8,10},{9,11},{10,... | collective-permute-start | bytes 98312 | tf_op jit(solution)/shard_map/ppermute | solution.py:413
  28.6 4.0 %collective-permute-start.11 = (f32[4,16,128]{2,1,0:T(8,128)S(1)}, f32[4,16,128]{2,1,0:T(8,128)S(1)}, u32[]{:S(2)}, u32[]{:S(2)}) collective-permute-start(f32[4,16,128]{2,1,0:T(8,128)S(1)} %get-tuple-element.79.refs_0_), channel_id=1, source_target_pairs={{0,2},{1,3},{2,0},{3,1},{4,6},{5,7},{6,4},{7,5},{8,10},{9,11},{10,... | collective-permute-start | bytes 98312 | tf_op jit(solution)/shard_map/ppermute | solution.py:413
